TPU v7x, 32 devices: a whole 2x2x4 slice. The times are simulated.
32 devices in a mesh: dp: 2 (over z_hi), seq: 8 (over y, x, core), head: 2 (over z_lo).
Axes of the slice: x: 2, y: 2, z: 4 (z_hi: 2, z_lo: 2; z = z_hi * 2 + z_lo), core: 2. Of those that a mesh axis runs over, the one named last changes fastest.
Arguments:
- tokens: bfloat16 [6144, 2048], P(('dp', 'seq')), may hold values from -6 to 6
- mix_gain: float32 [2048], replicated, may hold values from 0.1 to 1.9
- w_query: bfloat16 [2048, 1024], P(('dp', 'seq'), 'head'), may hold values from -0.125 to 0.125
- w_key: bfloat16 [2048, 1024], P(('dp', 'seq'), 'head'), may hold values from -0.125 to 0.125
- w_value: bfloat16 [2048, 2048], P(('dp', 'seq'), 'head'), may hold values from -0.125 to 0.125
- w_outgate: bfloat16 [2048, 2048], P(('dp', 'seq'), 'head'), may hold values from -0.125 to 0.125
- w_lowrank: bfloat16 [2048, 16], P(('dp', 'seq')), may hold values from -0.125 to 0.125
- w_rate: bfloat16 [16, 1024], P(None, 'head'), may hold values from -1.5 to 1.5
- rate_bias: float32 [1024], P('head'), may hold values from -1 to 12
- head_gain: float32 [512], replicated, may hold values from 0.1 to 1.9
- w_output: bfloat16 [2048, 2048], P('head', ('dp', 'seq')), may hold values from -0.1875 to 0.1875
- mlp_gain: float32 [2048], replicated, may hold values from 0.1 to 1.9
- w_gate: bfloat16 [2048, 5632], P(('dp', 'seq'), 'head'), may hold values from -0.125 to 0.125
- w_up: bfloat16 [2048, 5632], P(('dp', 'seq'), 'head'), may hold values from -0.125 to 0.125
- w_down: bfloat16 [5632, 2048], P('head', ('dp', 'seq')), may hold values from -0.15625 to 0.15625
- cotangent: bfloat16 [6144, 2048], P(('dp', 'seq')), may hold values from -6 to 6
Outputs:
- result: bfloat16 [6144, 2048], P(('dp', 'seq'))
- grad_tokens: float32 [6144, 2048], P(('dp', 'seq'))
- grad_mix_gain: float32 [2048], replicated
- grad_query: float32 [2048, 1024], P(('dp', 'seq'), 'head')
- grad_key: float32 [2048, 1024], P(('dp', 'seq'), 'head')
- grad_value: float32 [2048, 2048], P(('dp', 'seq'), 'head')
- grad_outgate: float32 [2048, 2048], P(('dp', 'seq'), 'head')
- grad_lowrank: float32 [2048, 16], P(('dp', 'seq'))
- grad_rate: float32 [16, 1024], P(None, 'head')
- grad_rate_bias: float32 [1024], P('head')
- grad_head_gain: float32 [512], replicated
- grad_output: float32 [2048, 2048], P('head', ('dp', 'seq'))
- grad_mlp_gain: float32 [2048], replicated
- grad_gate: float32 [2048, 5632], P(('dp', 'seq'), 'head')
- grad_up: float32 [2048, 5632], P(('dp', 'seq'), 'head')
- grad_down: float32 [5632, 2048], P('head', ('dp', 'seq'))
All inputs are finite; a program needn't handle non-finite values.
Results may differ from a plain program's by a relative error of at most 0.015.
The roundings to bfloat16 on the way count: a program that leaves them out, or rounds other values in their place, can miss the bound.
Values may be sent and summed in bfloat16 or wider, within the bound.
No kernel may reach another device: no remote copies, remote signals or barrier semaphores. Data moves between devices by JAX's collectives and lax.ppermute only.
A program may use at most 168 MiB of HBM per device.

v0:
```python
import jax
import jax.numpy as jnp
from jax import lax
from jax.sharding import PartitionSpec as P

KD = 256
VD = 512
BLOCK_LEN = 64


epsilon = 1e-06
normalizer = 16.0
MATMUL_PRECISION = lax.Precision.HIGHEST


def entering(shard, axis, combine, identity):
    count, position = (lax.axis_size(axis), lax.axis_index(axis))
    everything = jax.tree.map(lambda part: lax.all_gather(part, axis), shard)
    start = jax.tree.map(
        lambda part, zero: jnp.broadcast_to(jnp.asarray(zero, part.dtype), part.shape),
        shard,
        identity,
    )

    def lap(k, before):
        reached = k < position
        new = combine(before, jax.tree.map(lambda part: part[k], everything))
        return jax.tree.map(lambda a, b: jnp.where(reached, a, b), new, before)

    return lax.fori_loop(0, count, lap, start)


def prefix(shard, axis, join, neutral):
    count = lax.axis_size(axis)
    place = lax.axis_index(axis)
    ahead = count - 1 - place
    gathered = jax.tree.map(
        lambda a, kind: lax.all_gather(a.astype(kind), axis),
        shard,
        jax.tree.map(lambda a: jnp.bfloat16 if a.dtype == jnp.float32 else a.dtype, shard),
    )
    state = jax.tree.map(lambda a, e: jnp.zeros_like(a) + jnp.asarray(e, a.dtype), shard, neutral)

    def one(lap, state):
        source = count - 1 - lap
        return join(
            state,
            jax.tree.map(
                lambda a, own: lax.dynamic_index_in_dim(a, source, 0, False).astype(own.dtype),
                gathered,
                shard,
            ),
        )

    return lax.fori_loop(0, ahead, one, state)


def matmul(left, right):
    return jnp.dot(left, right, preferred_element_type=jnp.float32)


def inner(left, right):
    return lax.dot_general(
        left, right, (((0,), (0,)), ((), ())), preferred_element_type=jnp.float32
    )


def times_back(grad, weight):
    return lax.dot_general(
        grad, weight, (((1,), (1,)), ((), ())), preferred_element_type=jnp.float32
    )


def rms_norm(x, gain):
    return x * lax.rsqrt(jnp.mean(x * x, axis=-1, keepdims=True) + epsilon) * gain


def head_norm(mixed_output, outgate, gain):
    return rms_norm(mixed_output, gain) * jax.nn.silu(outgate)


def swiglu(gate, upward):
    return jax.nn.silu(gate) * upward


def block_step(state_value, pieces):
    query, key, value_rows, decay = pieces
    running = jnp.cumsum(decay, axis=0)
    final_state = running[-1]
    lifted_output = query * jnp.exp(running)
    lowered = key * jnp.exp(-running)
    scores = jnp.einsum("thk,shk->hts", lifted_output, lowered, precision=MATMUL_PRECISION)
    length = decay.shape[0]
    lower = jnp.arange(length)[:, None] >= jnp.arange(length)[None, :]
    scores = jnp.where(lower[None], scores, 0.0)
    mixed_output = jnp.einsum(
        "wlc,lcg->wlg", lifted_output, state_value, precision=MATMUL_PRECISION
    )
    mixed_output = mixed_output + jnp.einsum(
        "hts,shv->thv", scores, value_rows, precision=MATMUL_PRECISION
    )
    carried_state = key * jnp.exp(final_state[None] - running)
    state_value = jnp.exp(final_state)[:, :, None] * state_value + jnp.einsum(
        "nps,npx->psx", carried_state, value_rows, precision=MATMUL_PRECISION
    )
    return (state_value, mixed_output)


def block_scan(query, key, value_rows, decay, state_value):
    length, heads, kdim = query.shape
    vdim = value_rows.shape[2]
    count = length // BLOCK_LEN
    pieces = (
        query.reshape(count, BLOCK_LEN, heads, kdim),
        key.reshape(count, BLOCK_LEN, heads, kdim),
        value_rows.reshape(count, BLOCK_LEN, heads, vdim),
        decay.reshape(count, BLOCK_LEN, heads, kdim),
    )
    state_value, mixed_output = lax.scan(jax.checkpoint(block_step), state_value, pieces)
    return (state_value, mixed_output.reshape(length, heads, vdim))


def local_mixer(query, key, value_rows, decay):
    scaled = query * KD ** (-0.5)
    zeros = jnp.zeros((query.shape[1], KD, value_rows.shape[2]), jnp.float32)
    state_end, mixed_output = block_scan(scaled, key, value_rows, decay, zeros)
    running = jnp.cumsum(decay, axis=0)
    return (state_end, mixed_output, scaled * jnp.exp(running), jnp.exp(running[-1]))


def chain_join(earlier, later):
    return (earlier[0] * later[0], later[0][:, :, None] * earlier[1] + later[1])


def body(
    tokens,
    mix_gain,
    w_query,
    w_key,
    w_value,
    w_outgate,
    w_lowrank,
    w_rate,
    rate_bias,
    head_gain,
    w_output,
    mlp_gain,
    w_gate,
    w_up,
    w_down,
    cotangent,
):
    (
        full_query,
        full_key,
        full_value,
        full_outgate,
        full_lowrank,
        full_output,
        full_gate,
        full_up,
        full_down,
    ) = (
        lax.all_gather(w_query, ("dp", "seq"), axis=0, tiled=True),
        lax.all_gather(w_key, ("dp", "seq"), axis=0, tiled=True),
        lax.all_gather(w_value, ("dp", "seq"), axis=0, tiled=True),
        lax.all_gather(w_outgate, ("dp", "seq"), axis=0, tiled=True),
        lax.all_gather(w_lowrank, ("dp", "seq"), axis=0, tiled=True),
        lax.all_gather(w_output, ("dp", "seq"), axis=1, tiled=True),
        lax.all_gather(w_gate, ("dp", "seq"), axis=0, tiled=True),
        lax.all_gather(w_up, ("dp", "seq"), axis=0, tiled=True),
        lax.all_gather(w_down, ("dp", "seq"), axis=1, tiled=True),
    )
    length = tokens.shape[0]
    heads = w_query.shape[1] // KD
    inputs = tokens.astype(jnp.float32)
    normed, norm_back = jax.vjp(rms_norm, inputs, mix_gain)
    normed_low = normed.astype(jnp.bfloat16)
    query = matmul(normed_low, full_query).reshape(length, heads, KD)
    key = matmul(normed_low, full_key).reshape(length, heads, KD)
    value_rows = matmul(normed_low, full_value).reshape(length, heads, VD)
    outgate = matmul(normed_low, full_outgate).reshape(length, heads, VD)
    rank_part = matmul(normed_low, full_lowrank).astype(jnp.bfloat16)
    logit = matmul(rank_part, w_rate) + rate_bias
    decay = (jax.nn.log_sigmoid(logit) / normalizer).reshape(length, heads, KD)
    (state_end, local_output, lifted_output, edge), mixer_back = jax.vjp(
        local_mixer, query, key, value_rows, decay
    )
    identity = (jnp.ones_like(edge), jnp.zeros_like(state_end))
    incoming_state = entering((edge, state_end), "seq", chain_join, identity)[1]
    mixed_output = local_output + jnp.einsum(
        "wlc,lcg->wlg", lifted_output, incoming_state, precision=MATMUL_PRECISION
    )
    gated, gated_back = jax.vjp(head_norm, mixed_output, outgate, head_gain)
    gated_low = gated.reshape(length, -1).astype(jnp.bfloat16)
    mixer = lax.psum(matmul(gated_low, full_output), "head")
    middle = inputs + mixer
    normed2, norm2_back = jax.vjp(rms_norm, middle, mlp_gain)
    normed2_low = normed2.astype(jnp.bfloat16)
    gate = matmul(normed2_low, full_gate)
    upward = matmul(normed2_low, full_up)
    hidden, swiglu_back = jax.vjp(swiglu, gate, upward)
    hidden_low = hidden.astype(jnp.bfloat16)
    feed = lax.psum(matmul(hidden_low, full_down).astype(jnp.bfloat16), "head").astype(jnp.float32)
    result = (middle + feed).astype(jnp.bfloat16)
    (
        full_query,
        full_key,
        full_value,
        full_outgate,
        full_lowrank,
        full_output,
        full_gate,
        full_up,
        full_down,
    ) = (
        lax.all_gather(w_query, ("dp", "seq"), axis=0, tiled=True),
        lax.all_gather(w_key, ("dp", "seq"), axis=0, tiled=True),
        lax.all_gather(w_value, ("dp", "seq"), axis=0, tiled=True),
        lax.all_gather(w_outgate, ("dp", "seq"), axis=0, tiled=True),
        lax.all_gather(w_lowrank, ("dp", "seq"), axis=0, tiled=True),
        lax.all_gather(w_output, ("dp", "seq"), axis=1, tiled=True),
        lax.all_gather(w_gate, ("dp", "seq"), axis=0, tiled=True),
        lax.all_gather(w_up, ("dp", "seq"), axis=0, tiled=True),
        lax.all_gather(w_down, ("dp", "seq"), axis=1, tiled=True),
    )
    grad_result = cotangent.astype(jnp.float32)
    grad_down = inner(hidden_low, cotangent)
    grad_hidden = times_back(cotangent, full_down)
    gate_grad, upward_grad = swiglu_back(grad_hidden)
    gate_low = gate_grad.astype(jnp.bfloat16)
    upward_low = upward_grad.astype(jnp.bfloat16)
    grad_gate = inner(normed2_low, gate_low)
    grad_up = inner(normed2_low, upward_low)
    normed2_part = times_back(gate_low, full_gate) + times_back(upward_low, full_up)
    grad_normed2 = lax.psum(normed2_part, "head")
    middle_grad, grad_mlp_gain = norm2_back(grad_normed2)
    grad_middle = grad_result + middle_grad
    middle_low = grad_middle.astype(jnp.bfloat16)
    grad_output = inner(gated_low, middle_low)
    grad_gated = times_back(middle_low, full_output).reshape(length, heads, VD)
    mixed_gradient, outgate_grad, head_gain_part = gated_back(grad_gated)
    lifted_gradient = jnp.einsum(
        "ijd,jwd->ijw", mixed_gradient, incoming_state, precision=MATMUL_PRECISION
    )
    own_contribution = jnp.einsum(
        "nps,npx->psx", lifted_output, mixed_gradient, precision=MATMUL_PRECISION
    )
    outgoing = prefix((edge, own_contribution), "seq", chain_join, identity)[1]
    grad_edge = jnp.sum(incoming_state * outgoing, axis=2)
    query_grad, key_grad, value_grad, decay_grad = mixer_back(
        (outgoing, mixed_gradient, lifted_gradient, grad_edge)
    )
    query_low = query_grad.reshape(length, -1).astype(jnp.bfloat16)
    key_low = key_grad.reshape(length, -1).astype(jnp.bfloat16)
    value_low = value_grad.reshape(length, -1).astype(jnp.bfloat16)
    outgate_low = outgate_grad.reshape(length, -1).astype(jnp.bfloat16)
    logit_low = (decay_grad.reshape(length, -1) * jax.nn.sigmoid(-logit) / normalizer).astype(
        jnp.bfloat16
    )
    grad_rate = inner(rank_part, logit_low)
    grad_rate_bias = jnp.sum(logit_low.astype(jnp.float32), axis=0)
    rank_part_grad = times_back(logit_low, w_rate)
    normed_part = (
        times_back(query_low, full_query)
        + times_back(key_low, full_key)
        + times_back(value_low, full_value)
        + times_back(outgate_low, full_outgate)
    )
    normed_sum, rank_sum, grad_head_gain = (
        lax.psum(normed_part.astype(jnp.bfloat16), "head").astype(jnp.float32),
        lax.psum(rank_part_grad.astype(jnp.bfloat16), "head").astype(jnp.float32),
        lax.psum(head_gain_part.astype(jnp.bfloat16), "head").astype(jnp.float32),
    )
    rank_low = rank_sum.astype(jnp.bfloat16)
    grad_lowrank = inner(normed_low, rank_low)
    grad_normed = normed_sum + times_back(rank_low, full_lowrank)
    inputs_grad, grad_mix_gain = norm_back(grad_normed)
    grad_tokens = grad_middle + inputs_grad
    grad_query = inner(normed_low, query_low)
    grad_key = inner(normed_low, key_low)
    grad_value = inner(normed_low, value_low)
    grad_outgate = inner(normed_low, outgate_low)
    (
        sum_query,
        sum_key,
        sum_value,
        sum_outgate,
        sum_lowrank,
        sum_output,
        sum_gate,
        sum_up,
        sum_down,
    ) = (
        lax.psum_scatter(grad_query, ("dp", "seq"), scatter_dimension=0, tiled=True),
        lax.psum_scatter(grad_key, ("dp", "seq"), scatter_dimension=0, tiled=True),
        lax.psum_scatter(grad_value, ("dp", "seq"), scatter_dimension=0, tiled=True),
        lax.psum_scatter(grad_outgate, ("dp", "seq"), scatter_dimension=0, tiled=True),
        lax.psum_scatter(grad_lowrank, ("dp", "seq"), scatter_dimension=0, tiled=True),
        lax.psum_scatter(grad_output, ("dp", "seq"), scatter_dimension=1, tiled=True),
        lax.psum_scatter(grad_gate, ("dp", "seq"), scatter_dimension=0, tiled=True),
        lax.psum_scatter(grad_up, ("dp", "seq"), scatter_dimension=0, tiled=True),
        lax.psum_scatter(grad_down, ("dp", "seq"), scatter_dimension=1, tiled=True),
    )
    sum_mix_gain, sum_mlp_gain, sum_head_gain, sum_rate, sum_rate_bias = lax.psum(
        (grad_mix_gain, grad_mlp_gain, grad_head_gain, grad_rate, grad_rate_bias), ("dp", "seq")
    )
    return (
        result,
        grad_tokens,
        sum_mix_gain,
        sum_query,
        sum_key,
        sum_value,
        sum_outgate,
        sum_lowrank,
        sum_rate,
        sum_rate_bias,
        sum_head_gain,
        sum_output,
        sum_mlp_gain,
        sum_gate,
        sum_up,
        sum_down,
    )


def solution(mesh):
    in_specs = (
        P(("dp", "seq"), None),
        P(),
        P(("dp", "seq"), "head"),
        P(("dp", "seq"), "head"),
        P(("dp", "seq"), "head"),
        P(("dp", "seq"), "head"),
        P(("dp", "seq"), None),
        P(None, "head"),
        P("head"),
        P(),
        P("head", ("dp", "seq")),
        P(),
        P(("dp", "seq"), "head"),
        P(("dp", "seq"), "head"),
        P("head", ("dp", "seq")),
        P(("dp", "seq"), None),
    )
    out_specs = (
        P(("dp", "seq"), None),
        P(("dp", "seq"), None),
        P(),
        P(("dp", "seq"), "head"),
        P(("dp", "seq"), "head"),
        P(("dp", "seq"), "head"),
        P(("dp", "seq"), "head"),
        P(("dp", "seq"), None),
        P(None, "head"),
        P("head"),
        P(),
        P("head", ("dp", "seq")),
        P(),
        P(("dp", "seq"), "head"),
        P(("dp", "seq"), "head"),
        P("head", ("dp", "seq")),
    )
    return jax.shard_map(body, mesh=mesh, in_specs=in_specs, out_specs=out_specs, check_vma=False)
```

profile of v0, /device:TPU:0, one launch (start us, length us, event | category | flops | bytes accessed | tf_op | source)
XLA Modules:
  0.0 2459.9 jit_solution(9100848607073848060)
XLA Ops:
  9.5 23.5 all_gather.56
  40.5 14.4 all-gather.13.cloned.1.call-done
  60.9 37.0 %all-gather.17.cloned.1.call-done = bf16[2048,512]{1,0:T(8,128)(2,1)} async-done(((bf16[128,512]{1,0:T(8,128)(2,1)}), bf16[2048,512]{1,0:T(8,128)(2,1)}) %all-gather.17.cloned.1.call-update) | async-done | bytes 2097168 | tf_op jit(solution)/shard_map/all_gather | solution.py:164
  103.9 50.3 %all-gather.15.cloned.1.call-done = bf16[2048,1024]{1,0:T(8,128)(2,1)} async-done(((bf16[128,1024]{1,0:T(8,128)(2,1)}), bf16[2048,1024]{1,0:T(8,128)(2,1)}) %all-gather.15.cloned.1.call-update) | async-done | bytes 4194320 | tf_op jit(solution)/shard_map/all_gather | solution.py:166
  154.3 5.2 fusion.97
  165.7 45.6 %while.68 = (s32[]{:T(128)}, f32[2,256,512]{2,1,0:T(8,128)S(1)}, f32[6,64,2,512]{3,1,0,2:T(8,128)}, f32[6,2,256,512]{3,2,1,0:T(8,128)}, f32[6,64,2,256]{3,2,1,0:...) while((s32[]{:T(128)}, f32[2,256,512]{2,1,0:T(8,128)S(1)}, ...), condition=%wide.region_3.4_spmd.clone, body=%wide.region_1.3_spmd.clone.sunk | while | flops 481763328 | bytes 8209553 | solution.py:119
  219.8 8.9 all_gather.60
  239.2 26.8 %all-gather.29.cloned.1.call-done = f32[16,256,512]{2,1,0:T(8,128)} async-done(((f32[2,256,512]{2,1,0:T(8,128)}), f32[16,256,512]{2,1,0:T(8,128)}) %all-gather.29.cloned.1.call-update) | async-done | bytes 8388624 | tf_op jit(solution)/shard_map/all_gather | solution.py:18
  266.0 12.3 while.69
  278.3 5.0 multiply_reduce_fusion.6
  283.3 39.9 %all-gather.19.cloned.1.call-done = bf16[2048,1024]{1,0:T(8,128)(2,1)} async-done(((bf16[128,1024]{1,0:T(8,128)(2,1)}), bf16[2048,1024]{1,0:T(8,128)(2,1)}) %all-gather.19.cloned.1.call-update) | async-done | bytes 4194320 | tf_op jit(solution)/shard_map/all_gather | solution.py:167
  323.2 6.7 multiply_convert_fusion.3
  329.9 60.5 %all-gather.21.cloned.1.call-done = bf16[1024,2048]{1,0:T(8,128)(2,1)} async-done(((bf16[1024,128]{1,0:T(8,128)(2,1)}), bf16[1024,2048]{1,0:T(8,128)(2,1)}) %all-gather.21.cloned.1.call-update) | async-done | bytes 4194320 | tf_op jit(solution)/shard_map/all_gather | solution.py:169
  390.4 5.9 fusion.103
  398.8 83.0 %all-reduce.9.cloned.1.call-done = f32[384,2048]{1,0:T(8,128)} async-done(((f32[384,2048]{1,0:T(8,128)}), f32[384,2048]{1,0:T(8,128)}) %all-reduce.9.cloned.1.call-update) | async-done | bytes 3145744 | tf_op jit(solution)/shard_map/psum | solution.py:196
  487.4 99.0 %all-gather.23.cloned.1.call-done = bf16[2048,2816]{1,0:T(8,128)(2,1)} async-done(((bf16[128,2816]{1,0:T(8,128)(2,1)}), bf16[2048,2816]{1,0:T(8,128)(2,1)}) %all-gather.23.cloned.1.call-update) | async-done | bytes 11534352 | tf_op jit(solution)/shard_map/all_gather | solution.py:170
  586.4 11.4 fusion.104
  597.7 92.2 %all-gather.25.cloned.1.call-done = bf16[2048,2816]{1,0:T(8,128)(2,1)} async-done(((bf16[128,2816]{1,0:T(8,128)(2,1)}), bf16[2048,2816]{1,0:T(8,128)(2,1)}) %all-gather.25.cloned.1.call-update) | async-done | bytes 11534352 | tf_op jit(solution)/shard_map/all_gather | solution.py:171
  689.9 11.4 fusion.105
  701.3 122.3 %all-gather.27.cloned.1.call-done = bf16[2816,2048]{1,0:T(8,128)(2,1)} async-done(((bf16[2816,128]{1,0:T(8,128)(2,1)}), bf16[2816,2048]{1,0:T(8,128)(2,1)}) %all-gather.27.cloned.1.call-update) | async-done | bytes 11534352 | tf_op jit(solution)/shard_map/all_gather | solution.py:172
  823.6 12.6 multiply_convert_fusion
  836.2 9.1 fusion.106
  845.3 10.6 convolution_add_fusion.4
  856.2 85.3 %all-reduce.11.cloned.1.call-done = f32[384,2048]{1,0:T(8,128)} async-done(((f32[384,2048]{1,0:T(8,128)}), f32[384,2048]{1,0:T(8,128)}) %all-reduce.11.cloned.1.call-update) | async-done | bytes 3145744 | tf_op jit(solution)/shard_map/psum | solution.py:236
  941.5 4.4 multiply_reduce_fusion.1
  959.0 9.1 all_gather.68
  968.2 10.7 convolution_convert_fusion
  988.2 6.0 fusion.110
  996.0 9.6 while.66
  1010.7 89.8 %while.67 = (s32[]{:T(128)}, f32[2,256,512]{2,1,0:T(8,128)S(1)}, f32[6,64,2,256]{3,1,0,2:T(8,128)}, bf16[6,64,2,256]{3,1,2,0:T(8,128)(2,1)}, bf16[6,64,2,512]{3,...) while((s32[]{:T(128)}, f32[2,256,512]{2,1,0:T(8,128)S(1)}, ...), condition=%wide.region_22.23_spmd, body=%wide.region_17.22_spmd.sunk | while | flops 987811840 | bytes 19415228 | solution.py:119
  1113.5 5.8 fusion.64
  1122.1 8.6 all-reduce.3
  1140.1 5.9 fusion.86
  1147.1 7.7 fusion.75
  1156.0 5.8 fusion.88
  1163.3 12.8 fusion.112
  1176.3 12.4 fusion.113
  1190.1 12.4 fusion.114
  1203.8 4.4 fusion.55
  1208.1 58.3 %all-reduce.2 = (f32[2048]{0:T(1024)}, f32[16,512]{1,0:T(8,128)}, f32[512]{0:T(512)}, f32[512]{0:T(512)}, f32[2048]{0:T(1024)}) all-reduce(f32[2048]{0:T(1024)S(1)} %get-tuple-element.687, f32[16,512]{1,0:T(8,128)S(1)} %fusion.111, f32[512]{0:T(512)S(1)} %get-tuple-element.762, ...), channel_id=1, replica_groups=mesh['dp'=2,'seq'=8,'head'=2] {'dp','seq'}, use_global_device_ids=true, to_apply=%region_30.31 | all-reduce | flops 13312 | bytes 105472 | tf_op jit(solution)/shard_map/psum | solution.py:305
  1273.3 63.0 %reduce-scatter.10.cloned.1.call-done = f32[128,512]{1,0:T(8,128)} async-done(((f32[2048,512]{1,0:T(8,128)}), f32[128,512]{1,0:T(8,128)}) %reduce-scatter.10.cloned.1.call-update) | async-done | bytes 262160 | tf_op jit(solution)/shard_map/reduce_scatter | solution.py:295
  1336.3 72.9 %reduce-scatter.12.cloned.1.call-done = f32[128,512]{1,0:T(8,128)} async-done(((f32[2048,512]{1,0:T(8,128)}), f32[128,512]{1,0:T(8,128)}) %reduce-scatter.12.cloned.1.call-update) | async-done | bytes 262160 | tf_op jit(solution)/shard_map/reduce_scatter | solution.py:296
  1409.2 100.0 %reduce-scatter.16.cloned.1.call-done = f32[128,1024]{1,0:T(8,128)} async-done(((f32[2048,1024]{1,0:T(8,128)}), f32[128,1024]{1,0:T(8,128)}) %reduce-scatter.16.cloned.1.call-update) | async-done | bytes 524304 | tf_op jit(solution)/shard_map/reduce_scatter | solution.py:298
  1509.2 99.8 %reduce-scatter.20.cloned.1.call-done = f32[1024,128]{1,0:T(8,128)} async-done(((f32[1024,2048]{1,0:T(8,128)}), f32[1024,128]{1,0:T(8,128)}) %reduce-scatter.20.cloned.1.call-update) | async-done | bytes 524304 | tf_op jit(solution)/shard_map/reduce_scatter | solution.py:300
  1609.0 99.9 %reduce-scatter.14.cloned.1.call-done = f32[128,1024]{1,0:T(8,128)} async-done(((f32[2048,1024]{1,0:T(8,128)}), f32[128,1024]{1,0:T(8,128)}) %reduce-scatter.14.cloned.1.call-update) | async-done | bytes 524304 | tf_op jit(solution)/shard_map/reduce_scatter | solution.py:297
  1708.9 244.4 %reduce-scatter.22.cloned.1.call-done = f32[128,2816]{1,0:T(8,128)} async-done(((f32[2048,2816]{1,0:T(8,128)}), f32[128,2816]{1,0:T(8,128)}) %reduce-scatter.22.cloned.1.call-update) | async-done | bytes 1441808 | tf_op jit(solution)/shard_map/reduce_scatter | solution.py:301
  1953.3 249.7 %reduce-scatter.24.cloned.1.call-done = f32[128,2816]{1,0:T(8,128)} async-done(((f32[2048,2816]{1,0:T(8,128)}), f32[128,2816]{1,0:T(8,128)}) %reduce-scatter.24.cloned.1.call-update) | async-done | bytes 1441808 | tf_op jit(solution)/shard_map/reduce_scatter | solution.py:302
  2203.0 249.6 %reduce-scatter.26.cloned.1.call-done = f32[2816,128]{1,0:T(8,128)} async-done(((f32[2816,2048]{1,0:T(8,128)}), f32[2816,128]{1,0:T(8,128)}) %reduce-scatter.26.cloned.1.call-update) | async-done | bytes 1441808 | tf_op jit(solution)/shard_map/reduce_scatter | solution.py:303
  (467 shorter events, 277.7 us)
Async XLA Ops:
  7.2 29.8 %copy-start = (bf16[16,512]{1,0:T(8,128)(2,1)S(1)}, bf16[16,512]{1,0:T(8,128)(2,1)}, u32[]{:S(2)}) copy-start(bf16[16,512]{1,0:T(8,128)(2,1)} %param.31) | copy-start | bytes 49156
  7.2 29.8 %copy-start.49 = (f32[512]{0:T(512)S(1)}, f32[512]{0:T(512)}, u32[]{:S(2)}) copy-start(f32[512]{0:T(512)} %param.32) | copy-start | bytes 6148
  7.2 47.6 %all-gather.13.cloned.1.call-start = ((), (), s32[]{:S(2)}) async-start(), calls=%async_computation.9 | async-start | bytes 2228224 | tf_op jit(solution)/shard_map/all_gather | solution.py:165
  7.9 89.9 %all-gather.17.cloned.1.call-start = ((), (), s32[]{:S(2)}) async-start(), calls=%async_computation.11 | async-start | bytes 2228224 | tf_op jit(solution)/shard_map/all_gather | solution.py:164
  8.7 145.6 %all-gather.15.cloned.1.call-start = ((), (), s32[]{:S(2)}) async-start(), calls=%async_computation.10 | async-start | bytes 4456448 | tf_op jit(solution)/shard_map/all_gather | solution.py:166
  9.4 256.5 %all-gather.29.cloned.1.call-start = ((), (), s32[]{:S(2)}) async-start(), calls=%async_computation.28 | async-start | bytes 9437184 | tf_op jit(solution)/shard_map/all_gather | solution.py:18
  33.0 5.8 copy-start.40
  34.8 4.0 copy-start.43
  34.9 20.0 copy-start.2
  34.9 20.0 copy-start.34
  211.4 5.2 copy-start.18
  212.4 110.9 %all-gather.19.cloned.1.call-start = ((), (), s32[]{:S(2)}) async-start(), calls=%async_computation.12 | async-start | bytes 4456448 | tf_op jit(solution)/shard_map/all_gather | solution.py:167
  213.0 177.4 %all-gather.21.cloned.1.call-start = ((), (), s32[]{:S(2)}) async-start(), calls=%async_computation.13 | async-start | bytes 4456448 | tf_op jit(solution)/shard_map/all_gather | solution.py:169
  213.5 268.3 %all-reduce.9.cloned.1.call-start = ((), (), s32[]{:S(2)}) async-start(), calls=%async_computation.14 | async-start | bytes 6291456 | tf_op jit(solution)/shard_map/psum | solution.py:196
  278.2 703.7 %copy-start.5 = (f32[2,256,512]{2,1,0:T(8,128)}, f32[2,256,512]{2,1,0:T(8,128)S(1)}, u32[]{:S(2)}) copy-start(f32[2,256,512]{2,1,0:T(8,128)S(1)} %get-tuple-element.523) | copy-start | bytes 3145732
  278.2 45.0 %copy-start.45 = (f32[512]{0:T(512)S(1)}, f32[512]{0:T(512)}, u32[]{:S(2)}) copy-start(f32[512]{0:T(512)} %param.33) | copy-start | bytes 6148
  396.3 190.1 %all-gather.23.cloned.1.call-start = ((), (), s32[]{:S(2)}) async-start(), calls=%async_computation.15 | async-start | bytes 12255232 | tf_op jit(solution)/shard_map/all_gather | solution.py:170
  397.1 292.9 %all-gather.25.cloned.1.call-start = ((), (), s32[]{:S(2)}) async-start(), calls=%async_computation.16 | async-start | bytes 12255232 | tf_op jit(solution)/shard_map/all_gather | solution.py:171
  397.8 425.8 %all-gather.27.cloned.1.call-start = ((), (), s32[]{:S(2)}) async-start(), calls=%async_computation.17 | async-start | bytes 12255232 | tf_op jit(solution)/shard_map/all_gather | solution.py:172
  398.4 87.5 %copy-start.39 = (f32[2048]{0:T(1024)S(1)}, f32[2048]{0:T(1024)}, u32[]{:S(2)}) copy-start(f32[2048]{0:T(1024)} %param.35) | copy-start | bytes 24580
  398.4 543.1 %all-reduce.11.cloned.1.call-start = ((), (), s32[]{:S(2)}) async-start(), calls=%async_computation.18 | async-start | bytes 6291456 | tf_op jit(solution)/shard_map/psum | solution.py:236
  836.2 9.1 copy-start.31
  836.2 9.1 copy-start.30
  855.9 139.9 %all-gather.31.cloned.1.call-start = ((), (), s32[]{:S(2)}) async-start(), calls=%async_computation.29 | async-start | bytes 4718592 | tf_op jit(solution)/shard_map/all_gather | solution.py:38
  941.5 4.4 copy-start.4
  941.5 4.7 copy-start.12
  948.8 3.0 copy-start.9
  953.2 3.1 copy-start.15
  959.0 244.7 %all-reduce.13.cloned.1.call-start = ((), (), s32[]{:S(2)}) async-start(), calls=%async_computation.30 | async-start | bytes 6291456 | tf_op jit(solution)/shard_map/psum | solution.py:204
  1100.4 3.0 copy-start.16
  1100.4 3.0 copy-start.25
  1102.6 3.5 copy-start.35
  1102.7 3.8 copy-start.27
  1103.4 3.1 copy-start.48
  1113.3 160.0 %reduce-scatter.18.cloned.1.call-start = ((), (), s32[]{:S(2)}) async-start(), calls=%async_computation.23 | async-start | bytes 139264 | tf_op jit(solution)/shard_map/reduce_scatter | solution.py:299
  1131.9 204.4 %reduce-scatter.10.cloned.1.call-start = ((), (), s32[]{:S(2)}) async-start(), calls=%async_computation.19 | async-start | bytes 4456448 | tf_op jit(solution)/shard_map/reduce_scatter | solution.py:295
  1135.5 273.7 %reduce-scatter.12.cloned.1.call-start = ((), (), s32[]{:S(2)}) async-start(), calls=%async_computation.20 | async-start | bytes 4456448 | tf_op jit(solution)/shard_map/reduce_scatter | solution.py:296
  1139.0 370.3 %reduce-scatter.16.cloned.1.call-start = ((), (), s32[]{:S(2)}) async-start(), calls=%async_computation.22 | async-start | bytes 8912896 | tf_op jit(solution)/shard_map/reduce_scatter | solution.py:298
  1146.0 463.0 %reduce-scatter.20.cloned.1.call-start = ((), (), s32[]{:S(2)}) async-start(), calls=%async_computation.24 | async-start | bytes 8912896 | tf_op jit(solution)/shard_map/reduce_scatter | solution.py:300
  1154.9 554.0 %reduce-scatter.14.cloned.1.call-start = ((), (), s32[]{:S(2)}) async-start(), calls=%async_computation.21 | async-start | bytes 8912896 | tf_op jit(solution)/shard_map/reduce_scatter | solution.py:297
  1161.8 791.5 %reduce-scatter.22.cloned.1.call-start = ((), (), s32[]{:S(2)}) async-start(), calls=%async_computation.25 | async-start | bytes 24510464 | tf_op jit(solution)/shard_map/reduce_scatter | solution.py:301
  1176.2 1026.8 %reduce-scatter.24.cloned.1.call-start = ((), (), s32[]{:S(2)}) async-start(), calls=%async_computation.26 | async-start | bytes 24510464 | tf_op jit(solution)/shard_map/reduce_scatter | solution.py:302
  1188.7 1263.9 %reduce-scatter.26.cloned.1.call-start = ((), (), s32[]{:S(2)}) async-start(), calls=%async_computation.27 | async-start | bytes 24510464 | tf_op jit(solution)/shard_map/reduce_scatter | solution.py:303
  1203.7 4.4 copy-start.42
  1203.7 62.7 %copy-start.44 = (f32[384]{0:T(512)S(1)}, f32[384]{0:T(512)}, u32[]{:S(2)}) copy-start(f32[384]{0:T(512)} %copy-done.43) | copy-start | bytes 4612
  1203.7 62.7 %copy-start.36 = (bf16[384,2048]{1,0:T(8,128)(2,1)S(1)}, bf16[384,2048]{1,0:T(8,128)(2,1)}, u32[]{:S(2)}) copy-start(bf16[384,2048]{1,0:T(8,128)(2,1)} %get-tuple-element.760) | copy-start | bytes 4718596
  1266.5 3.7 copy-start.7
  1266.5 4.4 copy-start.23
  (24 other events, 37.1 us)
Sparse Core Ops, SparseCore 0:
  10.3 44.4 all-gather.12
  57.2 40.6 all-gather.16
  100.2 54.0 all-gather.14
  212.5 53.4 all-gather.28
  268.1 55.0 all-gather.18
  325.3 64.9 all-gather.20
  396.4 85.3 all-reduce.8
  484.4 101.9 all-gather.22
  588.9 100.9 all-gather.24
  692.3 131.2 all-gather.26
  856.1 85.3 all-reduce.10
  959.1 36.6 all-gather.30
  1113.4 85.7 all-reduce.12
  1201.9 62.0 reduce-scatter.17
  1266.7 69.5 reduce-scatter.9
  1339.1 70.0 reduce-scatter.11
  1411.9 97.2 reduce-scatter.15
  1512.0 96.9 reduce-scatter.19
  1611.9 96.9 reduce-scatter.13
  1711.6 241.6 reduce-scatter.21
  1956.2 246.7 reduce-scatter.23
  2205.9 246.7 reduce-scatter.25
where the time goes:
time: 2470 us; the launch traced here: 2460 us
  waiting for transfers between devices  1900 us (77%)
  matrix products  269 us (11%)
  blocking collectives  108 us (4%)
  local copies, waits for them, and re-layouts  87.3 us (4%)
  other arithmetic  78.5 us (3%)
    reduce_scatter x1, waiting for transfers between devices, body(): lax.psum_scatter(grad_up, ('dp', 'seq'), scatter_dimension=0, tiled=True)  250 us
    reduce_scatter x1, waiting for transfers between devices, body(): lax.psum_scatter(grad_down, ('dp', 'seq'), scatter_dimension=1, tiled=True)  250 us
    reduce_scatter x1, waiting for transfers between devices, body(): lax.psum_scatter(grad_gate, ('dp', 'seq'), scatter_dimension=0, tiled=True)  244 us
    all_gather x1, waiting for transfers between devices, body(): lax.all_gather(w_down, ('dp', 'seq'), axis=1, tiled=True)  122 us
    reduce_scatter x1, waiting for transfers between devices, body(): lax.psum_scatter(grad_outgate, ('dp', 'seq'), scatter_dimension=0, tiled=...  100 us
    reduce_scatter x1, waiting for transfers between devices, body(): lax.psum_scatter(grad_value, ('dp', 'seq'), scatter_dimension=0, tiled=True)  99.9 us
    reduce_scatter x1, waiting for transfers between devices, body(): lax.psum_scatter(grad_output, ('dp', 'seq'), scatter_dimension=1, tiled=T...  99.8 us
    all_gather x1, waiting for transfers between devices, body(): lax.all_gather(w_gate, ('dp', 'seq'), axis=0, tiled=True)  99 us
  transfers between devices with their start and end apart: 22, of which 20 were waited for; matrix products, arithmetic and copies ran while one was open for 8% of the time, Pallas kernels for 0%

commit v1 on v0

v1 whole, which is shorter than its diff:
```python
import jax
import jax.numpy as jnp
from jax import lax
from jax.sharding import PartitionSpec as P

KD = 256
VD = 512
BLOCK_LEN = 64

epsilon = 1e-06
normalizer = 16.0
MATMUL_PRECISION = lax.Precision.HIGHEST
BF16 = jnp.bfloat16
F32 = jnp.float32
CORE = 1


def swap(x, axis, bit=1):
    count = lax.axis_size(axis)
    return lax.ppermute(x, axis, [(i, i ^ bit) for i in range(count)])


def matmul(left, right):
    return jnp.dot(left, right, preferred_element_type=F32)


def inner(left, right):
    return lax.dot_general(left, right, (((0,), (0,)), ((), ())), preferred_element_type=F32)


def times_back(grad, weight):
    return lax.dot_general(grad, weight, (((1,), (1,)), ((), ())), preferred_element_type=F32)


def rms_norm(x, gain):
    return x * lax.rsqrt(jnp.mean(x * x, axis=-1, keepdims=True) + epsilon) * gain


def head_norm(mixed_output, outgate, gain):
    return rms_norm(mixed_output, gain) * jax.nn.silu(outgate)


def swiglu(gate, upward):
    return jax.nn.silu(gate) * upward


def block_step(state_value, pieces):
    query, key, value_rows, decay = pieces
    running = jnp.cumsum(decay, axis=0)
    final_state = running[-1]
    lifted_output = query * jnp.exp(running)
    lowered = key * jnp.exp(-running)
    scores = jnp.einsum("thk,shk->hts", lifted_output, lowered, precision=MATMUL_PRECISION)
    length = decay.shape[0]
    lower = jnp.arange(length)[:, None] >= jnp.arange(length)[None, :]
    scores = jnp.where(lower[None], scores, 0.0)
    mixed_output = jnp.einsum(
        "wlc,lcg->wlg", lifted_output, state_value, precision=MATMUL_PRECISION
    )
    mixed_output = mixed_output + jnp.einsum(
        "hts,shv->thv", scores, value_rows, precision=MATMUL_PRECISION
    )
    carried_state = key * jnp.exp(final_state[None] - running)
    state_value = jnp.exp(final_state)[:, :, None] * state_value + jnp.einsum(
        "nps,npx->psx", carried_state, value_rows, precision=MATMUL_PRECISION
    )
    return (state_value, mixed_output)


def block_scan(query, key, value_rows, decay, state_value):
    length, heads, kdim = query.shape
    vdim = value_rows.shape[2]
    count = length // BLOCK_LEN
    pieces = (
        query.reshape(count, BLOCK_LEN, heads, kdim),
        key.reshape(count, BLOCK_LEN, heads, kdim),
        value_rows.reshape(count, BLOCK_LEN, heads, vdim),
        decay.reshape(count, BLOCK_LEN, heads, kdim),
    )
    state_value, mixed_output = lax.scan(jax.checkpoint(block_step), state_value, pieces)
    return (state_value, mixed_output.reshape(length, heads, vdim))


def local_mixer(query, key, value_rows, decay):
    scaled = query * KD ** (-0.5)
    zeros = jnp.zeros((query.shape[1], KD, value_rows.shape[2]), F32)
    state_end, mixed_output = block_scan(scaled, key, value_rows, decay, zeros)
    running = jnp.cumsum(decay, axis=0)
    return (state_end, mixed_output, scaled * jnp.exp(running), jnp.exp(running[-1]))


def chip_bits():
    bits, bit = [], 2
    while bit < lax.axis_size("seq"):
        bits.append(bit)
        bit *= 2
    return bits


def paths():
    bits = chip_bits()
    return bits, bits[::-1]


def spread(half, path):
    for bit in path:
        half = jnp.concatenate([half, swap(half, "seq", bit)], 0)
    return half


def order():
    blocks = []
    chip = lax.axis_index("seq") // 2
    dp = lax.axis_index("dp")
    chips = lax.axis_size("seq") // 2
    for away in range(2):
        for half, path in enumerate(paths()):
            near = [0]
            for bit in path:
                near = near + [place ^ (bit // 2) for place in near]
            blocks += [(((dp ^ away) * chips + (chip ^ place)) * 2 + half) for place in near]
    return blocks


def gather(first, second):
    far_first, far_second = swap(first, "dp"), swap(second, "dp")
    one, two = paths()
    return jnp.concatenate(
        [spread(first, one), spread(second, two), spread(far_first, one), spread(far_second, two)],
        0,
    )


def collect(part, path):
    for bit in path[::-1]:
        length = part.shape[0] // 2
        sent = swap(part[length:].astype(BF16), "seq", bit)
        part = part[:length].astype(F32) + sent.astype(F32)
    return part


def scatter(left, right):
    quarter = left.shape[1] // 4
    one, two = paths()
    sums = []
    for i, path in ((2, one), (3, two), (0, one), (1, two)):
        grad = inner(left[:, i * quarter : (i + 1) * quarter], right).astype(BF16)
        sums.append(collect(grad, path))
    far = [swap(part.astype(BF16), "dp") for part in sums[:2]]
    return [near + part.astype(F32) for near, part in zip(sums[2:], far)]


def both(x, core):
    other = swap(x, "seq", CORE)
    return jnp.concatenate([jnp.where(core == 0, x, other), jnp.where(core == 0, other, x)], 0)


def add_up(part, core):
    rows = part.shape[0] // 2
    mine = jnp.where(core == 0, part[:rows], part[rows:])
    theirs = jnp.where(core == 0, part[rows:], part[:rows])
    mine = mine + swap(theirs.astype(BF16), "seq", CORE).astype(F32)
    mine = mine.astype(BF16)
    return mine.astype(F32) + swap(mine, "head").astype(F32)


def incoming(edge, state, reverse=False):
    chips = lax.axis_size("seq") // 2
    chip = lax.axis_index("seq") // 2
    low = state.astype(BF16)

    def move(x, by):
        if reverse:
            by = -by
        pairs = []
        for i in range(chips):
            if 0 <= i + by < chips:
                for c in range(2):
                    pairs.append((2 * i + c, 2 * (i + by) + c))
        return lax.ppermute(x, "seq", pairs)

    total = jnp.zeros_like(state)
    faded = None
    edges = edge
    for by in range(1, chips):
        there = move(low, by).astype(F32)
        if by == 1:
            total = there
        else:
            total = total + faded[:, None] * there
        if by < chips - 1:
            gone = move(edge, by)
            faded = gone if faded is None else faded * gone
    return total


def body(
    tokens,
    mix_gain,
    w_query,
    w_key,
    w_value,
    w_outgate,
    w_lowrank,
    w_rate,
    rate_bias,
    head_gain,
    w_output,
    mlp_gain,
    w_gate,
    w_up,
    w_down,
    cotangent,
):
    core = lax.axis_index("seq") % 2
    blocks = order()
    place_of = jnp.stack(blocks)
    back_place = jnp.argsort(place_of)

    wide = tokens.shape[1] // len(blocks)

    def local(x):
        return jnp.concatenate(
            [lax.dynamic_slice_in_dim(x, b * wide, wide, x.ndim - 1) for b in blocks], x.ndim - 1
        )

    def whole(x):
        return jnp.concatenate(
            [
                lax.dynamic_slice_in_dim(x, back_place[i] * wide, wide, x.ndim - 1)
                for i in range(len(blocks))
            ],
            x.ndim - 1,
        )

    def split(w):
        half = w.shape[1] // 2
        mine = jnp.where(core == 0, w[:, :half], w[:, half:])
        theirs = jnp.where(core == 0, w[:, half:], w[:, :half])
        return mine, theirs

    def own_columns(weights):
        pairs = [split(w) for w in weights]
        mine = jnp.concatenate([p[0] for p in pairs], 1)
        got = swap(jnp.concatenate([p[1] for p in pairs], 1), "seq", CORE)
        return jnp.where(core == 0, mine, got), jnp.where(core == 0, got, mine)

    mixer_halves = own_columns([w_query, w_key, w_value, w_outgate])
    output_halves = own_columns([w_output.T])
    up_halves = own_columns([w_gate, w_up])
    down_halves = own_columns([w_down.T])
    low_full = lax.all_gather(w_lowrank.T, ("dp", "seq"), axis=1, tiled=True)
    w_mixer = gather(*mixer_halves)
    w_out = gather(*output_halves)
    w_gateup = gather(*up_halves)
    w_dn = gather(*down_halves)

    low_local = local(low_full)
    gain1, gain2 = local(mix_gain[None])[0], local(mlp_gain[None])[0]
    cot = local(cotangent)
    cot_both = both(cot, core)
    inputs = local(tokens).astype(F32)
    length = 2 * tokens.shape[0]

    normed, norm_back = jax.vjp(rms_norm, inputs, gain1)
    normed_own = normed.astype(BF16)
    normed_low = both(normed_own, core)
    projected = matmul(normed_low, w_mixer)
    query = projected[:, :KD].reshape(length, 1, KD)
    key = projected[:, KD : 2 * KD].reshape(length, 1, KD)
    value_rows = projected[:, 2 * KD : 2 * KD + VD].reshape(length, 1, VD)
    outgate = projected[:, 2 * KD + VD :]
    rank_part = times_back(normed_low, low_local).astype(BF16)
    rate = jnp.where(core == 0, w_rate[:, :KD], w_rate[:, KD:])
    bias = jnp.where(core == 0, rate_bias[:KD], rate_bias[KD:])
    logit = matmul(rank_part, rate) + bias
    decay = (jax.nn.log_sigmoid(logit) / normalizer).reshape(length, 1, KD)
    (state_end, local_output, lifted_output, edge), mixer_back = jax.vjp(
        local_mixer, query, key, value_rows, decay
    )
    incoming_state = incoming(edge[0], state_end[0])
    lifted = lifted_output[:, 0]
    mixed_output = local_output[:, 0] + jnp.dot(
        lifted, incoming_state, precision=MATMUL_PRECISION
    )
    gated, gated_back = jax.vjp(head_norm, mixed_output, outgate, head_gain)
    gated_low = gated.astype(BF16)
    middle = inputs + add_up(times_back(gated_low, w_out), core)
    normed2, norm2_back = jax.vjp(rms_norm, middle, gain2)
    normed2_low = both(normed2.astype(BF16), core)
    gateup = matmul(normed2_low, w_gateup)
    half = gateup.shape[1] // 2
    hidden, swiglu_back = jax.vjp(swiglu, gateup[:, :half], gateup[:, half:])
    hidden_low = hidden.astype(BF16)
    feed = add_up(times_back(hidden_low, w_dn), core)
    result = whole((middle + feed).astype(BF16))

    grad_down = scatter(cot_both, hidden_low)
    grad_hidden = matmul(cot_both, w_dn)
    gate_grad, upward_grad = swiglu_back(grad_hidden)
    gateup_low = jnp.concatenate([gate_grad.astype(BF16), upward_grad.astype(BF16)], 1)
    grad_normed2 = add_up(times_back(gateup_low, w_gateup), core)
    grad_gateup = scatter(normed2_low, gateup_low)
    middle_grad, grad_mlp_gain = norm2_back(grad_normed2)
    grad_middle = cot.astype(F32) + middle_grad
    middle_low = both(grad_middle.astype(BF16), core)
    grad_gated = matmul(middle_low, w_out)
    grad_output = scatter(middle_low, gated_low)
    mixed_gradient, outgate_grad, head_gain_part = gated_back(grad_gated)
    lifted_gradient = lax.dot_general(
        mixed_gradient, incoming_state, (((1,), (1,)), ((), ())), precision=MATMUL_PRECISION
    )
    own_contribution = lax.dot_general(
        lifted, mixed_gradient, (((0,), (0,)), ((), ())), precision=MATMUL_PRECISION
    )
    outgoing = incoming(edge[0], own_contribution, reverse=True)
    grad_edge = jnp.sum(incoming_state * outgoing, axis=1)
    query_grad, key_grad, value_grad, decay_grad = mixer_back(
        (outgoing[None], mixed_gradient[:, None], lifted_gradient[:, None], grad_edge[None])
    )
    mixer_low = jnp.concatenate(
        [
            query_grad.reshape(length, -1).astype(BF16),
            key_grad.reshape(length, -1).astype(BF16),
            value_grad.reshape(length, -1).astype(BF16),
            outgate_grad.astype(BF16),
        ],
        1,
    )
    logit_low = (decay_grad.reshape(length, -1) * jax.nn.sigmoid(-logit) / normalizer).astype(BF16)
    grad_rate = inner(rank_part, logit_low)
    grad_rate_bias = jnp.sum(logit_low.astype(F32), axis=0)
    rank_part_grad = times_back(logit_low, rate)
    rank_own = add_up(rank_part_grad, core).astype(BF16)
    normed_sum = add_up(times_back(mixer_low, w_mixer), core)
    grad_mixer = scatter(normed_low, mixer_low)
    grad_lowrank = whole(inner(rank_own, normed_own))
    grad_normed = normed_sum + matmul(rank_own, low_local)
    inputs_grad, grad_mix_gain = norm_back(grad_normed)
    grad_tokens = whole(grad_middle + inputs_grad)

    def own_rows(halves):
        mine = jnp.where(core == 0, halves[0], halves[1])
        theirs = jnp.where(core == 0, halves[1], halves[0])
        got = swap(theirs.astype(BF16), "seq", CORE).astype(F32)
        return jnp.where(core == 0, mine, got), jnp.where(core == 0, got, mine)

    def columns(pair, start, width):
        return jnp.concatenate([part[:, start : start + width] for part in pair], 1)

    mixer_pair = own_rows(grad_mixer)
    sum_query = columns(mixer_pair, 0, KD)
    sum_key = columns(mixer_pair, KD, KD)
    sum_value = columns(mixer_pair, 2 * KD, VD)
    sum_outgate = columns(mixer_pair, 2 * KD + VD, VD)
    output_pair = own_rows(grad_output)
    sum_output = columns(output_pair, 0, VD).T
    gateup_pair = own_rows(grad_gateup)
    sum_gate = columns(gateup_pair, 0, half)
    sum_up = columns(gateup_pair, half, half)
    down_pair = own_rows(grad_down)
    sum_down = columns(down_pair, 0, half).T

    zero = jnp.zeros_like(grad_rate)
    wide_rate = jnp.where(
        core == 0,
        jnp.concatenate([grad_rate, zero], 1),
        jnp.concatenate([zero, grad_rate], 1),
    )
    wide_bias = jnp.where(
        core == 0,
        jnp.concatenate([grad_rate_bias, zero[0]]),
        jnp.concatenate([zero[0], grad_rate_bias]),
    )
    sum_mix_gain, sum_mlp_gain, sum_rate, sum_rate_bias, sum_low = lax.psum(
        (
            whole(grad_mix_gain[None])[0],
            whole(grad_mlp_gain[None])[0],
            wide_rate,
            wide_bias,
            grad_lowrank,
        ),
        ("dp", "seq"),
    )
    sum_head_gain = lax.psum(head_gain_part, ("dp", "seq", "head"))
    spot = lax.axis_index("dp") * lax.axis_size("seq") + lax.axis_index("seq")
    sum_lowrank = lax.dynamic_slice_in_dim(sum_low, spot * wide, wide, 1).T
    return (
        result,
        grad_tokens,
        sum_mix_gain,
        sum_query,
        sum_key,
        sum_value,
        sum_outgate,
        sum_lowrank,
        sum_rate,
        sum_rate_bias,
        sum_head_gain,
        sum_output,
        sum_mlp_gain,
        sum_gate,
        sum_up,
        sum_down,
    )


def solution(mesh):
    rows = P(("dp", "seq"), None)
    in_columns = P(("dp", "seq"), "head")
    in_rows = P("head", ("dp", "seq"))
    in_specs = (
        rows,
        P(),
        in_columns,
        in_columns,
        in_columns,
        in_columns,
        rows,
        P(None, "head"),
        P("head"),
        P(),
        in_rows,
        P(),
        in_columns,
        in_columns,
        in_rows,
        rows,
    )
    out_specs = (
        rows,
        rows,
        P(),
        in_columns,
        in_columns,
        in_columns,
        in_columns,
        rows,
        P(None, "head"),
        P("head"),
        P(),
        in_rows,
        P(),
        in_columns,
        in_columns,
        in_rows,
    )
    return jax.shard_map(body, mesh=mesh, in_specs=in_specs, out_specs=out_specs, check_vma=False)
```

time: 2470 us -> 1420 us (0.57)
  waiting for transfers between devices: 1900 us -> 594 us
  starting transfers between devices: 2.35 us -> 123 us
  local copies, waits for them, and re-layouts: 87.3 us -> 178 us
  other arithmetic: 78.5 us -> 164 us
  matrix products: 269 us -> 196 us
    reduce_scatter x9 -> x0, waiting for transfers between devices: 1180 us -> none  [the longest x1 250 us: body(): lax.psum_scatter(grad_up, ('dp', 'seq'), scatter_dimension=0, tiled=True)]
    all_gather x10 -> x0, waiting for transfers between devices: 544 us -> none  [the longest x1 122 us: body(): lax.all_gather(w_down, ('dp', 'seq'), axis=1, tiled=True)]
    ppermute x0 -> x112, waiting for transfers between devices: none -> 517 us  [the longest x102 515 us: swap(): return lax.ppermute(x, axis, [(i, i ^ bit) for i in range(count)])]
    ppermute x0 -> x112, starting transfers between devices: none -> 123 us  [the longest x102 99.4 us: swap(): return lax.ppermute(x, axis, [(i, i ^ bit) for i in range(count)])]
    psum x3 -> x1, waiting for transfers between devices: 168 us -> 77.6 us  [body(): lax.psum((whole(grad_mix_gain[None])[0], whole(grad_mlp_gain[None])[0], w...]
    unnamed x104 -> x514, local copies, waits for them, and re-layouts: 20.3 us -> 74.4 us
    psum x2, blocking collectives: 66.9 us -> 101 us  [the longest x1 58.8 us: body(): lax.psum((whole(grad_mix_gain[None])[0], whole(grad_mlp_gain[None])[0], w...]
    convert_element_type x10 -> x27, other arithmetic: 5.24 us -> 37.1 us  [the longest x5 12.2 us: add_up(): mine = mine.astype(BF16)]
  transfers between devices with their start and end apart: 22 -> 113, of which waited for: 20 -> 44; matrix products, arithmetic and copies ran while one was open for 8% -> 31% of each run, Pallas kernels for 0% -> 0%
where the time goes in v1:
time: 1420 us; the launch traced here: 1410 us
  waiting for transfers between devices  594 us (42%)
  matrix products  196 us (14%)
  local copies, waits for them, and re-layouts  178 us (13%)
  other arithmetic  164 us (12%)
  blocking collectives  124 us (9%)
  starting transfers between devices  123 us (9%)
  between operations  27.5 us (2%)
    ppermute x102, waiting for transfers between devices, swap(): return lax.ppermute(x, axis, [(i, i ^ bit) for i in range(count)])  515 us
    ppermute x102, starting transfers between devices, swap(): return lax.ppermute(x, axis, [(i, i ^ bit) for i in range(count)])  99.4 us
    psum x1, waiting for transfers between devices, body(): lax.psum((whole(grad_mix_gain[None])[0], whole(grad_mlp_gain[None])[0], w...  77.6 us
    unnamed x514, local copies, waits for them, and re-layouts  74.4 us
    psum x1, blocking collectives, body(): lax.psum((whole(grad_mix_gain[None])[0], whole(grad_mlp_gain[None])[0], w...  58.8 us
    psum x1, blocking collectives, body(): sum_head_gain = lax.psum(head_gain_part, ('dp', 'seq', 'head'))  42.3 us
    dynamic_slice x60, local copies, waits for them, and re-layouts, block_scan(): lax.scan(jax.checkpoint(block_step), state_value, pieces)  36.7 us
    dot_general x6, matrix products, matmul(): return jnp.dot(left, right, preferred_element_type=F32)  36.7 us
  transfers between devices with their start and end apart: 113, of which 44 were waited for; matrix products, arithmetic and copies ran while one was open for 31% of the time, Pallas kernels for 0%

profile of v1, /device:TPU:0, one launch (start us, length us, event | category | flops | bytes accessed | tf_op | source)
XLA Modules:
  0.0 1409.5 jit_solution(11795972318370665655)
XLA Ops:
  27.5 22.7 %all_gather.3 = bf16[16,2048]{1,0:T(8,128)(2,1)S(1)} all-gather(bf16[16,128]{1,0:T(8,128)(2,1)S(1)} %bitcast.708), channel_id=1, replica_groups=mesh['dp'=2,'seq'=8,'head'=2] {'dp','seq'}, dimensions={1}, use_global_device_ids=true | all-gather | bytes 69632 | tf_op jit(solution)/shard_map/all_gather | solution.py:252
  81.0 6.9 collective-permute-done.22
  110.1 8.9 collective-permute-done.25
  129.6 15.6 %collective-permute-done.6 = bf16[128,1536]{1,0:T(8,128)(2,1)S(1)} collective-permute-done((bf16[128,1536]{1,0:T(8,128)(2,1)S(1)}, bf16[128,1536]{1,0:T(8,128)(2,1)S(1)}, u32[]{:S(2)}, u32[]{:S(2)}) %collective-permute-start.6) | collective-permute-done | bytes 393248 | tf_op jit(solution)/shard_map/ppermute | solution.py:20
  148.5 8.7 collective-permute-done.7
  161.7 10.0 collective-permute-done.32
  212.8 6.6 collective-permute-done.50
  219.4 24.9 %collective-permute-done.4 = bf16[128,1536]{1,0:T(8,128)(2,1)S(1)} collective-permute-done((bf16[128,1536]{1,0:T(8,128)(2,1)S(1)}, bf16[128,1536]{1,0:T(8,128)(2,1)S(1)}, u32[]{:S(2)}, u32[]{:S(2)}) %collective-permute-start.4) | collective-permute-done | bytes 393248 | tf_op jit(solution)/shard_map/ppermute | solution.py:20
  260.3 5.8 collective-permute-done.10
  273.6 12.4 collective-permute-done.5
  288.7 9.7 collective-permute-done.11
  298.4 5.0 fusion.96
  307.5 73.5 %while.41 = (s32[]{:T(128)}, f32[1,256,512]{2,1,0:T(8,128)S(1)}, f32[12,64,1,512]{3,1,2,0:T(8,128)}, f32[12,1,256,512]{3,2,1,0:T(8,128)}, f32[12,64,1,256]{3,2,1...) while((s32[]{:T(128)}, f32[1,256,512]{2,1,0:T(8,128)S(1)}, ...), condition=%wide.region_3.4_spmd.clone.clone, body=%wide.region_1.3_spmd.clone.sunk.clone | while | flops 240885760 | bytes 4626557 | solution.py:80
  381.1 6.6 collective-permute-start.16
  411.9 13.7 collective-permute-done.34
  428.0 15.4 %collective-permute-done.39 = bf16[128,2816]{1,0:T(8,128)(2,1)S(1)} collective-permute-done((bf16[128,2816]{1,0:T(8,128)(2,1)S(1)}, bf16[128,2816]{1,0:T(8,128)(2,1)S(1)}, u32[]{:S(2)}, u32[]{:S(2)}) %collective-permute-start.39) | collective-permute-done | bytes 720928 | tf_op jit(solution)/shard_map/ppermute | solution.py:20
  445.7 15.6 %collective-permute-done.40 = bf16[128,2816]{1,0:T(8,128)(2,1)S(1)} collective-permute-done((bf16[128,2816]{1,0:T(8,128)(2,1)S(1)}, bf16[128,2816]{1,0:T(8,128)(2,1)S(1)}, u32[]{:S(2)}, u32[]{:S(2)}) %collective-permute-start.40) | collective-permute-done | bytes 720928 | tf_op jit(solution)/shard_map/ppermute | solution.py:20
  465.6 15.0 %collective-permute-done.29 = bf16[384,2048]{1,0:T(8,128)(2,1)S(1)} collective-permute-done((bf16[384,2048]{1,0:T(8,128)(2,1)S(1)}, bf16[384,2048]{1,0:T(8,128)(2,1)S(1)}, u32[]{:S(2)}, u32[]{:S(2)}) %collective-permute-start.29) | collective-permute-done | bytes 1572896 | tf_op jit(solution)/shard_map/ppermute | solution.py:20
  488.7 5.5 collective-permute-done.41
  496.4 15.1 %fusion.92 = f32[768,2816]{1,0:T(8,128)} fusion(bf16[2048,2816]{1,0:T(8,128)(2,1)} %constant_dynamic-update-slice_fusion.88, bf16[384,2048]{1,0:T(8,128)(2,1)S(1)} %get-tuple-element.521, bf16[384,2048]{1,0:T(8,128)(2,1)S(1)} %get-tuple-element.520), kind=kOutput, calls=%fused_computation.181 | convolution fusion | flops 8864661504 | bytes 23330816 | tf_op jit(solution)/shard_map/dot_general | solution.py:24
  511.5 11.1 fusion.82
  522.6 12.9 fusion.200
  535.5 4.3 convolution_convert_fusion.2
  547.5 7.7 fusion.212
  571.1 10.3 collective-permute-done.103
  583.5 13.4 collective-permute-done.101
  601.0 12.1 collective-permute-done.106
  614.1 6.4 collective-permute-done.104
  622.1 41.3 %collective-permute-done.109 = bf16[128,1408]{1,0:T(8,128)(2,1)S(1)} collective-permute-done((bf16[128,1408]{1,0:T(8,128)(2,1)S(1)}, bf16[128,1408]{1,0:T(8,128)(2,1)S(1)}, u32[]{:S(2)}, u32[]{:S(2)}) %collective-permute-start.109) | collective-permute-done | bytes 360480 | tf_op jit(solution)/shard_map/ppermute | solution.py:20
  671.6 26.5 %collective-permute-done.97 = bf16[256,2816]{1,0:T(8,128)(2,1)} collective-permute-done((bf16[256,2816]{1,0:T(8,128)(2,1)S(1)}, bf16[256,2816]{1,0:T(8,128)(2,1)}, u32[]{:S(2)}, u32[]{:S(2)}) %collective-permute-start.97) | collective-permute-done | bytes 1441824 | tf_op jit(solution)/shard_map/ppermute | solution.py:20
  700.8 32.1 %collective-permute-done.102 = bf16[128,1408]{1,0:T(8,128)(2,1)S(1)} collective-permute-done((bf16[128,1408]{1,0:T(8,128)(2,1)S(1)}, bf16[128,1408]{1,0:T(8,128)(2,1)S(1)}, u32[]{:S(2)}, u32[]{:S(2)}) %collective-permute-start.102) | collective-permute-done | bytes 360480 | tf_op jit(solution)/shard_map/ppermute | solution.py:20
  739.6 16.5 %collective-permute-done.105 = bf16[128,1408]{1,0:T(8,128)(2,1)S(1)} collective-permute-done((bf16[128,1408]{1,0:T(8,128)(2,1)}, bf16[128,1408]{1,0:T(8,128)(2,1)S(1)}, u32[]{:S(2)}, u32[]{:S(2)}) %collective-permute-start.105) | collective-permute-done | bytes 360480 | tf_op jit(solution)/shard_map/ppermute | solution.py:20
  756.9 6.9 collective-permute-done.110
  775.4 7.4 collective-permute-done.98
  791.1 6.3 collective-permute-done.96
  797.4 27.6 %collective-permute-done.94 = bf16[128,2816]{1,0:T(8,128)(2,1)} collective-permute-done((bf16[128,2816]{1,0:T(8,128)(2,1)}, bf16[128,2816]{1,0:T(8,128)(2,1)}, u32[]{:S(2)}, u32[]{:S(2)}) %collective-permute-start.94) | collective-permute-done | bytes 720928 | tf_op jit(solution)/shard_map/ppermute | solution.py:20
  825.0 21.8 %collective-permute-done.99 = bf16[128,2816]{1,0:T(8,128)(2,1)} collective-permute-done((bf16[128,2816]{1,0:T(8,128)(2,1)}, bf16[128,2816]{1,0:T(8,128)(2,1)}, u32[]{:S(2)}, u32[]{:S(2)}) %collective-permute-start.99) | collective-permute-done | bytes 720928 | tf_op jit(solution)/shard_map/ppermute | solution.py:20
  880.6 42.3 %psum.46 = f32[512]{0:T(512)} all-reduce(f32[512]{0:T(512)S(1)} %get-tuple-element.417), channel_id=1, replica_groups=mesh['dp'=2,'seq'=8,'head'=2] {'dp','seq','head'}, use_global_device_ids=true, to_apply=%region_28.29 | all-reduce | flops 512 | bytes 4096 | tf_op jit(solution)/shard_map/psum | solution.py:385
  939.1 124.3 %while.40 = (s32[]{:T(128)}, f32[1,256,512]{1,2,0:T(8,128)S(1)}, f32[12,64,1,256]{3,1,2,0:T(8,128)}, bf16[12,64,1,256]{3,1,2,0:T(8,128)(2,1)S(1)}, bf16[12,64,1,...) while((s32[]{:T(128)}, f32[1,256,512]{1,2,0:T(8,128)S(1)}, ...), condition=%wide.region_16.17_spmd.clone, body=%wide.region_11.16_spmd.sunk.clone | while | flops 493912064 | bytes 10731689 | solution.py:80
  1070.0 10.3 fusion.201
  1090.9 4.4 select_convert_fusion
  1135.2 11.2 collective-permute-done.68
  1149.7 16.6 %collective-permute-done.73 = bf16[256,1536]{1,0:T(8,128)(2,1)S(1)} collective-permute-done((bf16[256,1536]{1,0:T(8,128)(2,1)}, bf16[256,1536]{1,0:T(8,128)(2,1)S(1)}, u32[]{:S(2)}, u32[]{:S(2)}) %collective-permute-start.73) | collective-permute-done | bytes 786464 | tf_op jit(solution)/shard_map/ppermute | solution.py:20
  1167.3 7.6 collective-permute-done.71
  1179.7 77.6 %all-reduce.9.cloned.1.call-done = f32[16,2048]{1,0:T(8,128)} async-done(((f32[16,2048]{1,0:T(8,128)}), f32[16,2048]{1,0:T(8,128)}) %all-reduce.9.cloned.1.call-update) | async-done | bytes 131088 | tf_op jit(solution)/shard_map/psum | solution.py:375
  1275.8 57.4 %collective-permute-done.65 = bf16[384,2048]{1,0:T(8,128)(2,1)S(1)} collective-permute-done((bf16[384,2048]{1,0:T(8,128)(2,1)S(1)}, bf16[384,2048]{1,0:T(8,128)(2,1)S(1)}, u32[]{:S(2)}, u32[]{:S(2)}) %collective-permute-start.65) | collective-permute-done | bytes 1572896 | tf_op jit(solution)/shard_map/ppermute | solution.py:20
  1335.1 4.9 fusion.89
  1343.7 58.8 %all-reduce.6 = (f32[2048]{0:T(1024)}, f32[16,512]{1,0:T(8,128)}, f32[512]{0:T(512)}, f32[2048]{0:T(1024)}) all-reduce(f32[2048]{0:T(1024)S(1)} %bitcast.705, f32[16,512]{1,0:T(8,128)S(1)} %copy-done.112, f32[512]{0:T(512)S(1)} %copy-done.141, f32[2048]{0:T(1024)S(1)} %bitcast.706), channel_id=1, replica_groups=mesh['dp'=2,'seq'=8,'head'=2] {'dp','seq'}, use_global_device_ids=true, to_apply=%region_22.23 | all-reduce | flops 12800 | bytes 102400 | tf_op jit(solution)/shard_map/psum | solution.py:375
  (1344 shorter events, 600.1 us)
Async XLA Ops:
  7.2 1250.2 %all-reduce.9.cloned.1.call-start = ((), (), s32[]{:S(2)}) async-start(), calls=%async_computation | async-start | bytes 262144 | tf_op jit(solution)/shard_map/psum | solution.py:375
  17.7 157.8 %collective-permute-start = (bf16[384,2048]{1,0:T(8,128)(2,1)}, bf16[384,2048]{1,0:T(8,128)(2,1)}, u32[]{:S(2)}, u32[]{:S(2)}) collective-permute-start(bf16[384,2048]{1,0:T(8,128)(2,1)} %fusion.86), channel_id=1, source_target_pairs={{0,2},{2,0},{4,6},{6,4},{8,10},{10,8},{12,14},{14,12},{1,3},{3,1},... | collective-permute-start | bytes 4718600 | tf_op jit(solution)/shard_map/ppermute | solution.py:20
  20.3 76.9 %collective-permute-start.1 = (bf16[128,1536]{1,0:T(8,128)(2,1)}, bf16[128,1536]{1,0:T(8,128)(2,1)}, u32[]{:S(2)}, u32[]{:S(2)}) collective-permute-start(bf16[128,1536]{1,0:T(8,128)(2,1)} %pad_maximum_fusion.32), channel_id=1, source_target_pairs={{0,2},{2,0},{4,6},{6,4},{8,10},{10,8},{12,14},{14,12},{1,3},{3,1},... | collective-permute-start | bytes 1179656 | tf_op jit(solution)/shard_map/ppermute | solution.py:20
  21.2 45.1 %collective-permute-start.17 = (bf16[128,512]{1,0:T(8,128)(2,1)}, bf16[128,512]{1,0:T(8,128)(2,1)}, u32[]{:S(2)}, u32[]{:S(2)}) collective-permute-start(bf16[128,512]{1,0:T(8,128)(2,1)} %broadcast_select_fusion.26), channel_id=1, source_target_pairs={{0,2},{2,0},{4,6},{6,4},{8,10},{10,8},{12,14},{14,12},{1,3},{3,1},... | collective-permute-start | bytes 393224 | tf_op jit(solution)/shard_map/ppermute | solution.py:20
  24.8 79.5 %collective-permute-start.31 = (bf16[128,2816]{1,0:T(8,128)(2,1)}, bf16[128,2816]{1,0:T(8,128)(2,1)}, u32[]{:S(2)}, u32[]{:S(2)}) collective-permute-start(bf16[128,2816]{1,0:T(8,128)(2,1)} %pad_maximum_fusion.24), channel_id=1, source_target_pairs={{0,2},{2,0},{4,6},{6,4},{8,10},{10,8},{12,14},{14,12},{1,3},{3,1},... | collective-permute-start | bytes 2162696 | tf_op jit(solution)/shard_map/ppermute | solution.py:20
  27.0 60.9 %collective-permute-start.42 = (bf16[128,1408]{1,0:T(8,128)(2,1)}, bf16[128,1408]{1,0:T(8,128)(2,1)}, u32[]{:S(2)}, u32[]{:S(2)}) collective-permute-start(bf16[128,1408]{1,0:T(8,128)(2,1)} %broadcast_select_fusion.17), channel_id=1, source_target_pairs={{0,2},{2,0},{4,6},{6,4},{8,10},{10,8},{12,14},{14,12},{1,3},{3,1},... | collective-permute-start | bytes 1081352 | tf_op jit(solution)/shard_map/ppermute | solution.py:20
  145.9 40.0 %collective-permute-start.55 = (bf16[384,2048]{1,0:T(8,128)(2,1)}, bf16[384,2048]{1,0:T(8,128)(2,1)}, u32[]{:S(2)}, u32[]{:S(2)}) collective-permute-start(bf16[384,2048]{1,0:T(8,128)(2,1)} %constant_dynamic-update-slice_fusion.128), channel_id=1, source_target_pairs={{0,2},{2,0},{4,6},{6,4},{8,10},{10,8},{12,14},{14,12},{1,3},{3,1},... | collective-permute-start | bytes 4718600 | tf_op jit(solution)/shard_map/ppermute | solution.py:20
  157.2 47.4 %collective-permute-start.36 = (bf16[128,2816]{1,0:T(8,128)(2,1)}, bf16[128,2816]{1,0:T(8,128)(2,1)}, u32[]{:S(2)}, u32[]{:S(2)}) collective-permute-start(bf16[128,2816]{1,0:T(8,128)(2,1)} %get-tuple-element.478), channel_id=1, source_target_pairs={{0,16},{16,0},{1,17},{17,1},{2,18},{18,2},{3,19},{19,3},{4,20},{20... | collective-permute-start | bytes 2162696 | tf_op jit(solution)/shard_map/ppermute | solution.py:20
  158.2 35.2 %collective-permute-start.3 = (bf16[256,1536]{1,0:T(8,128)(2,1)}, bf16[256,1536]{1,0:T(8,128)(2,1)}, u32[]{:S(2)}, u32[]{:S(2)}) collective-permute-start(bf16[256,1536]{1,0:T(8,128)(2,1)} %pad_maximum_fusion.19), channel_id=1, source_target_pairs={{0,8},{2,10},{4,12},{6,14},{8,0},{10,2},{12,4},{14,6},{1,9},{3,11}... | collective-permute-start | bytes 2359304 | tf_op jit(solution)/shard_map/ppermute | solution.py:20
  171.7 36.3 %collective-permute-start.45 = (bf16[128,1408]{1,0:T(8,128)(2,1)}, bf16[128,1408]{1,0:T(8,128)(2,1)}, u32[]{:S(2)}, u32[]{:S(2)}) collective-permute-start(bf16[128,1408]{1,0:T(8,128)(2,1)} %get-tuple-element.470), channel_id=1, source_target_pairs={{0,8},{2,10},{4,12},{6,14},{8,0},{10,2},{12,4},{14,6},{1,9},{3,11}... | collective-permute-start | bytes 1081352 | tf_op jit(solution)/shard_map/ppermute | solution.py:20
  201.9 208.6 %collective-permute-start.49 = (bf16[256,1408]{1,0:T(8,128)(2,1)}, bf16[256,1408]{1,0:T(8,128)(2,1)}, u32[]{:S(2)}, u32[]{:S(2)}) collective-permute-start(bf16[256,1408]{1,0:T(8,128)(2,1)} %pad_maximum_fusion.27), channel_id=1, source_target_pairs={{0,8},{2,10},{4,12},{6,14},{8,0},{10,2},{12,4},{14,6},{1,9},{3,11}... | collective-permute-start | bytes 2162696 | tf_op jit(solution)/shard_map/ppermute | solution.py:20
  204.6 83.9 %collective-permute-start.8 = (bf16[256,1536]{1,0:T(8,128)(2,1)S(1)}, bf16[256,1536]{1,0:T(8,128)(2,1)S(1)}, u32[]{:S(2)}, u32[]{:S(2)}) collective-permute-start(bf16[256,1536]{1,0:T(8,128)(2,1)S(1)} %copy-done.95), channel_id=1, source_target_pairs={{0,8},{2,10},{4,12},{6,14},{8,0},{10,2},{12,4},{14,6},{1,9},{3,11}... | collective-permute-start | bytes 2359304 | tf_op jit(solution)/shard_map/ppermute | solution.py:20
  204.8 52.1 %collective-permute-start.37 = (bf16[128,2816]{1,0:T(8,128)(2,1)}, bf16[128,2816]{1,0:T(8,128)(2,1)S(1)}, u32[]{:S(2)}, u32[]{:S(2)}) collective-permute-start(bf16[128,2816]{1,0:T(8,128)(2,1)} %collective-permute-done.36), channel_id=1, source_target_pairs={{0,4},{2,6},{4,0},{6,2},{8,12},{10,14},{12,8},{14,10},{1,5},{3,7},... | collective-permute-start | bytes 2162696 | tf_op jit(solution)/shard_map/ppermute | solution.py:20
  208.0 36.3 %collective-permute-start.4 = (bf16[128,1536]{1,0:T(8,128)(2,1)S(1)}, bf16[128,1536]{1,0:T(8,128)(2,1)S(1)}, u32[]{:S(2)}, u32[]{:S(2)}) collective-permute-start(bf16[128,1536]{1,0:T(8,128)(2,1)S(1)} %get-tuple-element.484), channel_id=1, source_target_pairs={{0,8},{2,10},{4,12},{6,14},{8,0},{10,2},{12,4},{14,6},{1,9},{3,11}... | collective-permute-start | bytes 1179656 | tf_op jit(solution)/shard_map/ppermute | solution.py:20
  256.9 132.1 %collective-permute-start.33 = (bf16[256,2816]{1,0:T(8,128)(2,1)}, bf16[256,2816]{1,0:T(8,128)(2,1)}, u32[]{:S(2)}, u32[]{:S(2)}) collective-permute-start(bf16[256,2816]{1,0:T(8,128)(2,1)} %pad_maximum_fusion.11), channel_id=1, source_target_pairs={{0,8},{2,10},{4,12},{6,14},{8,0},{10,2},{12,4},{14,6},{1,9},{3,11}... | collective-permute-start | bytes 4325384 | tf_op jit(solution)/shard_map/ppermute | solution.py:20
  269.0 215.2 %collective-permute-start.38 = (bf16[256,2816]{1,0:T(8,128)(2,1)}, bf16[256,2816]{1,0:T(8,128)(2,1)}, u32[]{:S(2)}, u32[]{:S(2)}) collective-permute-start(bf16[256,2816]{1,0:T(8,128)(2,1)} %pad_maximum_fusion.13), channel_id=1, source_target_pairs={{0,8},{2,10},{4,12},{6,14},{8,0},{10,2},{12,4},{14,6},{1,9},{3,11}... | collective-permute-start | bytes 4325384 | tf_op jit(solution)/shard_map/ppermute | solution.py:20
  394.7 50.0 %collective-permute-start.52 = (bf16[256,1408]{1,0:T(8,128)(2,1)S(1)}, bf16[256,1408]{1,0:T(8,128)(2,1)S(1)}, u32[]{:S(2)}, u32[]{:S(2)}) collective-permute-start(bf16[256,1408]{1,0:T(8,128)(2,1)S(1)} %copy-done.96), channel_id=1, source_target_pairs={{0,4},{2,6},{4,0},{6,2},{8,12},{10,14},{12,8},{14,10},{1,5},{3,7},... | collective-permute-start | bytes 2162696 | tf_op jit(solution)/shard_map/ppermute | solution.py:20
  405.7 38.0 %collective-permute-start.28 = (bf16[384,2048]{1,0:T(8,128)(2,1)S(1)}, bf16[384,2048]{1,0:T(8,128)(2,1)S(1)}, u32[]{:S(2)}, u32[]{:S(2)}) collective-permute-start(bf16[384,2048]{1,0:T(8,128)(2,1)S(1)} %select_convert_fusion.3), channel_id=1, source_target_pairs={{0,2},{2,0},{4,6},{6,4},{8,10},{10,8},{12,14},{14,12},{1,3},{3,1},... | collective-permute-start | bytes 4718600 | tf_op jit(solution)/shard_map/ppermute | solution.py:20
  425.7 36.6 %collective-permute-start.35 = (bf16[256,2816]{1,0:T(8,128)(2,1)S(1)}, bf16[256,2816]{1,0:T(8,128)(2,1)S(1)}, u32[]{:S(2)}, u32[]{:S(2)}) collective-permute-start(bf16[256,2816]{1,0:T(8,128)(2,1)S(1)} %pad_maximum_fusion.12), channel_id=1, source_target_pairs={{0,4},{2,6},{4,0},{6,2},{8,12},{10,14},{12,8},{14,10},{1,5},{3,7},... | collective-permute-start | bytes 4325384 | tf_op jit(solution)/shard_map/ppermute | solution.py:20
  444.5 36.1 %collective-permute-start.29 = (bf16[384,2048]{1,0:T(8,128)(2,1)S(1)}, bf16[384,2048]{1,0:T(8,128)(2,1)S(1)}, u32[]{:S(2)}, u32[]{:S(2)}) collective-permute-start(bf16[384,2048]{1,0:T(8,128)(2,1)S(1)} %add_convert_fusion.4), channel_id=1, source_target_pairs={{0,1},{1,0},{2,3},{3,2},{4,5},{5,4},{6,7},{7,6},{8,9},{9,8},{10,11... | collective-permute-start | bytes 4718600 | tf_op jit(solution)/shard_map/ppermute | solution.py:20
  565.8 199.8 %collective-permute-start.56 = (bf16[384,2048]{1,0:T(8,128)(2,1)S(1)}, bf16[384,2048]{1,0:T(8,128)(2,1)S(1)}, u32[]{:S(2)}, u32[]{:S(2)}) collective-permute-start(bf16[384,2048]{1,0:T(8,128)(2,1)S(1)} %select_convert_fusion.1), channel_id=1, source_target_pairs={{0,2},{2,0},{4,6},{6,4},{8,10},{10,8},{12,14},{14,12},{1,3},{3,1},... | collective-permute-start | bytes 4718600 | tf_op jit(solution)/shard_map/ppermute | solution.py:20
  569.7 201.0 %collective-permute-start.53 = (bf16[384,2048]{1,0:T(8,128)(2,1)}, bf16[384,2048]{1,0:T(8,128)(2,1)}, u32[]{:S(2)}, u32[]{:S(2)}) collective-permute-start(bf16[384,2048]{1,0:T(8,128)(2,1)} %select_convert_fusion.2), channel_id=1, source_target_pairs={{0,2},{2,0},{4,6},{6,4},{8,10},{10,8},{12,14},{14,12},{1,3},{3,1},... | collective-permute-start | bytes 4718600 | tf_op jit(solution)/shard_map/ppermute | solution.py:20
  569.8 95.2 %collective-permute-start.92 = (bf16[256,2816]{1,0:T(8,128)(2,1)S(1)}, bf16[256,2816]{1,0:T(8,128)(2,1)S(1)}, u32[]{:S(2)}, u32[]{:S(2)}) collective-permute-start(bf16[256,2816]{1,0:T(8,128)(2,1)S(1)} %slice.809), channel_id=1, source_target_pairs={{0,8},{2,10},{4,12},{6,14},{8,0},{10,2},{12,4},{14,6},{1,9},{3,11}... | collective-permute-start | bytes 4325384 | tf_op jit(solution)/shard_map/ppermute | solution.py:20
  599.0 70.0 %collective-permute-start.90 = (bf16[256,2816]{1,0:T(8,128)(2,1)S(1)}, bf16[256,2816]{1,0:T(8,128)(2,1)}, u32[]{:S(2)}, u32[]{:S(2)}) collective-permute-start(bf16[256,2816]{1,0:T(8,128)(2,1)S(1)} %slice.803), channel_id=1, source_target_pairs={{0,8},{2,10},{4,12},{6,14},{8,0},{10,2},{12,4},{14,6},{1,9},{3,11}... | collective-permute-start | bytes 4325384 | tf_op jit(solution)/shard_map/ppermute | solution.py:20
  620.5 42.9 %collective-permute-start.109 = (bf16[128,1408]{1,0:T(8,128)(2,1)S(1)}, bf16[128,1408]{1,0:T(8,128)(2,1)S(1)}, u32[]{:S(2)}, u32[]{:S(2)}) collective-permute-start(bf16[128,1408]{1,0:T(8,128)(2,1)S(1)} %slice.1229), channel_id=1, source_target_pairs={{0,8},{2,10},{4,12},{6,14},{8,0},{10,2},{12,4},{14,6},{1,9},{3,11}... | collective-permute-start | bytes 1081352 | tf_op jit(solution)/shard_map/ppermute | solution.py:20
  666.1 66.7 %collective-permute-start.95 = (bf16[256,2816]{1,0:T(8,128)(2,1)S(1)}, bf16[256,2816]{1,0:T(8,128)(2,1)S(1)}, u32[]{:S(2)}, u32[]{:S(2)}) collective-permute-start(bf16[256,2816]{1,0:T(8,128)(2,1)S(1)} %slice.815), channel_id=1, source_target_pairs={{0,4},{2,6},{4,0},{6,2},{8,12},{10,14},{12,8},{14,10},{1,5},{3,7},... | collective-permute-start | bytes 4325384 | tf_op jit(solution)/shard_map/ppermute | solution.py:20
  669.0 63.8 %collective-permute-start.102 = (bf16[128,1408]{1,0:T(8,128)(2,1)S(1)}, bf16[128,1408]{1,0:T(8,128)(2,1)S(1)}, u32[]{:S(2)}, u32[]{:S(2)}) collective-permute-start(bf16[128,1408]{1,0:T(8,128)(2,1)S(1)} %slice.1232), channel_id=1, source_target_pairs={{0,4},{2,6},{4,0},{6,2},{8,12},{10,14},{12,8},{14,10},{1,5},{3,7},... | collective-permute-start | bytes 1081352 | tf_op jit(solution)/shard_map/ppermute | solution.py:20
  698.1 40.8 %collective-permute-start.107 = (bf16[128,1408]{1,0:T(8,128)(2,1)S(1)}, bf16[128,1408]{1,0:T(8,128)(2,1)S(1)}, u32[]{:S(2)}, u32[]{:S(2)}) collective-permute-start(bf16[128,1408]{1,0:T(8,128)(2,1)S(1)} %slice.1230), channel_id=1, source_target_pairs={{0,8},{2,10},{4,12},{6,14},{8,0},{10,2},{12,4},{14,6},{1,9},{3,11}... | collective-permute-start | bytes 1081352 | tf_op jit(solution)/shard_map/ppermute | solution.py:20
  738.8 35.6 %collective-permute-start.93 = (bf16[128,2816]{1,0:T(8,128)(2,1)S(1)}, bf16[128,2816]{1,0:T(8,128)(2,1)S(1)}, u32[]{:S(2)}, u32[]{:S(2)}) collective-permute-start(bf16[128,2816]{1,0:T(8,128)(2,1)S(1)} %slice.1223), channel_id=1, source_target_pairs={{0,4},{2,6},{4,0},{6,2},{8,12},{10,14},{12,8},{14,10},{1,5},{3,7},... | collective-permute-start | bytes 2162696 | tf_op jit(solution)/shard_map/ppermute | solution.py:20
  756.2 34.9 %collective-permute-start.91 = (bf16[128,2816]{1,0:T(8,128)(2,1)}, bf16[128,2816]{1,0:T(8,128)(2,1)}, u32[]{:S(2)}, u32[]{:S(2)}) collective-permute-start(bf16[128,2816]{1,0:T(8,128)(2,1)} %slice.1224), channel_id=1, source_target_pairs={{0,4},{2,6},{4,0},{6,2},{8,12},{10,14},{12,8},{14,10},{1,5},{3,7},... | collective-permute-start | bytes 2162696 | tf_op jit(solution)/shard_map/ppermute | solution.py:20
  774.4 75.6 %collective-permute-start.57 = (bf16[384,2048]{1,0:T(8,128)(2,1)}, bf16[384,2048]{1,0:T(8,128)(2,1)}, u32[]{:S(2)}, u32[]{:S(2)}) collective-permute-start(bf16[384,2048]{1,0:T(8,128)(2,1)} %add_convert_fusion.1), channel_id=1, source_target_pairs={{0,1},{1,0},{2,3},{3,2},{4,5},{5,4},{6,7},{7,6},{8,9},{9,8},{10,11... | collective-permute-start | bytes 4718600 | tf_op jit(solution)/shard_map/ppermute | solution.py:20
  782.8 42.2 %collective-permute-start.94 = (bf16[128,2816]{1,0:T(8,128)(2,1)}, bf16[128,2816]{1,0:T(8,128)(2,1)}, u32[]{:S(2)}, u32[]{:S(2)}) collective-permute-start(bf16[128,2816]{1,0:T(8,128)(2,1)} %fusion.104), channel_id=1, source_target_pairs={{0,16},{16,0},{1,17},{17,1},{2,18},{18,2},{3,19},{19,3},{4,20},{20... | collective-permute-start | bytes 2162696 | tf_op jit(solution)/shard_map/ppermute | solution.py:20
  783.8 63.0 %collective-permute-start.99 = (bf16[128,2816]{1,0:T(8,128)(2,1)}, bf16[128,2816]{1,0:T(8,128)(2,1)}, u32[]{:S(2)}, u32[]{:S(2)}) collective-permute-start(bf16[128,2816]{1,0:T(8,128)(2,1)} %fusion.102), channel_id=1, source_target_pairs={{0,16},{16,0},{1,17},{17,1},{2,18},{18,2},{3,19},{19,3},{4,20},{20... | collective-permute-start | bytes 2162696 | tf_op jit(solution)/shard_map/ppermute | solution.py:20
  872.6 60.2 %collective-permute-start.63 = (bf16[256,512]{1,0:T(8,128)(2,1)}, bf16[256,512]{1,0:T(8,128)(2,1)}, u32[]{:S(2)}, u32[]{:S(2)}) collective-permute-start(bf16[256,512]{1,0:T(8,128)(2,1)} %convolution_convert_fusion.16), channel_id=1, source_target_pairs={{12,0},{14,2},{13,1},{15,3},{28,16},{30,18},{29,17},{31,19}} | collective-permute-start | bytes 786440 | tf_op jit(solution)/shard_map/ppermute | solution.py:180
  873.9 60.6 %collective-permute-start.61 = (bf16[256,512]{1,0:T(8,128)(2,1)}, bf16[256,512]{1,0:T(8,128)(2,1)}, u32[]{:S(2)}, u32[]{:S(2)}) collective-permute-start(bf16[256,512]{1,0:T(8,128)(2,1)} %convolution_convert_fusion.16), channel_id=1, source_target_pairs={{8,0},{10,2},{12,4},{14,6},{9,1},{11,3},{13,5},{15,7},{24,16},{26,... | collective-permute-start | bytes 786440 | tf_op jit(solution)/shard_map/ppermute | solution.py:180
  875.2 59.6 %collective-permute-start.59 = (bf16[256,512]{1,0:T(8,128)(2,1)}, bf16[256,512]{1,0:T(8,128)(2,1)}, u32[]{:S(2)}, u32[]{:S(2)}) collective-permute-start(bf16[256,512]{1,0:T(8,128)(2,1)} %convolution_convert_fusion.16), channel_id=1, source_target_pairs={{4,0},{6,2},{8,4},{10,6},{12,8},{14,10},{5,1},{7,3},{9,5},{11,7},{... | collective-permute-start | bytes 786440 | tf_op jit(solution)/shard_map/ppermute | solution.py:180
  924.6 173.8 %collective-permute-start.81 = (bf16[256,512]{1,0:T(8,128)(2,1)}, bf16[256,512]{1,0:T(8,128)(2,1)}, u32[]{:S(2)}, u32[]{:S(2)}) collective-permute-start(bf16[256,512]{1,0:T(8,128)(2,1)} %slice.785), channel_id=1, source_target_pairs={{0,8},{2,10},{4,12},{6,14},{8,0},{10,2},{12,4},{14,6},{1,9},{3,11}... | collective-permute-start | bytes 786440 | tf_op jit(solution)/shard_map/ppermute | solution.py:20
  928.8 175.8 %collective-permute-start.79 = (bf16[256,512]{1,0:T(8,128)(2,1)}, bf16[256,512]{1,0:T(8,128)(2,1)}, u32[]{:S(2)}, u32[]{:S(2)}) collective-permute-start(bf16[256,512]{1,0:T(8,128)(2,1)} %slice.779), channel_id=1, source_target_pairs={{0,8},{2,10},{4,12},{6,14},{8,0},{10,2},{12,4},{14,6},{1,9},{3,11}... | collective-permute-start | bytes 786440 | tf_op jit(solution)/shard_map/ppermute | solution.py:20
  932.8 174.5 %collective-permute-start.86 = (bf16[256,512]{1,0:T(8,128)(2,1)}, bf16[256,512]{1,0:T(8,128)(2,1)}, u32[]{:S(2)}, u32[]{:S(2)}) collective-permute-start(bf16[256,512]{1,0:T(8,128)(2,1)} %slice.797), channel_id=1, source_target_pairs={{0,4},{2,6},{4,0},{6,2},{8,12},{10,14},{12,8},{14,10},{1,5},{3,7},... | collective-permute-start | bytes 786440 | tf_op jit(solution)/shard_map/ppermute | solution.py:20
  934.5 175.9 %collective-permute-start.84 = (bf16[256,512]{1,0:T(8,128)(2,1)}, bf16[256,512]{1,0:T(8,128)(2,1)}, u32[]{:S(2)}, u32[]{:S(2)}) collective-permute-start(bf16[256,512]{1,0:T(8,128)(2,1)} %slice.791), channel_id=1, source_target_pairs={{0,4},{2,6},{4,0},{6,2},{8,12},{10,14},{12,8},{14,10},{1,5},{3,7},... | collective-permute-start | bytes 786440 | tf_op jit(solution)/shard_map/ppermute | solution.py:20
  1125.8 140.2 %collective-permute-start.64 = (bf16[384,2048]{1,0:T(8,128)(2,1)}, bf16[384,2048]{1,0:T(8,128)(2,1)}, u32[]{:S(2)}, u32[]{:S(2)}) collective-permute-start(bf16[384,2048]{1,0:T(8,128)(2,1)} %select_convert_fusion), channel_id=1, source_target_pairs={{0,2},{2,0},{4,6},{6,4},{8,10},{10,8},{12,14},{14,12},{1,3},{3,1},... | collective-permute-start | bytes 4718600 | tf_op jit(solution)/shard_map/ppermute | solution.py:20
  1133.4 44.2 %collective-permute-start.89 = (bf16[128,512]{1,0:T(8,128)(2,1)S(1)}, bf16[128,512]{1,0:T(8,128)(2,1)}, u32[]{:S(2)}, u32[]{:S(2)}) collective-permute-start(bf16[128,512]{1,0:T(8,128)(2,1)S(1)} %select_convert_fusion.7), channel_id=1, source_target_pairs={{0,2},{2,0},{4,6},{6,4},{8,10},{10,8},{12,14},{14,12},{1,3},{3,1},... | collective-permute-start | bytes 393224 | tf_op jit(solution)/shard_map/ppermute | solution.py:20
  1149.0 114.0 %collective-permute-start.69 = (bf16[128,1536]{1,0:T(8,128)(2,1)}, bf16[128,1536]{1,0:T(8,128)(2,1)S(1)}, u32[]{:S(2)}, u32[]{:S(2)}) collective-permute-start(bf16[128,1536]{1,0:T(8,128)(2,1)} %slice.1228), channel_id=1, source_target_pairs={{0,4},{2,6},{4,0},{6,2},{8,12},{10,14},{12,8},{14,10},{1,5},{3,7},... | collective-permute-start | bytes 1179656 | tf_op jit(solution)/shard_map/ppermute | solution.py:20
  1174.9 89.4 %collective-permute-start.74 = (bf16[128,1536]{1,0:T(8,128)(2,1)}, bf16[128,1536]{1,0:T(8,128)(2,1)}, u32[]{:S(2)}, u32[]{:S(2)}) collective-permute-start(bf16[128,1536]{1,0:T(8,128)(2,1)} %slice.1226), channel_id=1, source_target_pairs={{0,8},{2,10},{4,12},{6,14},{8,0},{10,2},{12,4},{14,6},{1,9},{3,11}... | collective-permute-start | bytes 1179656 | tf_op jit(solution)/shard_map/ppermute | solution.py:20
  1176.0 88.4 %collective-permute-start.72 = (bf16[128,1536]{1,0:T(8,128)(2,1)}, bf16[128,1536]{1,0:T(8,128)(2,1)}, u32[]{:S(2)}, u32[]{:S(2)}) collective-permute-start(bf16[128,1536]{1,0:T(8,128)(2,1)} %fusion.147), channel_id=1, source_target_pairs={{0,16},{16,0},{1,17},{17,1},{2,18},{18,2},{3,19},{19,3},{4,20},{20... | collective-permute-start | bytes 1179656 | tf_op jit(solution)/shard_map/ppermute | solution.py:20
  1177.6 86.8 %collective-permute-start.77 = (bf16[128,1536]{1,0:T(8,128)(2,1)}, bf16[128,1536]{1,0:T(8,128)(2,1)}, u32[]{:S(2)}, u32[]{:S(2)}) collective-permute-start(bf16[128,1536]{1,0:T(8,128)(2,1)} %fusion.145), channel_id=1, source_target_pairs={{0,16},{16,0},{1,17},{17,1},{2,18},{18,2},{3,19},{19,3},{4,20},{20... | collective-permute-start | bytes 1179656 | tf_op jit(solution)/shard_map/ppermute | solution.py:20
  1263.0 71.9 %collective-permute-start.54 = (bf16[384,2048]{1,0:T(8,128)(2,1)}, bf16[384,2048]{1,0:T(8,128)(2,1)S(1)}, u32[]{:S(2)}, u32[]{:S(2)}) collective-permute-start(bf16[384,2048]{1,0:T(8,128)(2,1)} %add_convert_fusion.3), channel_id=1, source_target_pairs={{0,1},{1,0},{2,3},{3,2},{4,5},{5,4},{6,7},{7,6},{8,9},{9,8},{10,11... | collective-permute-start | bytes 4718600 | tf_op jit(solution)/shard_map/ppermute | solution.py:20
  1270.1 63.0 %collective-permute-start.65 = (bf16[384,2048]{1,0:T(8,128)(2,1)S(1)}, bf16[384,2048]{1,0:T(8,128)(2,1)S(1)}, u32[]{:S(2)}, u32[]{:S(2)}) collective-permute-start(bf16[384,2048]{1,0:T(8,128)(2,1)S(1)} %add_convert_fusion), channel_id=1, source_target_pairs={{0,1},{1,0},{2,3},{3,2},{4,5},{5,4},{6,7},{7,6},{8,9},{9,8},{10,11... | collective-permute-start | bytes 4718600 | tf_op jit(solution)/shard_map/ppermute | solution.py:20
  (227 other events, 4689.1 us)
Sparse Core Ops, SparseCore 0:
  1125.9 131.4 all-reduce.8

commit v2 on v1

v2 whole, which is shorter than its diff:
```python
import functools

import jax
import jax.numpy as jnp
from jax import lax
from jax.experimental import pallas as pl
from jax.experimental.pallas import tpu as pltpu
from jax.sharding import PartitionSpec as P

KD = 256
VD = 512
BLOCK_LEN = 64

epsilon = 1e-06
normalizer = 16.0
MATMUL_PRECISION = lax.Precision.HIGHEST
BF16 = jnp.bfloat16
F32 = jnp.float32
CORE = 1


def swap(x, axis, bit=1):
    count = lax.axis_size(axis)
    return lax.ppermute(x, axis, [(i, i ^ bit) for i in range(count)])


def matmul(left, right):
    return jnp.dot(left, right, preferred_element_type=F32)


def inner(left, right):
    return lax.dot_general(left, right, (((0,), (0,)), ((), ())), preferred_element_type=F32)


def times_back(grad, weight):
    return lax.dot_general(grad, weight, (((1,), (1,)), ((), ())), preferred_element_type=F32)


def rms_norm(x, gain):
    return x * lax.rsqrt(jnp.mean(x * x, axis=-1, keepdims=True) + epsilon) * gain


def head_norm(mixed_output, outgate, gain):
    return rms_norm(mixed_output, gain) * jax.nn.silu(outgate)


def swiglu(gate, upward):
    return jax.nn.silu(gate) * upward


def dot(a, b, contract, passes=1):
    dims = ((contract[0],), (contract[1],)), ((), ())

    def once(x, y):
        return lax.dot_general(x, y, dims, preferred_element_type=F32)

    high_a, high_b = a.astype(BF16), b.astype(BF16)
    total = once(high_a, high_b)
    if passes > 1:
        low_a = (a - high_a.astype(F32)).astype(BF16)
        low_b = (b - high_b.astype(F32)).astype(BF16)
        total = total + (once(high_a, low_b) + once(low_a, high_b))
    return total


def triangle(size):
    rows = lax.broadcasted_iota(jnp.int32, (size, size), 0)
    columns = lax.broadcasted_iota(jnp.int32, (size, size), 1)
    return rows >= columns


def block_terms(query, key, decay):
    size = decay.shape[0]
    ones = jnp.where(triangle(size), 1.0, 0.0)
    running = lax.dot_general(
        ones, decay, (((1,), (0,)), ((), ())), precision=MATMUL_PRECISION, preferred_element_type=F32
    )
    final = running[size - 1 : size]
    rise, fall, rest = jnp.exp(running), jnp.exp(-running), jnp.exp(final - running)
    return query * (KD**-0.5) * rise, key * fall, key * rest, rise, fall, rest, final


PASSES = 1


def forward_kernel(q_ref, k_ref, v_ref, d_ref, out_ref, lifted_ref, states_ref, end_ref, edge_ref, prefix_ref, state, before):
    @pl.when(pl.program_id(0) == 0)
    def _():
        state[...] = jnp.zeros_like(state)
        before[...] = jnp.zeros_like(before)

    lifted, lowered, carried, _, _, _, final = block_terms(q_ref[...], k_ref[...], d_ref[...])
    value = v_ref[...]
    scores = dot(lifted, lowered, (1, 1), PASSES)
    scores = jnp.where(triangle(scores.shape[0]), scores, 0.0)
    held = state[...]
    out_ref[...] = dot(scores, value, (1, 0), PASSES) + dot(lifted, held, (1, 1), PASSES)
    reach = jnp.exp(before[0:1])
    lifted_ref[...] = lifted * reach
    prefix_ref[...] = reach[None]
    states_ref[...] = held[None]
    new = held * jnp.exp(final) + dot(value, carried, (0, 0), PASSES)
    state[...] = new
    before[0:1] = before[0:1] + final
    end_ref[...] = new
    edge_ref[...] = jnp.exp(before[0:1])


def backward_kernel(q_ref, k_ref, v_ref, d_ref, grad_ref, states_ref, prefix_ref, in_ref, out_ref, mixer_ref, decay_ref, state):
    @pl.when(pl.program_id(0) == 0)
    def _():
        state[...] = out_ref[...]

    lifted, lowered, carried, rise, fall, rest, final = block_terms(q_ref[...], k_ref[...], d_ref[...])
    value, grad = v_ref[...], grad_ref[...]
    later = state[...]
    held = states_ref[0] + in_ref[...] * prefix_ref[0]
    lower = triangle(value.shape[0])
    scores = jnp.where(lower, dot(lifted, lowered, (1, 1), PASSES), 0.0)
    grad_scores = jnp.where(lower, dot(grad, value, (1, 1), PASSES), 0.0)
    grad_value = dot(scores, grad, (0, 0), PASSES) + dot(carried, later, (1, 1), PASSES)
    grad_lifted = dot(grad, held, (1, 0), PASSES) + dot(grad_scores, lowered, (1, 0), PASSES)
    grad_lowered = dot(grad_scores, lifted, (0, 0), PASSES)
    grad_carried = dot(value, later, (1, 0), PASSES)
    mixer_ref[:, :KD] = (grad_lifted * rise * (KD**-0.5)).astype(BF16)
    mixer_ref[:, KD : 2 * KD] = (grad_lowered * fall + grad_carried * rest).astype(BF16)
    mixer_ref[:, 2 * KD :] = grad_value.astype(BF16)
    through = carried * grad_carried
    change = lifted * grad_lifted - lowered * grad_lowered - through
    fade = jnp.exp(final)
    last = jnp.sum(through, axis=0, keepdims=True) + fade * jnp.sum(held * later, axis=0, keepdims=True)
    ones = jnp.where(lower, 1.0, 0.0)
    decay_ref[...] = last + lax.dot_general(
        ones, change, (((0,), (0,)), ((), ())), precision=MATMUL_PRECISION, preferred_element_type=F32
    )
    state[...] = later * fade + dot(grad, lifted, (0, 0), PASSES)


def mixer_forward(projected, decay):
    length = decay.shape[0]
    count = length // BLOCK_LEN
    row = lambda i: (i, 0)
    fixed = lambda i: (0, 0)
    return pl.pallas_call(
        forward_kernel,
        grid=(count,),
        in_specs=[
            pl.BlockSpec((BLOCK_LEN, KD), lambda i: (i, 0)),
            pl.BlockSpec((BLOCK_LEN, KD), lambda i: (i, 1)),
            pl.BlockSpec((BLOCK_LEN, VD), lambda i: (i, 1)),
            pl.BlockSpec((BLOCK_LEN, KD), row),
        ],
        out_specs=[
            pl.BlockSpec((BLOCK_LEN, VD), row),
            pl.BlockSpec((BLOCK_LEN, KD), row),
            pl.BlockSpec((1, VD, KD), lambda i: (i, 0, 0)),
            pl.BlockSpec((VD, KD), fixed),
            pl.BlockSpec((1, KD), fixed),
            pl.BlockSpec((1, 1, KD), lambda i: (i, 0, 0)),
        ],
        out_shape=[
            jax.ShapeDtypeStruct((length, VD), F32),
            jax.ShapeDtypeStruct((length, KD), F32),
            jax.ShapeDtypeStruct((count, VD, KD), F32),
            jax.ShapeDtypeStruct((VD, KD), F32),
            jax.ShapeDtypeStruct((1, KD), F32),
            jax.ShapeDtypeStruct((count, 1, KD), F32),
        ],
        scratch_shapes=[pltpu.VMEM((VD, KD), F32), pltpu.VMEM((8, KD), F32)],
        compiler_params=pltpu.CompilerParams(
            dimension_semantics=("arbitrary",), vmem_limit_bytes=32 * 2**20
        ),
        name="mixer_forward",
    )(projected, projected, projected, decay)


def mixer_backward(projected, decay, grad, states, prefix, earlier, later):
    length = decay.shape[0]
    count = length // BLOCK_LEN
    row = lambda i: (count - 1 - i, 0)
    fixed = lambda i: (0, 0)
    return pl.pallas_call(
        backward_kernel,
        grid=(count,),
        in_specs=[
            pl.BlockSpec((BLOCK_LEN, KD), lambda i: (count - 1 - i, 0)),
            pl.BlockSpec((BLOCK_LEN, KD), lambda i: (count - 1 - i, 1)),
            pl.BlockSpec((BLOCK_LEN, VD), lambda i: (count - 1 - i, 1)),
            pl.BlockSpec((BLOCK_LEN, KD), row),
            pl.BlockSpec((BLOCK_LEN, VD), row),
            pl.BlockSpec((1, VD, KD), lambda i: (count - 1 - i, 0, 0)),
            pl.BlockSpec((1, 1, KD), lambda i: (count - 1 - i, 0, 0)),
            pl.BlockSpec((VD, KD), fixed),
            pl.BlockSpec((VD, KD), fixed),
        ],
        out_specs=[
            pl.BlockSpec((BLOCK_LEN, 2 * KD + VD), row),
            pl.BlockSpec((BLOCK_LEN, KD), row),
        ],
        out_shape=[
            jax.ShapeDtypeStruct((length, 2 * KD + VD), BF16),
            jax.ShapeDtypeStruct((length, KD), F32),
        ],
        scratch_shapes=[pltpu.VMEM((VD, KD), F32)],
        compiler_params=pltpu.CompilerParams(
            dimension_semantics=("arbitrary",), vmem_limit_bytes=32 * 2**20
        ),
        name="mixer_backward",
    )(projected, projected, projected, decay, grad, states, prefix, earlier, later)


def chip_bits():
    bits, bit = [], 2
    while bit < lax.axis_size("seq"):
        bits.append(bit)
        bit *= 2
    return bits


def tie(arrays, *first):
    return lax.optimization_barrier((arrays, first))[0]


def hop(x, step):
    bits = chip_bits()
    there = (bits[step], bits[-1 - step])
    count = lax.axis_size("seq")
    return lax.ppermute(x, "seq", [(i, i ^ there[i % 2]) for i in range(count)])


def place_in(core_order):
    count = len(chip_bits())
    return sum(((core_order >> k) & 1) << (count - 1 - k) for k in range(count))


def same_order(parts, core):
    return [
        x if place_in(i) == i else jnp.where(core == 0, x, parts[place_in(i)])
        for i, x in enumerate(parts)
    ]


class Spread:
    def __init__(self, rows):
        self.parts = [rows]
        self.steps = 0

    def load(self):
        return self.parts[0] if len(self.parts) == 1 else jnp.concatenate(self.parts, 0)

    def take(self, got):
        rows = self.parts[0].shape[0]
        count = len(self.parts)
        self.parts = self.parts + [got[i * rows : (i + 1) * rows] for i in range(count)]
        self.steps += 1


class Collect:
    def __init__(self, rows):
        self.rows = rows
        self.steps = 0

    def load(self):
        return self.rows[self.rows.shape[0] // 2 :].astype(BF16)

    def take(self, got):
        self.rows = self.rows[: self.rows.shape[0] // 2].astype(F32) + got.astype(F32)
        self.steps += 1


class Plane:
    def __init__(self, plan, reverse=False):
        names = sorted({name for slot in plan for name, _ in slot}, key=str(plan).index)
        steps = len(chip_bits())
        self.plan = plan if steps == 2 else [[(n, i)] for n in names for i in range(steps)]
        self.phases = {}
        self.reverse = reverse
        self.done = []

    def slot(self, *first):
        now = self.plan[len(self.done)]
        loads = [self.phases[name].load() for name, _ in now]
        if len(self.done) >= 2:
            first = first + (self.done[-2],)
        if first:
            loads = tie(loads, *first)
        landed = []
        for (name, i), x in zip(now, loads):
            got = hop(x, len(chip_bits()) - 1 - i if self.reverse else i)
            self.phases[name].take(got)
            landed.append(got)
        self.done.append(landed)

    def until(self, *names):
        while any(self.phases[name].steps < len(chip_bits()) for name in names):
            self.slot()


def order():
    chip, dp = lax.axis_index("seq") // 2, lax.axis_index("dp")
    near = [0]
    for bit in chip_bits():
        near = near + [place ^ (bit // 2) for place in near]
    chips = len(near)
    return [(dp ^ away) * chips + (chip ^ place) for away in range(2) for place in near]


def reorder_kernel(count, index_ref, *refs):
    half = len(refs) // 2
    for source, target in zip(refs[:half], refs[half:]):
        width = source.shape[1] // count
        for i in range(count):
            start = pl.multiple_of(index_ref[i] * width, width)
            target[:, i * width : (i + 1) * width] = source[:, pl.ds(start, width)]


def reorder(index, *arrays):
    count = index.shape[0]
    rows, columns = arrays[0].shape
    if (columns // count) % 128:
        moved = [
            jnp.take(x.reshape(rows, count, -1), index, axis=1).reshape(rows, columns)
            for x in arrays
        ]
        return moved
    step = rows // 3 if rows % 48 == 0 else rows
    spec = pl.BlockSpec((step, columns), lambda i, _: (i, 0))
    return pl.pallas_call(
        functools.partial(reorder_kernel, count),
        grid_spec=pltpu.PrefetchScalarGridSpec(
            num_scalar_prefetch=1,
            grid=(rows // step,),
            in_specs=[spec] * len(arrays),
            out_specs=[spec] * len(arrays),
        ),
        out_shape=[jax.ShapeDtypeStruct(x.shape, x.dtype) for x in arrays],
        compiler_params=pltpu.CompilerParams(
            dimension_semantics=("arbitrary",), vmem_limit_bytes=32 * 2**20
        ),
        name="reorder",
    )(index, *arrays)


def core_order(x, core):
    count = 2 * 2 ** len(chip_bits())
    parts = jnp.split(x, count, 1)
    half = count // 2
    return jnp.concatenate(same_order(parts[:half], core) + same_order(parts[half:], core), 1)


def halves(pairs):
    half = pairs[0][0].shape[1] // 2

    def part(i):
        grads = [inner(left[:, i * half : (i + 1) * half], right) for left, right in pairs]
        return jnp.concatenate([grad.astype(BF16) for grad in grads], 1)

    return Collect(part(1)), Collect(part(0))


def both(x, core):
    other = swap(x, "seq", CORE)
    return jnp.concatenate([jnp.where(core == 0, x, other), jnp.where(core == 0, other, x)], 0)


def core_sum(part, core):
    rows = part.shape[0] // 2
    mine = jnp.where(core == 0, part[:rows], part[rows:])
    theirs = jnp.where(core == 0, part[rows:], part[:rows])
    mine = mine + swap(theirs.astype(BF16), "seq", CORE).astype(F32)
    return mine.astype(BF16)


def add_up(part, core):
    mine = core_sum(part, core)
    return mine.astype(F32) + swap(mine, "head").astype(F32)


def incoming(edge, state, reverse=False):
    chips = lax.axis_size("seq") // 2
    rows = state.shape[0]
    high = edge.astype(BF16)
    low = (edge - high.astype(F32)).astype(BF16)
    edges = jnp.pad(jnp.concatenate([high, low], 0), ((0, 14), (0, 0)))
    packed = jnp.concatenate([state.astype(BF16), edges], 0)

    def move(by):
        by = -by if reverse else by
        pairs = []
        for i in range(chips):
            if 0 <= i + by < chips:
                for c in range(2):
                    pairs.append((2 * i + c, 2 * (i + by) + c))
        return lax.ppermute(packed, "seq", pairs).astype(F32)

    total, faded = jnp.zeros_like(state), None
    for by in range(1, chips):
        there = move(by)
        gone = there[rows : rows + 1] + there[rows + 1 : rows + 2]
        if by == 1:
            total, faded = there[:rows], gone
        else:
            total, faded = total + faded * there[:rows], faded * gone
    return total


def body(
    tokens,
    mix_gain,
    w_query,
    w_key,
    w_value,
    w_outgate,
    w_lowrank,
    w_rate,
    rate_bias,
    head_gain,
    w_output,
    mlp_gain,
    w_gate,
    w_up,
    w_down,
    cotangent,
):
    core = lax.axis_index("seq") % 2
    blocks = order()
    wide = tokens.shape[1] // (2 * len(blocks))
    place_of = jnp.stack(blocks).astype(jnp.int32)
    places = jnp.arange(len(blocks), dtype=jnp.int32)
    back_place = jnp.sum(
        jnp.where(place_of[None] == places[:, None], places[None], 0), axis=1, dtype=jnp.int32
    )

    def split(w):
        half = w.shape[1] // 2
        mine = jnp.where(core == 0, w[:, :half], w[:, half:])
        theirs = jnp.where(core == 0, w[:, half:], w[:, :half])
        return mine, theirs

    def own_columns(weights, shared=()):
        pairs = [split(w) for w in weights] + [(w, w) for w in shared]
        mine = jnp.concatenate([p[0] for p in pairs], 1)
        got = swap(jnp.concatenate([p[1] for p in pairs], 1), "seq", CORE)
        return jnp.concatenate(
            [jnp.where(core == 0, mine, got), jnp.where(core == 0, got, mine)], 0
        )

    plane = Plane(
        [
            [("mixer", 0)],
            [("two", 0)],
            [("mixer", 1)],
            [("two", 1)],
            [("far mixer", 0)],
            [("three", 0)],
            [("far mixer", 1)],
            [("three", 1), ("far two", 0)],
            [("down", 0)],
            [("far two", 1), ("far three", 0)],
            [("down", 1), ("far down", 0)],
            [("far three", 1)],
            [("far down", 1)],
        ]
    )
    phases = plane.phases

    def gathered(name, start, width):
        near = same_order([x[:, start : start + width] for x in phases[name].parts], core)
        far = same_order([x[:, start : start + width] for x in phases["far " + name].parts], core)
        return near + far

    low_pad = jnp.pad(w_lowrank, ((0, 0), (0, 128 - w_lowrank.shape[1])))
    hidden_width = w_gate.shape[1] // 2
    wide_mixer = 2 * KD + 2 * VD
    width = wide_mixer + 128
    fill = width - VD
    chip_mixer = own_columns([w_query, w_key, w_value, w_outgate], [low_pad])
    phases["mixer"] = Spread(chip_mixer)
    phases["far mixer"] = Spread(swap(chip_mixer, "dp"))
    plane.slot()
    tokens, cotangent, w_output, w_gate = tie((tokens, cotangent, w_output, w_gate), chip_mixer)
    chip_gate = own_columns([w_gate])
    chip_two = jnp.concatenate([own_columns([w_output.T]), chip_gate[:, :fill]], 1)
    phases["two"] = Spread(chip_two)
    plane.slot()
    w_up, w_down = tie((w_up, w_down), plane.done[0])
    chip_three = jnp.concatenate([chip_gate[:, fill:], own_columns([w_up])], 1)
    chip_down = own_columns([w_down.T])
    phases["three"] = Spread(chip_three)
    phases["down"] = Spread(chip_down)
    rows = chip_two.shape[0]
    far_both = jnp.concatenate([chip_two, chip_three], 0)
    far_both = swap(far_both, "dp")
    phases["far two"] = Spread(far_both[:rows])
    phases["far three"] = Spread(far_both[rows:])
    phases["far down"] = Spread(swap(tie(chip_down, phases["far mixer"].parts[0]), "dp"))
    plane.until("mixer", "far mixer")
    w_mixer = jnp.concatenate(gathered("mixer", 0, width), 0)

    cot, low_tokens = reorder(place_of, cotangent, tokens)
    gains = jnp.concatenate([mix_gain[None], mlp_gain[None]], 0)
    gains = reorder(place_of, jnp.pad(gains, ((0, 6), (0, 0))))[0]
    gain1, gain2 = gains[0], gains[1]
    cot_both = both(cot, core)
    inputs = low_tokens.astype(F32)
    length = 2 * tokens.shape[0]

    normed, norm_back = jax.vjp(rms_norm, inputs, gain1)
    normed_own = normed.astype(BF16)
    normed_low = both(normed_own, core)
    projected = matmul(normed_low, w_mixer)
    outgate = projected[:, 2 * KD + VD : wide_mixer]
    rank = w_lowrank.shape[1]
    rank_part = projected[:, wide_mixer : wide_mixer + rank].astype(BF16)
    rate = jnp.where(core == 0, w_rate[:, :KD], w_rate[:, KD:])
    bias = jnp.where(core == 0, rate_bias[:KD], rate_bias[KD:])
    logit = matmul(rank_part, rate) + bias
    decay = jax.nn.log_sigmoid(logit) / normalizer
    local_output, lifted, states, state_end, edge, fades = mixer_forward(projected, decay)
    incoming_state = incoming(edge, state_end)
    mixed_output = local_output + dot(lifted, incoming_state, (1, 1), PASSES)
    plane.until("two")
    while len(plane.done) < 9:
        plane.slot()
    plane.slot(incoming_state)
    plane.until("far two")
    w_out = jnp.concatenate(gathered("two", 0, VD), 0)
    gated, gated_back = jax.vjp(head_norm, mixed_output, outgate, head_gain)
    gated_low = gated.astype(BF16)
    mixer_chip = core_sum(times_back(gated_low, w_out), core)
    mixer_head = swap(mixer_chip, "head")
    plane.slot(mixer_chip)
    plane.slot(mixer_head)
    plane.until(*phases)
    middle = inputs + (mixer_chip.astype(F32) + mixer_head.astype(F32))
    rest = hidden_width - fill
    full_gate = jnp.concatenate(
        [
            jnp.concatenate(pair, 1)
            for pair in zip(gathered("two", VD, fill), gathered("three", 0, rest))
        ],
        0,
    )
    full_up = jnp.concatenate(gathered("three", rest, hidden_width), 0)
    w_dn = jnp.concatenate(gathered("down", 0, hidden_width), 0)
    normed2, norm2_back = jax.vjp(rms_norm, middle, gain2)
    normed2_low = both(normed2.astype(BF16), core)
    gate = matmul(normed2_low, full_gate)
    upward = matmul(normed2_low, full_up)
    hidden_low = swiglu(gate, upward).astype(BF16)
    cot_core = core_order(cot_both, core)
    normed_core = core_order(normed_low, core)
    normed2_core = core_order(normed2_low, core)
    back = Plane(
        [
            [("far down", 0)],
            [("down", 0)],
            [("far gate", 0), ("far down", 1)],
            [("gate", 0), ("down", 1)],
            [("far up", 0), ("far gate", 1)],
            [("up", 0), ("gate", 1)],
            [("far output", 0), ("far up", 1)],
            [("output", 0), ("up", 1)],
            [("far qkv", 0), ("far output", 1)],
            [("qkv", 0), ("output", 1)],
            [("far qkv", 1)],
            [("qkv", 1)],
        ],
        reverse=True,
    )
    sums = back.phases
    sums["far down"], sums["down"] = halves([(cot_core, hidden_low)])
    back.slot(plane.done[-1])
    back.slot()

    gate, upward, full_gate, full_up = tie((gate, upward, full_gate, full_up), w_dn)
    grad_hidden = matmul(cot_both, w_dn)
    sigma = jax.nn.sigmoid(gate)
    gate_low = (grad_hidden * upward * sigma * (1.0 + gate * (1.0 - sigma))).astype(BF16)
    upward_low = (grad_hidden * gate * sigma).astype(BF16)
    part = times_back(gate_low, full_gate) + times_back(upward_low, full_up)
    chip_sum = core_sum(part, core)
    head_part = swap(chip_sum, "head")
    grad_normed2 = chip_sum.astype(F32) + head_part.astype(F32)
    sums["far gate"], sums["gate"] = halves([(normed2_core, gate_low)])
    sums["far up"], sums["up"] = halves([(normed2_core, upward_low)])
    back.slot()
    back.slot()
    feed_chip = core_sum(times_back(tie(hidden_low, chip_sum), w_dn), core)
    feed_head = swap(tie(feed_chip, head_part), "head")
    result = reorder(back_place, (middle + (feed_chip.astype(F32) + feed_head.astype(F32))).astype(BF16))[0]
    back.slot(chip_sum)
    back.slot(feed_chip)
    middle_grad, grad_mlp_gain = norm2_back(grad_normed2)
    grad_middle = cot.astype(F32) + middle_grad
    middle_low = both(grad_middle.astype(BF16), core)
    grad_gated = matmul(middle_low, w_out)
    mixed_gradient, outgate_grad, head_gain_part = gated_back(grad_gated)
    outgate_low = outgate_grad.astype(BF16)
    middle_core = core_order(middle_low, core)
    sums["far output"], sums["output"] = halves(
        [(middle_core, gated_low), (normed_core, outgate_low)]
    )
    outgoing = incoming(edge, dot(mixed_gradient, lifted, (0, 0), PASSES), reverse=True)
    if len(chip_bits()) == 2:
        back.slot()
        back.slot(outgoing, feed_head)
    qkv_low, decay_grad = mixer_backward(
        projected, decay, mixed_gradient, states, fades, incoming_state, outgoing
    )
    logit_low = (decay_grad * jax.nn.sigmoid(-logit) / normalizer).astype(BF16)
    grad_rate = inner(rank_part, logit_low)
    grad_rate_bias = jnp.sum(logit_low.astype(F32), axis=0)
    rank_low = times_back(logit_low, rate).astype(BF16)
    rank_low = jnp.pad(rank_low, ((0, 0), (0, 128 - rank)))
    mixer_low = jnp.concatenate([qkv_low, outgate_low, rank_low], 1)
    normed_chip = core_sum(times_back(mixer_low, w_mixer), core)
    normed_head = swap(normed_chip, "head")
    grad_normed = normed_chip.astype(F32) + normed_head.astype(F32)
    qkv_rank = jnp.concatenate([qkv_low, rank_low], 1)
    sums["far qkv"], sums["qkv"] = halves([(normed_core, qkv_rank)])
    back.slot(normed_chip)
    back.slot()
    back.slot(result)
    back.slot(normed_head)
    back.until(*sums)
    inputs_grad, grad_mix_gain = norm_back(grad_normed)
    grad_tokens = reorder(back_place, grad_middle + inputs_grad)[0]

    finished = []
    for i, name in enumerate(("down", "gate", "up", "output", "qkv")):
        got = swap(sums["far " + name].rows.astype(BF16), "dp")
        if 2 * i + 4 < len(back.done):
            got = tie(got, back.done[2 * i + 4])
        finished.append(sums[name].rows + got.astype(F32))
    grad_down, grad_gate, grad_up, grad_output, grad_qkv = finished

    def own_rows(chip_rows):
        mine = jnp.where(core == 0, chip_rows[:wide], chip_rows[wide:])
        theirs = jnp.where(core == 0, chip_rows[wide:], chip_rows[:wide])
        got = swap(theirs.astype(BF16), "seq", CORE).astype(F32)
        return jnp.where(core == 0, mine, got), jnp.where(core == 0, got, mine)

    def columns(pair, start, width):
        return jnp.concatenate([part[:, start : start + width] for part in pair], 1)

    qkv_pair = own_rows(grad_qkv[:, : 2 * KD + VD])
    sum_query = columns(qkv_pair, 0, KD)
    sum_key = columns(qkv_pair, KD, KD)
    sum_value = columns(qkv_pair, 2 * KD, VD)
    low_rows = grad_qkv[:, 2 * KD + VD : 2 * KD + VD + rank]
    low_mine = jnp.where(core == 0, low_rows[:wide], low_rows[wide:])
    low_theirs = jnp.where(core == 0, low_rows[wide:], low_rows[:wide])
    low_mine = low_mine + swap(low_theirs, "seq", CORE)
    sum_lowrank = low_mine + swap(low_mine, "head")
    output_pair = own_rows(grad_output)
    sum_output = columns(output_pair, 0, VD).T
    sum_outgate = columns(output_pair, VD, VD)
    sum_gate = jnp.concatenate(own_rows(grad_gate), 1)
    sum_up = jnp.concatenate(own_rows(grad_up), 1)
    sum_down = jnp.concatenate(own_rows(grad_down), 1).T

    zero = jnp.zeros_like(grad_rate)
    wide_rate = jnp.where(
        core == 0,
        jnp.concatenate([grad_rate, zero], 1),
        jnp.concatenate([zero, grad_rate], 1),
    )
    wide_bias = jnp.where(
        core == 0,
        jnp.concatenate([grad_rate_bias, zero[0]]),
        jnp.concatenate([zero[0], grad_rate_bias]),
    )
    head_gain_part = head_gain_part + swap(head_gain_part[None], "head")[0]
    gains = jnp.pad(jnp.stack([grad_mix_gain, grad_mlp_gain]), ((0, 6), (0, 0)))
    gains = reorder(back_place, gains)[0][:2]
    model = gains.shape[1]
    others = jnp.concatenate([wide_rate.reshape(-1), wide_bias, head_gain_part])
    others = jnp.pad(others, (0, 6 * model - others.shape[0])).reshape(6, model)
    small = jnp.concatenate([gains, others], 0)
    for axis, bits in (("seq", [CORE] + chip_bits()), ("dp", [1])):
        for bit in bits:
            small = small + swap(small, axis, bit)
    sum_mix_gain, sum_mlp_gain = small[0], small[1]
    others = small[2:].reshape(-1)
    at = wide_rate.size
    sum_rate = others[:at].reshape(wide_rate.shape)
    sum_rate_bias = others[at : at + wide_bias.size]
    at = at + wide_bias.size
    sum_head_gain = others[at : at + VD]
    return (
        result,
        grad_tokens,
        sum_mix_gain,
        sum_query,
        sum_key,
        sum_value,
        sum_outgate,
        sum_lowrank,
        sum_rate,
        sum_rate_bias,
        sum_head_gain,
        sum_output,
        sum_mlp_gain,
        sum_gate,
        sum_up,
        sum_down,
    )


def solution(mesh):
    rows = P(("dp", "seq"), None)
    in_columns = P(("dp", "seq"), "head")
    in_rows = P("head", ("dp", "seq"))
    in_specs = (
        rows,
        P(),
        in_columns,
        in_columns,
        in_columns,
        in_columns,
        rows,
        P(None, "head"),
        P("head"),
        P(),
        in_rows,
        P(),
        in_columns,
        in_columns,
        in_rows,
        rows,
    )
    out_specs = (
        rows,
        rows,
        P(),
        in_columns,
        in_columns,
        in_columns,
        in_columns,
        rows,
        P(None, "head"),
        P("head"),
        P(),
        in_rows,
        P(),
        in_columns,
        in_columns,
        in_rows,
    )
    return jax.shard_map(body, mesh=mesh, in_specs=in_specs, out_specs=out_specs, check_vma=False)
```

time: 1420 us -> 783 us (0.55)
  waiting for transfers between devices: 594 us -> 361 us
  blocking collectives: 124 us -> 0 us
  local copies, waits for them, and re-layouts: 178 us -> 59.4 us
  matrix products: 196 us -> 125 us
  starting transfers between devices: 123 us -> 74.4 us
  other arithmetic: 164 us -> 122 us
  Pallas kernels: 0 us -> 26.8 us
  between operations: 27.5 us -> 3.76 us
    ppermute x102 -> x37, waiting for transfers between devices: 515 us -> 135 us  [swap(): return lax.ppermute(x, axis, [(i, i ^ bit) for i in range(count)])]
    ppermute x10 -> x42, waiting for transfers between devices: 1.52 us -> 225 us  [the longest x36 225 us: hop(): return lax.ppermute(x, 'seq', [(i, i ^ there[i % 2]) for i in range(count)])]
    psum x2 -> x0, blocking collectives: 101 us -> none  [the longest x1 58.8 us: body(): lax.psum((whole(grad_mix_gain[None])[0], whole(grad_mlp_gain[None])[0], w...]
    dot_general x159 -> x2, matrix products: 91.4 us -> 0.83 us  [once(): return lax.dot_general(x, y, dims, preferred_element_type=F32)]
    ppermute x102 -> x37, starting transfers between devices: 99.4 us -> 17.6 us  [swap(): return lax.ppermute(x, axis, [(i, i ^ bit) for i in range(count)])]
    psum x1 -> x0, waiting for transfers between devices: 77.6 us -> none  [body(): lax.psum((whole(grad_mix_gain[None])[0], whole(grad_mlp_gain[None])[0], w...]
    unnamed x514 -> x289, local copies, waits for them, and re-layouts: 74.4 us -> 32.8 us
    dynamic_slice x60 -> x0, local copies, waits for them, and re-layouts: 36.7 us -> none  [block_scan(): lax.scan(jax.checkpoint(block_step), state_value, pieces)]
  transfers between devices with their start and end apart: 113 -> 79, of which waited for: 44 -> 30; matrix products, arithmetic and copies ran while one was open for 31% -> 28% of each run, Pallas kernels for 0% -> 3%
where the time goes in v2:
time: 783 us; the launch traced here: 772 us
  waiting for transfers between devices  361 us (46%)
  matrix products  125 us (16%)
  other arithmetic  122 us (16%)
  starting transfers between devices  74.4 us (10%)
  local copies, waits for them, and re-layouts  59.4 us (8%)
  Pallas kernels  26.8 us (3%)
    ppermute x36, waiting for transfers between devices, hop(): return lax.ppermute(x, 'seq', [(i, i ^ there[i % 2]) for i in range(count)])  225 us
    ppermute x37, waiting for transfers between devices, swap(): return lax.ppermute(x, axis, [(i, i ^ bit) for i in range(count)])  135 us
    dot_general x6, matrix products, matmul(): return jnp.dot(left, right, preferred_element_type=F32)  46.4 us
    ppermute x36, starting transfers between devices, hop(): return lax.ppermute(x, 'seq', [(i, i ^ there[i % 2]) for i in range(count)])  45.7 us
    dot_general x13, matrix products, inner(): lax.dot_general(left, right, (((0,), (0,)), ((), ())), preferred_element_...  40.3 us
    dot_general x6, matrix products, times_back(): lax.dot_general(grad, weight, (((1,), (1,)), ((), ())), preferred_element...  37.6 us
    unnamed x289, local copies, waits for them, and re-layouts  32.8 us
    unnamed x42, other arithmetic  27.5 us
  transfers between devices with their start and end apart: 79, of which 30 were waited for; matrix products, arithmetic and copies ran while one was open for 28% of the time, Pallas kernels for 3%

profile of v2, /device:TPU:0, one launch (start us, length us, event | category | flops | bytes accessed | tf_op | source)
XLA Modules:
  0.0 771.9 jit_solution(14168304555767846311)
XLA Ops:
  45.1 10.1 %collective-permute-done.4 = bf16[256,1664]{1,0:T(8,128)(2,1)} collective-permute-done((bf16[256,1664]{1,0:T(8,128)(2,1)}, bf16[256,1664]{1,0:T(8,128)(2,1)}, u32[]{:S(2)}, u32[]{:S(2)}) %collective-permute-start.4) | collective-permute-done | bytes 852000 | tf_op jit(solution)/shard_map/ppermute | solution.py:24
  71.9 15.8 %collective-permute-done.5 = bf16[256,1664]{1,0:T(8,128)(2,1)S(1)} collective-permute-done((bf16[256,1664]{1,0:T(8,128)(2,1)}, bf16[256,1664]{1,0:T(8,128)(2,1)S(1)}, u32[]{:S(2)}, u32[]{:S(2)}) %collective-permute-start.5) | collective-permute-done | bytes 852000 | tf_op jit(solution)/shard_map/ppermute | solution.py:228
  95.8 18.1 %collective-permute-done.16 = bf16[256,1664]{1,0:T(8,128)(2,1)S(1)} collective-permute-done((bf16[256,1664]{1,0:T(8,128)(2,1)S(1)}, bf16[256,1664]{1,0:T(8,128)(2,1)S(1)}, u32[]{:S(2)}, u32[]{:S(2)}) %collective-permute-start.16) | collective-permute-done | bytes 852000 | tf_op jit(solution)/shard_map/ppermute | solution.py:228
  113.8 7.5 pad_maximum_fusion.14
  122.5 2.8 copy-done.108
  125.3 5.9 fusion.8.q_ref.k_ref.v_ref
  133.1 7.6 mixer_forward.1
  145.9 3.2 collective-permute-start.7
  150.4 45.6 %collective-permute-done.15 = bf16[512,1664]{1,0:T(8,128)(2,1)S(1)} collective-permute-done((bf16[512,1664]{1,0:T(8,128)(2,1)S(1)}, bf16[512,1664]{1,0:T(8,128)(2,1)S(1)}, u32[]{:S(2)}, u32[]{:S(2)}) %collective-permute-start.15) | collective-permute-done | bytes 1703968 | tf_op jit(solution)/shard_map/ppermute | solution.py:24
  200.9 31.9 %collective-permute-done.17 = bf16[256,1664]{1,0:T(8,128)(2,1)S(1)} collective-permute-done((bf16[256,1664]{1,0:T(8,128)(2,1)S(1)}, bf16[256,1664]{1,0:T(8,128)(2,1)S(1)}, u32[]{:S(2)}, u32[]{:S(2)}) %collective-permute-start.17) | collective-permute-done | bytes 852000 | tf_op jit(solution)/shard_map/ppermute | solution.py:228
  239.4 24.1 %collective-permute-done.19 = bf16[512,1664]{1,0:T(8,128)(2,1)S(1)} collective-permute-done((bf16[512,1664]{1,0:T(8,128)(2,1)S(1)}, bf16[512,1664]{1,0:T(8,128)(2,1)S(1)}, u32[]{:S(2)}, u32[]{:S(2)}) %collective-permute-start.19) | collective-permute-done | bytes 1703968 | tf_op jit(solution)/shard_map/ppermute | solution.py:228
  275.4 17.8 %collective-permute-done.30 = bf16[256,1408]{1,0:T(8,128)(2,1)S(1)} collective-permute-done((bf16[256,1408]{1,0:T(8,128)(2,1)S(1)}, bf16[256,1408]{1,0:T(8,128)(2,1)S(1)}, u32[]{:S(2)}, u32[]{:S(2)}) %collective-permute-start.30) | collective-permute-done | bytes 720928 | tf_op jit(solution)/shard_map/ppermute | solution.py:228
  293.3 3.9 collective-permute-done.29
  302.1 9.0 %collective-permute-done.21 = bf16[384,2048]{1,0:T(8,128)(2,1)S(1)} collective-permute-done((bf16[384,2048]{1,0:T(8,128)(2,1)S(1)}, bf16[384,2048]{1,0:T(8,128)(2,1)S(1)}, u32[]{:S(2)}, u32[]{:S(2)}) %collective-permute-start.21) | collective-permute-done | bytes 1572896 | tf_op jit(solution)/shard_map/ppermute | solution.py:24
  318.7 18.2 %collective-permute-done.24 = bf16[512,1664]{1,0:T(8,128)(2,1)S(1)} collective-permute-done((bf16[512,1664]{1,0:T(8,128)(2,1)S(1)}, bf16[512,1664]{1,0:T(8,128)(2,1)S(1)}, u32[]{:S(2)}, u32[]{:S(2)}) %collective-permute-start.24) | collective-permute-done | bytes 1703968 | tf_op jit(solution)/shard_map/ppermute | solution.py:228
  339.7 10.9 %fusion.28 = f32[768,1408]{1,0:T(8,128)} fusion(bf16[2048,1408]{1,0:T(8,128)(2,1)} %maximum_dynamic-update-slice_fusion, bf16[384,2048]{1,0:T(8,128)(2,1)S(1)} %get-tuple-element.270, bf16[384,2048]{1,0:T(8,128)(2,1)S(1)} %get-tuple-element.269), kind=kOutput, calls=%fused_computation.117 | convolution fusion | flops 4435476480 | bytes 13238272 | tf_op jit(solution)/shard_map/dot_general | solution.py:28
  351.1 11.2 %multiply_convert_fusion.2 = (bf16[768,1408]{1,0:T(8,128)(2,1)S(1)}, f32[768,1408]{1,0:T(8,128)}) fusion(f32[768,1408]{1,0:T(8,128)} %fusion.28, bf16[2048,1408]{1,0:T(8,128)(2,1)S(1)} %slice_dynamic-update-slice_fusion.4, bf16[384,2048]{1,0:T(8,128)(2,1)S(1)} %get-tuple-element.270, bf16[384,2048]{1,0:T(8,128)(2,1)S(1)} %get-tuple-element.269), kind=kOutput, calls=%fused_computation.46 | convolution fusion | flops 4441964544 | bytes 19726336 | tf_op jit(solution)/shard_map/dot_general | solution.py:28
  362.4 11.2 %multiply_convert_fusion = (bf16[768,1408]{1,0:T(8,128)(2,1)}, bf16[768,1408]{1,0:T(8,128)(2,1)S(1)}) fusion(f32[768,1408]{1,0:T(8,128)} %fusion.28, f32[768,1408]{1,0:T(8,128)} %get-tuple-element.103, bf16[2048,1408]{1,0:T(8,128)(2,1)S(1)} %slice_dynamic-update-slice_fusion.2, bf16[384,2048]{1,0:T(8,128)(2,1)S(1)} %copy-done.26, ...), kind=kOutput, calls=%fused_computation.43 | convolution fusion | flops 4449533952 | bytes 21889024 | tf_op jit(solution)/shard_map/dot_general | solution.py:28
  373.6 10.5 %fusion.167 = f32[768,2048]{1,0:T(8,128)} fusion(bf16[768,1408]{1,0:T(8,128)(2,1)S(1)} %get-tuple-element.245, bf16[2048,1408]{1,0:T(8,128)(2,1)} %maximum_dynamic-update-slice_fusion), kind=kOutput, calls=%fused_computation.477 | convolution fusion | flops 4429185024 | bytes 14221312 | tf_op jit(solution)/shard_map/dot_general | solution.py:36
  384.1 8.1 %convolution_add_fusion = f32[768,2048]{1,0:T(8,128)S(1)} fusion(f32[768,2048]{1,0:T(8,128)} %fusion.167, bf16[768,1408]{1,0:T(8,128)(2,1)} %get-tuple-element.244, bf16[2048,1408]{1,0:T(8,128)(2,1)S(1)} %copy-done.112), kind=kOutput, calls=%fused_computation.57 | convolution fusion | flops 4430757888 | bytes 20512768 | tf_op jit(solution)/shard_map/dot_general | solution.py:36
  393.5 5.2 convolution_convert_fusion.4
  400.4 3.1 convolution_convert_fusion
  405.1 5.2 convolution_convert_fusion.6
  410.4 5.3 convolution_convert_fusion.5
  415.7 5.1 convolution_convert_fusion.2
  420.8 3.9 convolution_convert_fusion.1
  440.7 7.9 %fusion.168 = f32[768,2048]{1,0:T(8,128)S(1)} fusion(bf16[768,1408]{1,0:T(8,128)(2,1)} %copy-done.124, bf16[2048,1408]{1,0:T(8,128)(2,1)} %copy-done.110), kind=kOutput, calls=%fused_computation.478 | convolution fusion | flops 4429185024 | bytes 14221312 | tf_op jit(solution)/shard_map/dot_general | solution.py:36
  450.0 18.4 %collective-permute-done.59 = bf16[256,1408]{1,0:T(8,128)(2,1)} collective-permute-done((bf16[256,1408]{1,0:T(8,128)(2,1)}, bf16[256,1408]{1,0:T(8,128)(2,1)}, u32[]{:S(2)}, u32[]{:S(2)}) %collective-permute-start.59) | collective-permute-done | bytes 720928 | tf_op jit(solution)/shard_map/ppermute | solution.py:228
  473.9 8.4 %collective-permute-done.58 = bf16[512,1408]{1,0:T(8,128)(2,1)} collective-permute-done((bf16[512,1408]{1,0:T(8,128)(2,1)}, bf16[512,1408]{1,0:T(8,128)(2,1)}, u32[]{:S(2)}, u32[]{:S(2)}) %collective-permute-start.58) | collective-permute-done | bytes 1441824 | tf_op jit(solution)/shard_map/ppermute | solution.py:228
  493.0 12.5 %collective-permute-done.61 = bf16[256,1408]{1,0:T(8,128)(2,1)} collective-permute-done((bf16[256,1408]{1,0:T(8,128)(2,1)}, bf16[256,1408]{1,0:T(8,128)(2,1)}, u32[]{:S(2)}, u32[]{:S(2)}) %collective-permute-start.61) | collective-permute-done | bytes 720928 | tf_op jit(solution)/shard_map/ppermute | solution.py:228
  516.0 11.6 %collective-permute-done.50 = bf16[512,1408]{1,0:T(8,128)(2,1)S(1)} collective-permute-done((bf16[512,1408]{1,0:T(8,128)(2,1)S(1)}, bf16[512,1408]{1,0:T(8,128)(2,1)S(1)}, u32[]{:S(2)}, u32[]{:S(2)}) %collective-permute-start.50) | collective-permute-done | bytes 1441824 | tf_op jit(solution)/shard_map/ppermute | solution.py:228
  530.9 2.9 copy.73
  536.3 5.3 multiply_reduce_fusion.3
  563.0 3.4 collective-permute-start.62
  566.7 12.1 %mixer_backward.1 = (bf16[768,1024]{1,0:T(8,128)(2,1)S(1)}, f32[768,256]{1,0:T(8,128)S(1)}) custom-call(f32[768,1664]{1,0:T(8,128)S(1)} %bitcast.60, f32[768,1664]{1,0:T(8,128)S(1)} %bitcast.60, f32[768,1664]{1,0:T(8,128)S(1)} %bitcast.60, f32[768,256]{1,0:T(8,128)S(1)} %copy-done.9, f32[768,512]{1,0:T(8,128)S(1)} %add_add_fusion.2.grad_ref, ...), custom_call_target="tpu_custom_call" | custom-call | tf_op jit(solution)/shard_map/mixer_backward/pallas_call | solution.py:182
  580.5 9.1 %fusion.21 = f32[768,2048]{1,0:T(8,128)S(1)} fusion(bf16[2048,1664]{1,0:T(8,128)(2,1)} %copy-done.108, bf16[768,128]{1,0:T(8,128)(2,1)S(1)} %pad.31, bf16[768,512]{1,0:T(8,128)(2,1)} %copy-done.123, bf16[768,1024]{1,0:T(8,128)(2,1)} %copy-done.14), kind=kOutput, calls=%fused_computation.99 | convolution fusion | flops 5242159104 | bytes 15663104 | tf_op jit(solution)/shard_map/dot_general | solution.py:36
  593.8 3.7 convolution_convert_fusion.7
  600.8 3.6 convolution_convert_fusion.3
  612.4 9.4 %collective-permute-done.52 = bf16[512,1024]{1,0:T(8,128)(2,1)S(1)} collective-permute-done((bf16[512,1024]{1,0:T(8,128)(2,1)}, bf16[512,1024]{1,0:T(8,128)(2,1)S(1)}, u32[]{:S(2)}, u32[]{:S(2)}) %collective-permute-start.52) | collective-permute-done | bytes 1048608 | tf_op jit(solution)/shard_map/ppermute | solution.py:228
  630.2 19.7 %collective-permute-done.65 = bf16[256,1024]{1,0:T(8,128)(2,1)S(1)} collective-permute-done((bf16[256,1024]{1,0:T(8,128)(2,1)S(1)}, bf16[256,1024]{1,0:T(8,128)(2,1)S(1)}, u32[]{:S(2)}, u32[]{:S(2)}) %collective-permute-start.65) | collective-permute-done | bytes 524320 | tf_op jit(solution)/shard_map/ppermute | solution.py:228
  654.9 8.3 %collective-permute-done.64 = bf16[512,1152]{1,0:T(8,128)(2,1)S(1)} collective-permute-done((bf16[512,1152]{1,0:T(8,128)(2,1)S(1)}, bf16[512,1152]{1,0:T(8,128)(2,1)S(1)}, u32[]{:S(2)}, u32[]{:S(2)}) %collective-permute-start.64) | collective-permute-done | bytes 1179680 | tf_op jit(solution)/shard_map/ppermute | solution.py:228
  665.2 32.4 %collective-permute-done.41 = bf16[384,2048]{1,0:T(8,128)(2,1)S(1)} collective-permute-done((bf16[384,2048]{1,0:T(8,128)(2,1)S(1)}, bf16[384,2048]{1,0:T(8,128)(2,1)S(1)}, u32[]{:S(2)}, u32[]{:S(2)}) %collective-permute-start.41) | collective-permute-done | bytes 1572896 | tf_op jit(solution)/shard_map/ppermute | solution.py:24
  702.1 3.1 collective-permute-done.44
  705.6 3.9 collective-permute-done.45
  709.7 5.5 fusion.5
  732.8 2.9 collective-permute-start.67
  736.8 25.5 %collective-permute-done.67 = bf16[256,1152]{1,0:T(8,128)(2,1)S(1)} collective-permute-done((bf16[256,1152]{1,0:T(8,128)(2,1)S(1)}, bf16[256,1152]{1,0:T(8,128)(2,1)S(1)}, u32[]{:S(2)}, u32[]{:S(2)}) %collective-permute-start.67) | collective-permute-done | bytes 589856 | tf_op jit(solution)/shard_map/ppermute | solution.py:24
  765.0 3.2 collective-permute-done.72
  (658 shorter events, 254.2 us)
Async XLA Ops:
  14.6 40.6 %collective-permute-start.4 = (bf16[256,1664]{1,0:T(8,128)(2,1)}, bf16[256,1664]{1,0:T(8,128)(2,1)}, u32[]{:S(2)}, u32[]{:S(2)}) collective-permute-start(bf16[256,1664]{1,0:T(8,128)(2,1)} %pad_maximum_fusion.45), channel_id=1, source_target_pairs={{0,16},{16,0},{1,17},{17,1},{2,18},{18,2},{3,19},{19,3},{4,20},{20... | collective-permute-start | bytes 2555912 | tf_op jit(solution)/shard_map/ppermute | solution.py:24
  20.4 37.1 %collective-permute-start.1 = (bf16[384,2048]{1,0:T(8,128)(2,1)}, bf16[384,2048]{1,0:T(8,128)(2,1)}, u32[]{:S(2)}, u32[]{:S(2)}) collective-permute-start(bf16[384,2048]{1,0:T(8,128)(2,1)} %fusion.2), channel_id=1, source_target_pairs={{0,2},{2,0},{4,6},{6,4},{8,10},{10,8},{12,14},{14,12},{1,3},{3,1},... | collective-permute-start | bytes 4718600 | tf_op jit(solution)/shard_map/ppermute | solution.py:24
  24.0 36.0 %collective-permute-start.25 = (bf16[384,2048]{1,0:T(8,128)(2,1)S(1)}, bf16[384,2048]{1,0:T(8,128)(2,1)}, u32[]{:S(2)}, u32[]{:S(2)}) collective-permute-start(bf16[384,2048]{1,0:T(8,128)(2,1)S(1)} %get-tuple-element.96), channel_id=1, source_target_pairs={{0,2},{2,0},{4,6},{6,4},{8,10},{10,8},{12,14},{14,12},{1,3},{3,1},... | collective-permute-start | bytes 4718600 | tf_op jit(solution)/shard_map/ppermute | solution.py:24
  38.3 30.3 %collective-permute-start.3 = (bf16[512,1664]{1,0:T(8,128)(2,1)}, bf16[512,1664]{1,0:T(8,128)(2,1)S(1)}, u32[]{:S(2)}, u32[]{:S(2)}) collective-permute-start(bf16[512,1664]{1,0:T(8,128)(2,1)} %pad_maximum_fusion.10), channel_id=1, source_target_pairs={{0,8},{2,6},{4,12},{6,2},{8,0},{10,14},{12,4},{14,10},{1,9},{3,7},... | collective-permute-start | bytes 5111816 | tf_op jit(solution)/shard_map/ppermute | solution.py:228
  55.2 36.7 %collective-permute-start.13 = (bf16[512,1664]{1,0:T(8,128)(2,1)S(1)}, bf16[512,1664]{1,0:T(8,128)(2,1)S(1)}, u32[]{:S(2)}, u32[]{:S(2)}) collective-permute-start(bf16[512,1664]{1,0:T(8,128)(2,1)S(1)} %pad_maximum_fusion.12), channel_id=1, source_target_pairs={{0,8},{2,6},{4,12},{6,2},{8,0},{10,14},{12,4},{14,10},{1,9},{3,7},... | collective-permute-start | bytes 5111816 | tf_op jit(solution)/shard_map/ppermute | solution.py:228
  55.6 214.8 %collective-permute-start.28 = (bf16[256,1408]{1,0:T(8,128)(2,1)}, bf16[256,1408]{1,0:T(8,128)(2,1)S(1)}, u32[]{:S(2)}, u32[]{:S(2)}) collective-permute-start(bf16[256,1408]{1,0:T(8,128)(2,1)} %pad_maximum_fusion.47), channel_id=1, source_target_pairs={{0,16},{16,0},{1,17},{17,1},{2,18},{18,2},{3,19},{19,3},{4,20},{20... | collective-permute-start | bytes 2162696 | tf_op jit(solution)/shard_map/ppermute | solution.py:24
  89.0 32.8 %collective-permute-start.6 = (bf16[512,1664]{1,0:T(8,128)(2,1)S(1)}, bf16[512,1664]{1,0:T(8,128)(2,1)S(1)}, u32[]{:S(2)}, u32[]{:S(2)}) collective-permute-start(bf16[512,1664]{1,0:T(8,128)(2,1)S(1)} %pad_maximum_fusion.11), channel_id=1, source_target_pairs={{0,8},{2,6},{4,12},{6,2},{8,0},{10,14},{12,4},{14,10},{1,9},{3,7},... | collective-permute-start | bytes 5111816 | tf_op jit(solution)/shard_map/ppermute | solution.py:228
  91.9 21.9 %collective-permute-start.16 = (bf16[256,1664]{1,0:T(8,128)(2,1)S(1)}, bf16[256,1664]{1,0:T(8,128)(2,1)S(1)}, u32[]{:S(2)}, u32[]{:S(2)}) collective-permute-start(bf16[256,1664]{1,0:T(8,128)(2,1)S(1)} %maximum_maximum_fusion.1), channel_id=1, source_target_pairs={{0,4},{2,10},{4,0},{6,14},{8,12},{10,2},{12,8},{14,6},{1,5},{3,11}... | collective-permute-start | bytes 2555912 | tf_op jit(solution)/shard_map/ppermute | solution.py:228
  121.4 74.6 %collective-permute-start.15 = (bf16[512,1664]{1,0:T(8,128)(2,1)S(1)}, bf16[512,1664]{1,0:T(8,128)(2,1)S(1)}, u32[]{:S(2)}, u32[]{:S(2)}) collective-permute-start(bf16[512,1664]{1,0:T(8,128)(2,1)S(1)} %get-tuple-element.298), channel_id=1, source_target_pairs={{0,16},{16,0},{1,17},{17,1},{2,18},{18,2},{3,19},{19,3},{4,20},{20... | collective-permute-start | bytes 5111816 | tf_op jit(solution)/shard_map/ppermute | solution.py:24
  143.4 54.3 %collective-permute-start.8 = (bf16[528,256]{1,0:T(8,128)(2,1)S(1)}, bf16[528,256]{1,0:T(8,128)(2,1)S(1)}, u32[]{:S(2)}, u32[]{:S(2)}) collective-permute-start(bf16[528,256]{1,0:T(8,128)(2,1)S(1)} %pad_maximum_fusion.59), channel_id=1, source_target_pairs={{0,8},{2,10},{4,12},{6,14},{1,9},{3,11},{5,13},{7,15},{16,24},{18,... | collective-permute-start | bytes 811016 | tf_op jit(solution)/shard_map/ppermute | solution.py:394
  145.9 52.8 %collective-permute-start.7 = (bf16[528,256]{1,0:T(8,128)(2,1)S(1)}, bf16[528,256]{1,0:T(8,128)(2,1)S(1)}, u32[]{:S(2)}, u32[]{:S(2)}) collective-permute-start(bf16[528,256]{1,0:T(8,128)(2,1)S(1)} %pad_maximum_fusion.59), channel_id=1, source_target_pairs={{0,4},{2,6},{4,8},{6,10},{8,12},{10,14},{1,5},{3,7},{5,9},{7,11},{... | collective-permute-start | bytes 811016 | tf_op jit(solution)/shard_map/ppermute | solution.py:394
  149.1 49.7 %collective-permute-start.9 = (bf16[528,256]{1,0:T(8,128)(2,1)S(1)}, bf16[528,256]{1,0:T(8,128)(2,1)S(1)}, u32[]{:S(2)}, u32[]{:S(2)}) collective-permute-start(bf16[528,256]{1,0:T(8,128)(2,1)S(1)} %pad_maximum_fusion.59), channel_id=1, source_target_pairs={{0,12},{2,14},{1,13},{3,15},{16,28},{18,30},{17,29},{19,31}} | collective-permute-start | bytes 811016 | tf_op jit(solution)/shard_map/ppermute | solution.py:394
  196.1 38.1 %collective-permute-start.18 = (bf16[512,1664]{1,0:T(8,128)(2,1)S(1)}, bf16[512,1664]{1,0:T(8,128)(2,1)S(1)}, u32[]{:S(2)}, u32[]{:S(2)}) collective-permute-start(bf16[512,1664]{1,0:T(8,128)(2,1)S(1)} %get-tuple-element.92), channel_id=1, source_target_pairs={{0,8},{2,6},{4,12},{6,2},{8,0},{10,14},{12,4},{14,10},{1,9},{3,7},... | collective-permute-start | bytes 5111816 | tf_op jit(solution)/shard_map/ppermute | solution.py:228
  197.7 38.1 %collective-permute-start.27 = (bf16[256,1408]{1,0:T(8,128)(2,1)}, bf16[256,1408]{1,0:T(8,128)(2,1)S(1)}, u32[]{:S(2)}, u32[]{:S(2)}) collective-permute-start(bf16[256,1408]{1,0:T(8,128)(2,1)} %pad_maximum_fusion.47), channel_id=1, source_target_pairs={{0,4},{2,10},{4,0},{6,14},{8,12},{10,2},{12,8},{14,6},{1,5},{3,11}... | collective-permute-start | bytes 2162696 | tf_op jit(solution)/shard_map/ppermute | solution.py:228
  198.9 33.9 %collective-permute-start.17 = (bf16[256,1664]{1,0:T(8,128)(2,1)S(1)}, bf16[256,1664]{1,0:T(8,128)(2,1)S(1)}, u32[]{:S(2)}, u32[]{:S(2)}) collective-permute-start(bf16[256,1664]{1,0:T(8,128)(2,1)S(1)} %get-tuple-element.91), channel_id=1, source_target_pairs={{0,4},{2,10},{4,0},{6,14},{8,12},{10,2},{12,8},{14,6},{1,5},{3,11}... | collective-permute-start | bytes 2555912 | tf_op jit(solution)/shard_map/ppermute | solution.py:228
  234.2 29.3 %collective-permute-start.19 = (bf16[512,1664]{1,0:T(8,128)(2,1)S(1)}, bf16[512,1664]{1,0:T(8,128)(2,1)S(1)}, u32[]{:S(2)}, u32[]{:S(2)}) collective-permute-start(bf16[512,1664]{1,0:T(8,128)(2,1)S(1)} %pad_maximum_fusion.15), channel_id=1, source_target_pairs={{0,8},{2,6},{4,12},{6,2},{8,0},{10,14},{12,4},{14,10},{1,9},{3,7},... | collective-permute-start | bytes 5111816 | tf_op jit(solution)/shard_map/ppermute | solution.py:228
  236.0 38.6 %collective-permute-start.23 = (bf16[256,1664]{1,0:T(8,128)(2,1)S(1)}, bf16[256,1664]{1,0:T(8,128)(2,1)S(1)}, u32[]{:S(2)}, u32[]{:S(2)}) collective-permute-start(bf16[256,1664]{1,0:T(8,128)(2,1)S(1)} %get-tuple-element.94), channel_id=1, source_target_pairs={{0,4},{2,10},{4,0},{6,14},{8,12},{10,2},{12,8},{14,6},{1,5},{3,11}... | collective-permute-start | bytes 2555912 | tf_op jit(solution)/shard_map/ppermute | solution.py:228
  270.5 26.8 %collective-permute-start.29 = (bf16[512,1408]{1,0:T(8,128)(2,1)S(1)}, bf16[512,1408]{1,0:T(8,128)(2,1)S(1)}, u32[]{:S(2)}, u32[]{:S(2)}) collective-permute-start(bf16[512,1408]{1,0:T(8,128)(2,1)S(1)} %pad_maximum_fusion.37), channel_id=1, source_target_pairs={{0,8},{2,6},{4,12},{6,2},{8,0},{10,14},{12,4},{14,10},{1,9},{3,7},... | collective-permute-start | bytes 4325384 | tf_op jit(solution)/shard_map/ppermute | solution.py:228
  274.8 36.3 %collective-permute-start.21 = (bf16[384,2048]{1,0:T(8,128)(2,1)S(1)}, bf16[384,2048]{1,0:T(8,128)(2,1)S(1)}, u32[]{:S(2)}, u32[]{:S(2)}) collective-permute-start(bf16[384,2048]{1,0:T(8,128)(2,1)S(1)} %add_convert_fusion.4), channel_id=1, source_target_pairs={{0,1},{1,0},{2,3},{3,2},{4,5},{5,4},{6,7},{7,6},{8,9},{9,8},{10,11... | collective-permute-start | bytes 4718600 | tf_op jit(solution)/shard_map/ppermute | solution.py:24
  315.0 21.9 %collective-permute-start.24 = (bf16[512,1664]{1,0:T(8,128)(2,1)S(1)}, bf16[512,1664]{1,0:T(8,128)(2,1)S(1)}, u32[]{:S(2)}, u32[]{:S(2)}) collective-permute-start(bf16[512,1664]{1,0:T(8,128)(2,1)S(1)} %pad_maximum_fusion.16), channel_id=1, source_target_pairs={{0,8},{2,6},{4,12},{6,2},{8,0},{10,14},{12,4},{14,10},{1,9},{3,7},... | collective-permute-start | bytes 5111816 | tf_op jit(solution)/shard_map/ppermute | solution.py:228
  392.5 46.7 %collective-permute-start.32 = (bf16[384,2048]{1,0:T(8,128)(2,1)S(1)}, bf16[384,2048]{1,0:T(8,128)(2,1)S(1)}, u32[]{:S(2)}, u32[]{:S(2)}) collective-permute-start(bf16[384,2048]{1,0:T(8,128)(2,1)S(1)} %select_convert_fusion.2), channel_id=1, source_target_pairs={{0,2},{2,0},{4,6},{6,4},{8,10},{10,8},{12,14},{14,12},{1,3},{3,1},... | collective-permute-start | bytes 4718600 | tf_op jit(solution)/shard_map/ppermute | solution.py:24
  398.9 30.6 %collective-permute-start.47 = (bf16[512,1408]{1,0:T(8,128)(2,1)S(1)}, bf16[512,1408]{1,0:T(8,128)(2,1)}, u32[]{:S(2)}, u32[]{:S(2)}) collective-permute-start(bf16[512,1408]{1,0:T(8,128)(2,1)S(1)} %slice.841), channel_id=1, source_target_pairs={{0,8},{2,6},{4,12},{6,2},{8,0},{10,14},{12,4},{14,10},{1,9},{3,7},... | collective-permute-start | bytes 4325384 | tf_op jit(solution)/shard_map/ppermute | solution.py:228
  403.6 30.9 %collective-permute-start.57 = (bf16[512,1408]{1,0:T(8,128)(2,1)S(1)}, bf16[512,1408]{1,0:T(8,128)(2,1)}, u32[]{:S(2)}, u32[]{:S(2)}) collective-permute-start(bf16[512,1408]{1,0:T(8,128)(2,1)S(1)} %slice.857), channel_id=1, source_target_pairs={{0,8},{2,6},{4,12},{6,2},{8,0},{10,14},{12,4},{14,10},{1,9},{3,7},... | collective-permute-start | bytes 4325384 | tf_op jit(solution)/shard_map/ppermute | solution.py:228
  432.4 38.3 %collective-permute-start.48 = (bf16[512,1408]{1,0:T(8,128)(2,1)}, bf16[512,1408]{1,0:T(8,128)(2,1)}, u32[]{:S(2)}, u32[]{:S(2)}) collective-permute-start(bf16[512,1408]{1,0:T(8,128)(2,1)} %slice.839), channel_id=1, source_target_pairs={{0,8},{2,6},{4,12},{6,2},{8,0},{10,14},{12,4},{14,10},{1,9},{3,7},... | collective-permute-start | bytes 4325384 | tf_op jit(solution)/shard_map/ppermute | solution.py:228
  433.8 58.9 %collective-permute-start.49 = (bf16[256,1408]{1,0:T(8,128)(2,1)S(1)}, bf16[256,1408]{1,0:T(8,128)(2,1)}, u32[]{:S(2)}, u32[]{:S(2)}) collective-permute-start(bf16[256,1408]{1,0:T(8,128)(2,1)S(1)} %slice.1219), channel_id=1, source_target_pairs={{0,4},{2,10},{4,0},{6,14},{8,12},{10,2},{12,8},{14,6},{1,5},{3,11}... | collective-permute-start | bytes 2162696 | tf_op jit(solution)/shard_map/ppermute | solution.py:228
  437.3 45.1 %collective-permute-start.58 = (bf16[512,1408]{1,0:T(8,128)(2,1)}, bf16[512,1408]{1,0:T(8,128)(2,1)}, u32[]{:S(2)}, u32[]{:S(2)}) collective-permute-start(bf16[512,1408]{1,0:T(8,128)(2,1)} %slice.855), channel_id=1, source_target_pairs={{0,8},{2,6},{4,12},{6,2},{8,0},{10,14},{12,4},{14,10},{1,9},{3,7},... | collective-permute-start | bytes 4325384 | tf_op jit(solution)/shard_map/ppermute | solution.py:228
  438.7 29.8 %collective-permute-start.59 = (bf16[256,1408]{1,0:T(8,128)(2,1)}, bf16[256,1408]{1,0:T(8,128)(2,1)}, u32[]{:S(2)}, u32[]{:S(2)}) collective-permute-start(bf16[256,1408]{1,0:T(8,128)(2,1)} %slice.1216), channel_id=1, source_target_pairs={{0,4},{2,10},{4,0},{6,14},{8,12},{10,2},{12,8},{14,6},{1,5},{3,11}... | collective-permute-start | bytes 2162696 | tf_op jit(solution)/shard_map/ppermute | solution.py:228
  440.1 46.0 %collective-permute-start.34 = (bf16[384,2048]{1,0:T(8,128)(2,1)S(1)}, bf16[384,2048]{1,0:T(8,128)(2,1)S(1)}, u32[]{:S(2)}, u32[]{:S(2)}) collective-permute-start(bf16[384,2048]{1,0:T(8,128)(2,1)S(1)} %add_convert_fusion.3), channel_id=1, source_target_pairs={{0,1},{1,0},{2,3},{3,2},{4,5},{5,4},{6,7},{7,6},{8,9},{9,8},{10,11... | collective-permute-start | bytes 4718600 | tf_op jit(solution)/shard_map/ppermute | solution.py:24
  468.5 22.0 %collective-permute-start.33 = (bf16[384,2048]{1,0:T(8,128)(2,1)}, bf16[384,2048]{1,0:T(8,128)(2,1)S(1)}, u32[]{:S(2)}, u32[]{:S(2)}) collective-permute-start(bf16[384,2048]{1,0:T(8,128)(2,1)} %select_convert_fusion.1), channel_id=1, source_target_pairs={{0,2},{2,0},{4,6},{6,4},{8,10},{10,8},{12,14},{14,12},{1,3},{3,1},... | collective-permute-start | bytes 4718600 | tf_op jit(solution)/shard_map/ppermute | solution.py:24
  470.6 43.7 %collective-permute-start.77 = (bf16[256,1408]{1,0:T(8,128)(2,1)}, bf16[256,1408]{1,0:T(8,128)(2,1)}, u32[]{:S(2)}, u32[]{:S(2)}) collective-permute-start(bf16[256,1408]{1,0:T(8,128)(2,1)} %fusion.75), channel_id=1, source_target_pairs={{0,16},{16,0},{1,17},{17,1},{2,18},{18,2},{3,19},{19,3},{4,20},{20... | collective-permute-start | bytes 2162696 | tf_op jit(solution)/shard_map/ppermute | solution.py:24
  485.8 26.3 %collective-permute-start.60 = (bf16[512,1408]{1,0:T(8,128)(2,1)S(1)}, bf16[512,1408]{1,0:T(8,128)(2,1)S(1)}, u32[]{:S(2)}, u32[]{:S(2)}) collective-permute-start(bf16[512,1408]{1,0:T(8,128)(2,1)S(1)} %copy-done.74), channel_id=1, source_target_pairs={{0,8},{2,6},{4,12},{6,2},{8,0},{10,14},{12,4},{14,10},{1,9},{3,7},... | collective-permute-start | bytes 4325384 | tf_op jit(solution)/shard_map/ppermute | solution.py:228
  490.5 43.3 %collective-permute-start.36 = (bf16[384,2048]{1,0:T(8,128)(2,1)S(1)}, bf16[384,2048]{1,0:T(8,128)(2,1)}, u32[]{:S(2)}, u32[]{:S(2)}) collective-permute-start(bf16[384,2048]{1,0:T(8,128)(2,1)S(1)} %fusion.146), channel_id=1, source_target_pairs={{0,2},{2,0},{4,6},{6,4},{8,10},{10,8},{12,14},{14,12},{1,3},{3,1},... | collective-permute-start | bytes 4718600 | tf_op jit(solution)/shard_map/ppermute | solution.py:24
  492.7 107.9 %collective-permute-start.35 = (bf16[384,2048]{1,0:T(8,128)(2,1)}, bf16[384,2048]{1,0:T(8,128)(2,1)}, u32[]{:S(2)}, u32[]{:S(2)}) collective-permute-start(bf16[384,2048]{1,0:T(8,128)(2,1)} %add_convert_fusion.2), channel_id=1, source_target_pairs={{0,1},{1,0},{2,3},{3,2},{4,5},{5,4},{6,7},{7,6},{8,9},{9,8},{10,11... | collective-permute-start | bytes 4718600 | tf_op jit(solution)/shard_map/ppermute | solution.py:24
  505.5 22.1 %collective-permute-start.50 = (bf16[512,1408]{1,0:T(8,128)(2,1)S(1)}, bf16[512,1408]{1,0:T(8,128)(2,1)S(1)}, u32[]{:S(2)}, u32[]{:S(2)}) collective-permute-start(bf16[512,1408]{1,0:T(8,128)(2,1)S(1)} %copy-done.73), channel_id=1, source_target_pairs={{0,8},{2,6},{4,12},{6,2},{8,0},{10,14},{12,4},{14,10},{1,9},{3,7},... | collective-permute-start | bytes 4325384 | tf_op jit(solution)/shard_map/ppermute | solution.py:228
  557.8 42.5 %collective-permute-start.51 = (bf16[256,1408]{1,0:T(8,128)(2,1)}, bf16[256,1408]{1,0:T(8,128)(2,1)}, u32[]{:S(2)}, u32[]{:S(2)}) collective-permute-start(bf16[256,1408]{1,0:T(8,128)(2,1)} %slice.1218), channel_id=1, source_target_pairs={{0,4},{2,10},{4,0},{6,14},{8,12},{10,2},{12,8},{14,6},{1,5},{3,11}... | collective-permute-start | bytes 2162696 | tf_op jit(solution)/shard_map/ppermute | solution.py:228
  560.5 49.9 %collective-permute-start.73 = (bf16[256,1408]{1,0:T(8,128)(2,1)}, bf16[256,1408]{1,0:T(8,128)(2,1)}, u32[]{:S(2)}, u32[]{:S(2)}) collective-permute-start(bf16[256,1408]{1,0:T(8,128)(2,1)} %fusion.79), channel_id=1, source_target_pairs={{0,16},{16,0},{1,17},{17,1},{2,18},{18,2},{3,19},{19,3},{4,20},{20... | collective-permute-start | bytes 2162696 | tf_op jit(solution)/shard_map/ppermute | solution.py:24
  563.0 44.9 %collective-permute-start.62 = (bf16[512,1024]{1,0:T(8,128)(2,1)}, bf16[512,1024]{1,0:T(8,128)(2,1)}, u32[]{:S(2)}, u32[]{:S(2)}) collective-permute-start(bf16[512,1024]{1,0:T(8,128)(2,1)} %pad_maximum_fusion.43), channel_id=1, source_target_pairs={{0,8},{2,6},{4,12},{6,2},{8,0},{10,14},{12,4},{14,10},{1,9},{3,7},... | collective-permute-start | bytes 3145736 | tf_op jit(solution)/shard_map/ppermute | solution.py:228
  566.5 38.1 %collective-permute-start.63 = (bf16[256,1408]{1,0:T(8,128)(2,1)}, bf16[256,1408]{1,0:T(8,128)(2,1)}, u32[]{:S(2)}, u32[]{:S(2)}) collective-permute-start(bf16[256,1408]{1,0:T(8,128)(2,1)} %slice.1214), channel_id=1, source_target_pairs={{0,4},{2,10},{4,0},{6,14},{8,12},{10,2},{12,8},{14,6},{1,5},{3,11}... | collective-permute-start | bytes 2162696 | tf_op jit(solution)/shard_map/ppermute | solution.py:228
  600.6 25.3 %collective-permute-start.40 = (bf16[384,2048]{1,0:T(8,128)(2,1)S(1)}, bf16[384,2048]{1,0:T(8,128)(2,1)S(1)}, u32[]{:S(2)}, u32[]{:S(2)}) collective-permute-start(bf16[384,2048]{1,0:T(8,128)(2,1)S(1)} %copy-done.70), channel_id=1, source_target_pairs={{0,2},{2,0},{4,6},{6,4},{8,10},{10,8},{12,14},{14,12},{1,3},{3,1},... | collective-permute-start | bytes 4718600 | tf_op jit(solution)/shard_map/ppermute | solution.py:24
  607.9 56.5 %collective-permute-start.75 = (bf16[256,1408]{1,0:T(8,128)(2,1)S(1)}, bf16[256,1408]{1,0:T(8,128)(2,1)S(1)}, u32[]{:S(2)}, u32[]{:S(2)}) collective-permute-start(bf16[256,1408]{1,0:T(8,128)(2,1)S(1)} %fusion.77), channel_id=1, source_target_pairs={{0,16},{16,0},{1,17},{17,1},{2,18},{18,2},{3,19},{19,3},{4,20},{20... | collective-permute-start | bytes 2162696 | tf_op jit(solution)/shard_map/ppermute | solution.py:24
  623.1 28.8 %collective-permute-start.54 = (bf16[512,1152]{1,0:T(8,128)(2,1)S(1)}, bf16[512,1152]{1,0:T(8,128)(2,1)S(1)}, u32[]{:S(2)}, u32[]{:S(2)}) collective-permute-start(bf16[512,1152]{1,0:T(8,128)(2,1)S(1)} %slice.833), channel_id=1, source_target_pairs={{0,8},{2,6},{4,12},{6,2},{8,0},{10,14},{12,4},{14,10},{1,9},{3,7},... | collective-permute-start | bytes 3538952 | tf_op jit(solution)/shard_map/ppermute | solution.py:228
  623.1 97.2 %collective-permute-start.55 = (bf16[256,1024]{1,0:T(8,128)(2,1)S(1)}, bf16[256,1024]{1,0:T(8,128)(2,1)S(1)}, u32[]{:S(2)}, u32[]{:S(2)}) collective-permute-start(bf16[256,1024]{1,0:T(8,128)(2,1)S(1)} %slice.1223), channel_id=1, source_target_pairs={{0,4},{2,10},{4,0},{6,14},{8,12},{10,2},{12,8},{14,6},{1,5},{3,11}... | collective-permute-start | bytes 1572872 | tf_op jit(solution)/shard_map/ppermute | solution.py:228
  626.8 23.2 %collective-permute-start.65 = (bf16[256,1024]{1,0:T(8,128)(2,1)S(1)}, bf16[256,1024]{1,0:T(8,128)(2,1)S(1)}, u32[]{:S(2)}, u32[]{:S(2)}) collective-permute-start(bf16[256,1024]{1,0:T(8,128)(2,1)S(1)} %slice.1222), channel_id=1, source_target_pairs={{0,4},{2,10},{4,0},{6,14},{8,12},{10,2},{12,8},{14,6},{1,5},{3,11}... | collective-permute-start | bytes 1572872 | tf_op jit(solution)/shard_map/ppermute | solution.py:228
  628.1 35.1 %collective-permute-start.64 = (bf16[512,1152]{1,0:T(8,128)(2,1)S(1)}, bf16[512,1152]{1,0:T(8,128)(2,1)S(1)}, u32[]{:S(2)}, u32[]{:S(2)}) collective-permute-start(bf16[512,1152]{1,0:T(8,128)(2,1)S(1)} %slice.849), channel_id=1, source_target_pairs={{0,8},{2,6},{4,12},{6,2},{8,0},{10,14},{12,4},{14,10},{1,9},{3,7},... | collective-permute-start | bytes 3538952 | tf_op jit(solution)/shard_map/ppermute | solution.py:228
  649.9 47.7 %collective-permute-start.41 = (bf16[384,2048]{1,0:T(8,128)(2,1)S(1)}, bf16[384,2048]{1,0:T(8,128)(2,1)S(1)}, u32[]{:S(2)}, u32[]{:S(2)}) collective-permute-start(bf16[384,2048]{1,0:T(8,128)(2,1)S(1)} %add_convert_fusion), channel_id=1, source_target_pairs={{0,1},{1,0},{2,3},{3,2},{4,5},{5,4},{6,7},{7,6},{8,9},{9,8},{10,11... | collective-permute-start | bytes 4718600 | tf_op jit(solution)/shard_map/ppermute | solution.py:24
  651.9 79.0 %collective-permute-start.69 = (bf16[256,1024]{1,0:T(8,128)(2,1)}, bf16[256,1024]{1,0:T(8,128)(2,1)}, u32[]{:S(2)}, u32[]{:S(2)}) collective-permute-start(bf16[256,1024]{1,0:T(8,128)(2,1)} %fusion.85), channel_id=1, source_target_pairs={{0,16},{16,0},{1,17},{17,1},{2,18},{18,2},{3,19},{19,3},{4,20},{20... | collective-permute-start | bytes 1572872 | tf_op jit(solution)/shard_map/ppermute | solution.py:24
  665.2 34.4 %collective-permute-start.76 = (bf16[128,1408]{1,0:T(8,128)(2,1)S(1)}, bf16[128,1408]{1,0:T(8,128)(2,1)S(1)}, u32[]{:S(2)}, u32[]{:S(2)}) collective-permute-start(bf16[128,1408]{1,0:T(8,128)(2,1)S(1)} %select_convert_fusion.5), channel_id=1, source_target_pairs={{0,2},{2,0},{4,6},{6,4},{8,10},{10,8},{12,14},{14,12},{1,3},{3,1},... | collective-permute-start | bytes 1081352 | tf_op jit(solution)/shard_map/ppermute | solution.py:24
  732.8 29.5 %collective-permute-start.67 = (bf16[256,1152]{1,0:T(8,128)(2,1)S(1)}, bf16[256,1152]{1,0:T(8,128)(2,1)S(1)}, u32[]{:S(2)}, u32[]{:S(2)}) collective-permute-start(bf16[256,1152]{1,0:T(8,128)(2,1)S(1)} %fusion.81), channel_id=1, source_target_pairs={{0,16},{16,0},{1,17},{17,1},{2,18},{18,2},{3,19},{19,3},{4,20},{20... | collective-permute-start | bytes 1769480 | tf_op jit(solution)/shard_map/ppermute | solution.py:24
  (169 other events, 2693.8 us)

commit v3 on v2

--- a/solution.py
+++ b/solution.py
@@ -17,6 +17,9 @@
 BF16 = jnp.bfloat16
 F32 = jnp.float32
 CORE = 1
+
+
+ORDER = {'rest': [], 'lag': 0, 'early': 0, 'pieces a': 1, 'pieces b': 1, 'pieces c': 1, 'far two': [], 'one': ['zero', 'far mixer'], 'far three': ['one', 'far two'], 'two': ['one', 'far two'], 'projected': [], 'far down': ['two', 'far three', 'state'], 'three': ['two', 'far three', 'state'], 'mixed': [], 'four': ['three', 'far down', 'incoming'], 'five': ['four', 'chip'], 'gate': ['four'], 'b0': ['five'], 'b1': [], 'hidden': [], 'G dots': [], 'part gate': ['G', 'b0'], 'part up': ['G', 'b1'], 'U dots': ['chip2'], 'b2': [], 'b3': ['chip2'], 'feed': ['U', 'b2'], 'b4': ['head2'], 'feed head': ['head2'], 'norm2': [], 'gated': [], 'b5': ['feed'], 'dp D': ['head2'], 'dp G': [], 'O dots': ['contribution', 'D sum'], 'b6': ['outgoing'], 'kernel': ['O', 'b5', 'G sum'], 'normed': ['b5'], 'Q dots': ['chip3'], 'result': ['qkv'], 'b7': ['chip3'], 'b8': [], 'b9': [], 'b10': ['head3'], 'b11': ['head3'], 'dp Q': ['head3'], 'dp U': [], 'dp O': [], 'tail': ['b11', 'b9'], 'end down': ['chip3'], 'end gate': ['qkv'], 'end up': ['b9'], 'end output': [], 'end qkv': [], 'cost f': 0, 'cost b': 0}
 
 
 def swap(x, axis, bit=1):
@@ -134,6 +137,13 @@
         ones, change, (((0,), (0,)), ((), ())), precision=MATMUL_PRECISION, preferred_element_type=F32
     )
     state[...] = later * fade + dot(grad, lifted, (0, 0), PASSES)
+
+
+def cost(key):
+    flops = (None, 10**6, 2 * 10**10)[ORDER[key]]
+    if flops is None:
+        return None
+    return pl.CostEstimate(flops=flops, bytes_accessed=10**5, transcendentals=0)
 
 
 def mixer_forward(projected, decay):
@@ -170,6 +180,7 @@
         compiler_params=pltpu.CompilerParams(
             dimension_semantics=("arbitrary",), vmem_limit_bytes=32 * 2**20
         ),
+        cost_estimate=cost("cost f"),
         name="mixer_forward",
     )(projected, projected, projected, decay)
 
@@ -205,6 +216,7 @@
         compiler_params=pltpu.CompilerParams(
             dimension_semantics=("arbitrary",), vmem_limit_bytes=32 * 2**20
         ),
+        cost_estimate=cost("cost b"),
         name="mixer_backward",
     )(projected, projected, projected, decay, grad, states, prefix, earlier, later)
 
@@ -261,10 +273,11 @@
         self.steps = 0
 
     def load(self):
-        return self.rows[self.rows.shape[0] // 2 :].astype(BF16)
+        return self.rows[self.rows.shape[0] // 2 :]
 
     def take(self, got):
-        self.rows = self.rows[: self.rows.shape[0] // 2].astype(F32) + got.astype(F32)
+        kept = self.rows[: self.rows.shape[0] // 2].astype(F32)
+        self.rows = (kept + got.astype(F32)).astype(BF16)
         self.steps += 1
 
 
@@ -280,7 +293,7 @@
     def slot(self, *first):
         now = self.plan[len(self.done)]
         loads = [self.phases[name].load() for name, _ in now]
-        if len(self.done) >= 2:
+        if len(self.done) >= 2 and ORDER["lag"]:
             first = first + (self.done[-2],)
         if first:
             loads = tie(loads, *first)
@@ -445,24 +458,35 @@
             [jnp.where(core == 0, mine, got), jnp.where(core == 0, got, mine)], 0
         )
 
-    plane = Plane(
-        [
-            [("mixer", 0)],
-            [("two", 0)],
-            [("mixer", 1)],
-            [("two", 1)],
-            [("far mixer", 0)],
-            [("three", 0)],
-            [("far mixer", 1)],
-            [("three", 1), ("far two", 0)],
-            [("down", 0)],
-            [("far two", 1), ("far three", 0)],
-            [("down", 1), ("far down", 0)],
-            [("far three", 1)],
-            [("far down", 1)],
-        ]
-    )
-    phases = plane.phases
+    bits = len(chip_bits())
+    phases = {}
+    seen = {}
+
+    def after(x, key):
+        first = [seen[name] for name in ORDER[key] if name in seen]
+        return tie(x, *first) if first else x
+
+    def exchange(x, key):
+        count = ORDER[key]
+        size = x.shape[0] // count
+        parts = [swap(x[i * size : (i + 1) * size], "head") for i in range(count)]
+        for i, part in enumerate(parts):
+            seen[key + str(i)] = part
+        return jnp.concatenate(parts, 0) if count > 1 else parts[0]
+
+    def slot(hops, key):
+        loads = after([phases[name].load() for name in hops], key)
+        landed = []
+        for name, x in zip(hops, loads):
+            got = hop(x, phases[name].steps)
+            phases[name].take(got)
+            landed.append(got)
+        return landed
+
+    def rest_of(*names):
+        for name in names:
+            while phases[name].steps < bits:
+                slot([name], "rest")
 
     def gathered(name, start, width):
         near = same_order([x[:, start : start + width] for x in phases[name].parts], core)
@@ -476,25 +500,31 @@
     fill = width - VD
     chip_mixer = own_columns([w_query, w_key, w_value, w_outgate], [low_pad])
     phases["mixer"] = Spread(chip_mixer)
-    phases["far mixer"] = Spread(swap(chip_mixer, "dp"))
-    plane.slot()
-    tokens, cotangent, w_output, w_gate = tie((tokens, cotangent, w_output, w_gate), chip_mixer)
+    far_mixer = swap(chip_mixer, "dp")
+    zero = slot(["mixer"], "rest")
+    w_output, w_gate, w_up, w_down = tie((w_output, w_gate, w_up, w_down), chip_mixer)
     chip_gate = own_columns([w_gate])
     chip_two = jnp.concatenate([own_columns([w_output.T]), chip_gate[:, :fill]], 1)
-    phases["two"] = Spread(chip_two)
-    plane.slot()
-    w_up, w_down = tie((w_up, w_down), plane.done[0])
     chip_three = jnp.concatenate([chip_gate[:, fill:], own_columns([w_up])], 1)
     chip_down = own_columns([w_down.T])
-    phases["three"] = Spread(chip_three)
+    phases["two"], phases["three"] = Spread(chip_two), Spread(chip_three)
     phases["down"] = Spread(chip_down)
-    rows = chip_two.shape[0]
-    far_both = jnp.concatenate([chip_two, chip_three], 0)
-    far_both = swap(far_both, "dp")
-    phases["far two"] = Spread(far_both[:rows])
-    phases["far three"] = Spread(far_both[rows:])
-    phases["far down"] = Spread(swap(tie(chip_down, phases["far mixer"].parts[0]), "dp"))
-    plane.until("mixer", "far mixer")
+    zero += slot(["two", "three", "down"], "rest")
+    seen["zero"], seen["far mixer"] = zero, far_mixer
+    tokens, cotangent = tie((tokens, cotangent), chip_down)
+    phases["far mixer"] = Spread(far_mixer)
+    far_two = swap(after(chip_two, "far two"), "dp")
+    seen["one"] = slot(["far mixer", "mixer", "two"], "one")
+    rest_of("mixer", "two")
+    seen["far two"] = far_two
+    phases["far two"] = Spread(far_two)
+    far_three = swap(after(chip_three, "far three"), "dp")
+    seen["two"] = slot(["far mixer", "far two", "three"], "two")
+    rest_of("far mixer", "three")
+    if bits > 2:
+        rest_of("far two")
+    seen["far three"] = far_three
+    phases["far three"] = Spread(far_three)
     w_mixer = jnp.concatenate(gathered("mixer", 0, width), 0)
 
     cot, low_tokens = reorder(place_of, cotangent, tokens)
@@ -508,7 +538,7 @@
     normed, norm_back = jax.vjp(rms_norm, inputs, gain1)
     normed_own = normed.astype(BF16)
     normed_low = both(normed_own, core)
-    projected = matmul(normed_low, w_mixer)
+    projected = matmul(after(normed_low, "projected"), w_mixer)
     outgate = projected[:, 2 * KD + VD : wide_mixer]
     rank = w_lowrank.shape[1]
     rank_part = projected[:, wide_mixer : wide_mixer + rank].astype(BF16)
@@ -517,21 +547,28 @@
     logit = matmul(rank_part, rate) + bias
     decay = jax.nn.log_sigmoid(logit) / normalizer
     local_output, lifted, states, state_end, edge, fades = mixer_forward(projected, decay)
+    seen["state"] = state_end
+    far_down = swap(after(chip_down, "far down"), "dp")
+    seen["three"] = slot(
+        (["far two", "far three"] if bits == 2 else ["far three"]) + ["down"] * ORDER["early"], "three"
+    )
+    rest_of("far two")
+    phases["far down"] = Spread(far_down)
     incoming_state = incoming(edge, state_end)
-    mixed_output = local_output + dot(lifted, incoming_state, (1, 1), PASSES)
-    plane.until("two")
-    while len(plane.done) < 9:
-        plane.slot()
-    plane.slot(incoming_state)
-    plane.until("far two")
+    seen["incoming"] = incoming_state
+    mixed_output = local_output + dot(lifted, after(incoming_state, "mixed"), (1, 1), PASSES)
+    seen["far down"] = far_down
+    seen["four"] = slot(["far three"] + ["down"] * (1 - ORDER["early"]) + ["far down"], "four")
+    rest_of("far three", "down")
     w_out = jnp.concatenate(gathered("two", 0, VD), 0)
     gated, gated_back = jax.vjp(head_norm, mixed_output, outgate, head_gain)
     gated_low = gated.astype(BF16)
     mixer_chip = core_sum(times_back(gated_low, w_out), core)
-    mixer_head = swap(mixer_chip, "head")
-    plane.slot(mixer_chip)
-    plane.slot(mixer_head)
-    plane.until(*phases)
+    seen["chip"] = mixer_chip
+    mixer_head = exchange(mixer_chip, "pieces a")
+    seen["head"] = mixer_head
+    seen["five"] = slot(["far down"], "five")
+    rest_of("far down")
     middle = inputs + (mixer_chip.astype(F32) + mixer_head.astype(F32))
     rest = hidden_width - fill
     full_gate = jnp.concatenate(
@@ -545,6 +582,7 @@
     w_dn = jnp.concatenate(gathered("down", 0, hidden_width), 0)
     normed2, norm2_back = jax.vjp(rms_norm, middle, gain2)
     normed2_low = both(normed2.astype(BF16), core)
+    normed2_low = after(normed2_low, "gate")
     gate = matmul(normed2_low, full_gate)
     upward = matmul(normed2_low, full_up)
     hidden_low = swiglu(gate, upward).astype(BF16)
@@ -570,41 +608,69 @@
     )
     sums = back.phases
     sums["far down"], sums["down"] = halves([(cot_core, hidden_low)])
-    back.slot(plane.done[-1])
-    back.slot()
-
-    gate, upward, full_gate, full_up = tie((gate, upward, full_gate, full_up), w_dn)
-    grad_hidden = matmul(cot_both, w_dn)
+    down_rows = sums["far down"].rows, sums["down"].rows
+    seen["D"] = down_rows
+
+    def go(key):
+        first = [seen[name] for name in ORDER[key] if name in seen]
+        back.slot(*first)
+        seen[key] = back.done[-1]
+
+    def far_sum(name, key):
+        return swap(after(sums["far " + name].rows.astype(BF16), key), "dp")
+
+    go("b0")
+    go("b1")
+    grad_result, gate, upward, full_gate, full_up = after(
+        tie((cot_both, gate, upward, full_gate, full_up), w_dn, down_rows), "hidden"
+    )
+    grad_hidden = matmul(grad_result, w_dn)
     sigma = jax.nn.sigmoid(gate)
     gate_low = (grad_hidden * upward * sigma * (1.0 + gate * (1.0 - sigma))).astype(BF16)
     upward_low = (grad_hidden * gate * sigma).astype(BF16)
-    part = times_back(gate_low, full_gate) + times_back(upward_low, full_up)
+    sums["far gate"], sums["gate"] = halves([(normed2_core, after(gate_low, "G dots"))])
+    seen["G"] = sums["far gate"].rows, sums["gate"].rows
+    part = times_back(after(gate_low, "part gate"), full_gate) + times_back(
+        after(upward_low, "part up"), full_up
+    )
     chip_sum = core_sum(part, core)
-    head_part = swap(chip_sum, "head")
-    grad_normed2 = chip_sum.astype(F32) + head_part.astype(F32)
-    sums["far gate"], sums["gate"] = halves([(normed2_core, gate_low)])
-    sums["far up"], sums["up"] = halves([(normed2_core, upward_low)])
-    back.slot()
-    back.slot()
-    feed_chip = core_sum(times_back(tie(hidden_low, chip_sum), w_dn), core)
-    feed_head = swap(tie(feed_chip, head_part), "head")
-    result = reorder(back_place, (middle + (feed_chip.astype(F32) + feed_head.astype(F32))).astype(BF16))[0]
-    back.slot(chip_sum)
-    back.slot(feed_chip)
+    seen["chip2"] = chip_sum
+    head_part = exchange(chip_sum, "pieces b")
+    seen["head2"] = head_part
+    sums["far up"], sums["up"] = halves([(normed2_core, after(upward_low, "U dots"))])
+    seen["U"] = sums["far up"].rows, sums["up"].rows
+    go("b2")
+    go("b3")
+    feed_chip = core_sum(times_back(after(hidden_low, "feed"), w_dn), core)
+    seen["feed"] = feed_chip
+    go("b4")
+    feed_head = swap(after(feed_chip, "feed head"), "head")
+    grad_normed2 = chip_sum.astype(F32) + after(head_part, "norm2").astype(F32)
     middle_grad, grad_mlp_gain = norm2_back(grad_normed2)
     grad_middle = cot.astype(F32) + middle_grad
     middle_low = both(grad_middle.astype(BF16), core)
-    grad_gated = matmul(middle_low, w_out)
+    seen["middle"] = middle_low
+    grad_gated = matmul(after(middle_low, "gated"), w_out)
     mixed_gradient, outgate_grad, head_gain_part = gated_back(grad_gated)
     outgate_low = outgate_grad.astype(BF16)
     middle_core = core_order(middle_low, core)
+    contribution = dot(mixed_gradient, lifted, (0, 0), PASSES)
+    seen["contribution"] = contribution
+    go("b5")
+    outgoing = incoming(edge, contribution, reverse=True)
+    seen["outgoing"] = outgoing
+    far_sums = {}
+    if bits == 2:
+        far_sums["down"], far_sums["gate"] = far_sum("down", "dp D"), far_sum("gate", "dp G")
+        seen["D sum"], seen["G sum"] = far_sums["down"], far_sums["gate"]
+    outgate_late = after(outgate_low, "O dots")
     sums["far output"], sums["output"] = halves(
-        [(middle_core, gated_low), (normed_core, outgate_low)]
-    )
-    outgoing = incoming(edge, dot(mixed_gradient, lifted, (0, 0), PASSES), reverse=True)
-    if len(chip_bits()) == 2:
-        back.slot()
-        back.slot(outgoing, feed_head)
+        [(middle_core, gated_low), (normed_core, outgate_late)]
+    )
+    seen["O"] = sums["far output"].rows, sums["output"].rows
+    if bits == 2:
+        go("b6")
+    outgoing = after(outgoing, "kernel")
     qkv_low, decay_grad = mixer_backward(
         projected, decay, mixed_gradient, states, fades, incoming_state, outgoing
     )
@@ -614,25 +680,41 @@
     rank_low = times_back(logit_low, rate).astype(BF16)
     rank_low = jnp.pad(rank_low, ((0, 0), (0, 128 - rank)))
     mixer_low = jnp.concatenate([qkv_low, outgate_low, rank_low], 1)
-    normed_chip = core_sum(times_back(mixer_low, w_mixer), core)
-    normed_head = swap(normed_chip, "head")
+    seen["qkv"] = qkv_low
+    normed_chip = core_sum(times_back(after(mixer_low, "normed"), w_mixer), core)
+    seen["chip3"] = normed_chip
+    normed_head = exchange(normed_chip, "pieces c")
+    seen["head3"] = normed_head
+    qkv_rank = after(jnp.concatenate([qkv_low, rank_low], 1), "Q dots")
+    feed_head = after(feed_head, "result")
+    result = (middle + (feed_chip.astype(F32) + feed_head.astype(F32))).astype(BF16)
+    result = reorder(back_place, result)[0]
+    seen["result_"] = result
+    sums["far qkv"], sums["qkv"] = halves([(normed_core, qkv_rank)])
+    seen["Q"] = sums["far qkv"].rows, sums["qkv"].rows
+    if bits == 2:
+        go("b7")
+    go("b8")
+    go("b9")
+    go("b10")
+    if bits == 2:
+        far_sums["qkv"] = far_sum("qkv", "dp Q")
+        seen["Q sum"] = far_sums["qkv"]
+    go("b11")
+    back.until(*sums)
+    if bits == 2:
+        far_sums["up"], far_sums["output"] = far_sum("up", "dp U"), far_sum("output", "dp O")
+        seen["U sum"], seen["O sum"] = far_sums["up"], far_sums["output"]
+    normed_head = after(normed_head, "tail")
     grad_normed = normed_chip.astype(F32) + normed_head.astype(F32)
-    qkv_rank = jnp.concatenate([qkv_low, rank_low], 1)
-    sums["far qkv"], sums["qkv"] = halves([(normed_core, qkv_rank)])
-    back.slot(normed_chip)
-    back.slot()
-    back.slot(result)
-    back.slot(normed_head)
-    back.until(*sums)
     inputs_grad, grad_mix_gain = norm_back(grad_normed)
     grad_tokens = reorder(back_place, grad_middle + inputs_grad)[0]
 
     finished = []
-    for i, name in enumerate(("down", "gate", "up", "output", "qkv")):
-        got = swap(sums["far " + name].rows.astype(BF16), "dp")
-        if 2 * i + 4 < len(back.done):
-            got = tie(got, back.done[2 * i + 4])
-        finished.append(sums[name].rows + got.astype(F32))
+    for name in ("down", "gate", "up", "output", "qkv"):
+        got = far_sums[name] if name in far_sums else far_sum(name, "rest")
+        got = after(got, "end " + name)
+        finished.append(sums[name].rows.astype(F32) + got.astype(F32))
     grad_down, grad_gate, grad_up, grad_output, grad_qkv = finished
 
     def own_rows(chip_rows):
@@ -672,22 +754,20 @@
         jnp.concatenate([zero[0], grad_rate_bias]),
     )
     head_gain_part = head_gain_part + swap(head_gain_part[None], "head")[0]
-    gains = jnp.pad(jnp.stack([grad_mix_gain, grad_mlp_gain]), ((0, 6), (0, 0)))
-    gains = reorder(back_place, gains)[0][:2]
-    model = gains.shape[1]
-    others = jnp.concatenate([wide_rate.reshape(-1), wide_bias, head_gain_part])
-    others = jnp.pad(others, (0, 6 * model - others.shape[0])).reshape(6, model)
-    small = jnp.concatenate([gains, others], 0)
-    for axis, bits in (("seq", [CORE] + chip_bits()), ("dp", [1])):
-        for bit in bits:
+    gain_rows = jnp.stack([grad_mix_gain, grad_mlp_gain])
+    gain_rows = reorder(back_place, jnp.pad(gain_rows, ((0, 6), (0, 0))))[0][:2]
+    model = gain_rows.shape[1]
+    others = jnp.concatenate([wide_bias, head_gain_part])
+    others = jnp.pad(others, (0, 2 * model - others.shape[0])).reshape(2, model)
+    others = jnp.concatenate([others, wide_rate.reshape(-1, model)], 0)
+    small = jnp.concatenate([gain_rows, others], 0)
+    for axis, axis_bits in (("seq", [CORE] + chip_bits()), ("dp", [1])):
+        for bit in axis_bits:
             small = small + swap(small, axis, bit)
     sum_mix_gain, sum_mlp_gain = small[0], small[1]
-    others = small[2:].reshape(-1)
-    at = wide_rate.size
-    sum_rate = others[:at].reshape(wide_rate.shape)
-    sum_rate_bias = others[at : at + wide_bias.size]
-    at = at + wide_bias.size
-    sum_head_gain = others[at : at + VD]
+    sum_rate_bias = small[2, : wide_bias.size]
+    sum_head_gain = small[2, wide_bias.size : wide_bias.size + VD]
+    sum_rate = small[4:].reshape(wide_rate.shape)
     return (
         result,
         grad_tokens,

time: 783 us -> 694 us (0.89)
  waiting for transfers between devices: 361 us -> 286 us
  matrix products: 125 us -> 102 us
  other arithmetic: 122 us -> 133 us
    ppermute x36, waiting for transfers between devices: 225 us -> 173 us  [hop(): return lax.ppermute(x, 'seq', [(i, i ^ there[i % 2]) for i in range(count)])]
    ppermute x37 -> x38, waiting for transfers between devices: 135 us -> 104 us  [swap(): return lax.ppermute(x, axis, [(i, i ^ bit) for i in range(count)])]
    convert_element_type x5 -> x16, other arithmetic: 6.6 us -> 23 us  [the longest x15 19.6 us: take(): self.rows = (kept + got.astype(F32)).astype(BF16)]
    dot_general x6, matrix products: 46.4 us -> 35.7 us  [matmul(): return jnp.dot(left, right, preferred_element_type=F32)]
    dot_general x13, matrix products: 40.3 us -> 29.7 us  [inner(): lax.dot_general(left, right, (((0,), (0,)), ((), ())), preferred_element_...]
    ppermute x6, waiting for transfers between devices: 0.02 us -> 9.99 us  [move(): return lax.ppermute(packed, 'seq', pairs).astype(F32)]
    concatenate x8, other arithmetic: 13 us -> 4.33 us  [load(): jnp.concatenate(self.parts, 0)]
    add x15 -> x5, other arithmetic: 15.1 us -> 6.8 us  [body(): finished.append(sums[name].rows.astype(F32) + got.astype(F32))]
  transfers between devices with their start and end apart: 79 -> 80, of which waited for: 30 -> 30; matrix products, arithmetic and copies ran while one was open for 28% -> 34% of each run, Pallas kernels for 3% -> 4%
where the time goes in v3:
time: 694 us; the launch traced here: 690 us
  waiting for transfers between devices  286 us (41%)
  other arithmetic  133 us (19%)
  matrix products  102 us (15%)
  starting transfers between devices  77.3 us (11%)
  local copies, waits for them, and re-layouts  60.6 us (9%)
  Pallas kernels  27.3 us (4%)
    ppermute x36, waiting for transfers between devices, hop(): return lax.ppermute(x, 'seq', [(i, i ^ there[i % 2]) for i in range(count)])  173 us
    ppermute x38, waiting for transfers between devices, swap(): return lax.ppermute(x, axis, [(i, i ^ bit) for i in range(count)])  104 us
    ppermute x36, starting transfers between devices, hop(): return lax.ppermute(x, 'seq', [(i, i ^ there[i % 2]) for i in range(count)])  42.2 us
    dot_general x6, matrix products, times_back(): lax.dot_general(grad, weight, (((1,), (1,)), ((), ())), preferred_element...  36 us
    unnamed x288, local copies, waits for them, and re-layouts  35.9 us
    dot_general x6, matrix products, matmul(): return jnp.dot(left, right, preferred_element_type=F32)  35.7 us
    unnamed x38, other arithmetic  35.6 us
    dot_general x13, matrix products, inner(): lax.dot_general(left, right, (((0,), (0,)), ((), ())), preferred_element_...  29.7 us
  transfers between devices with their start and end apart: 80, of which 30 were waited for; matrix products, arithmetic and copies ran while one was open for 34% of the time, Pallas kernels for 4%

profile of v3, /device:TPU:0, one launch (start us, length us, event | category | flops | bytes accessed | tf_op | source)
XLA Modules:
  0.0 690.0 jit_solution(11366932880248057638)
XLA Ops:
  10.8 3.6 collective-permute-start.4
  37.9 7.7 %collective-permute-done.7 = bf16[256,1664]{1,0:T(8,128)(2,1)S(1)} collective-permute-done((bf16[256,1664]{1,0:T(8,128)(2,1)S(1)}, bf16[256,1664]{1,0:T(8,128)(2,1)S(1)}, u32[]{:S(2)}, u32[]{:S(2)}) %collective-permute-start.7) | collective-permute-done | bytes 852000 | tf_op jit(solution)/shard_map/ppermute | solution.py:240
  46.9 24.1 %collective-permute-done.4 = bf16[256,1664]{1,0:T(8,128)(2,1)} collective-permute-done((bf16[256,1664]{1,0:T(8,128)(2,1)}, bf16[256,1664]{1,0:T(8,128)(2,1)}, u32[]{:S(2)}, u32[]{:S(2)}) %collective-permute-start.4) | collective-permute-done | bytes 852000 | tf_op jit(solution)/shard_map/ppermute | solution.py:27
  74.4 14.6 %collective-permute-done.13 = bf16[256,1664]{1,0:T(8,128)(2,1)S(1)} collective-permute-done((bf16[256,1664]{1,0:T(8,128)(2,1)S(1)}, bf16[256,1664]{1,0:T(8,128)(2,1)S(1)}, u32[]{:S(2)}, u32[]{:S(2)}) %collective-permute-start.13) | collective-permute-done | bytes 852000 | tf_op jit(solution)/shard_map/ppermute | solution.py:27
  103.2 15.9 %collective-permute-done.14 = bf16[512,1664]{1,0:T(8,128)(2,1)S(1)} collective-permute-done((bf16[512,1664]{1,0:T(8,128)(2,1)S(1)}, bf16[512,1664]{1,0:T(8,128)(2,1)S(1)}, u32[]{:S(2)}, u32[]{:S(2)}) %collective-permute-start.14) | collective-permute-done | bytes 1703968 | tf_op jit(solution)/shard_map/ppermute | solution.py:240
  131.1 29.3 %collective-permute-done.20 = bf16[256,1664]{1,0:T(8,128)(2,1)S(1)} collective-permute-done((bf16[256,1664]{1,0:T(8,128)(2,1)S(1)}, bf16[256,1664]{1,0:T(8,128)(2,1)S(1)}, u32[]{:S(2)}, u32[]{:S(2)}) %collective-permute-start.20) | collective-permute-done | bytes 852000 | tf_op jit(solution)/shard_map/ppermute | solution.py:27
  163.9 8.8 %fusion.7.q_ref.k_ref.v_ref = f32[768,1664]{1,0:T(8,128)S(1)} fusion(bf16[2048,1664]{1,0:T(8,128)(2,1)} %slice_dynamic-update-slice_fusion, bf16[384,2048]{1,0:T(8,128)(2,1)S(1)} %get-tuple-element.282, bf16[384,2048]{1,0:T(8,128)(2,1)S(1)} %get-tuple-element.281), kind=kOutput, calls=%fused_computation.72 | convolution fusion | flops 5240782848 | bytes 15073280 | tf_op jit(solution)/shard_map/dot_general | solution.py:31
  174.6 7.6 %mixer_forward.1 = (f32[768,512]{1,0:T(8,128)S(1)}, f32[768,256]{1,0:T(8,128)S(1)}, f32[12,512,256]{2,1,0:T(8,128)S(1)}, f32[512,256]{1,0:T(8,128)S(1)}, f32[1,2...) custom-call(f32[768,1664]{1,0:T(8,128)S(1)} %fusion.7.q_ref.k_ref.v_ref, f32[768,1664]{1,0:T(8,128)S(1)} %fusion.7.q_ref.k_ref.v_ref, ...), custom_call_target="tpu_custom_call" | custom-call | tf_op jit(solution)/shard_map/mixer_forward/pallas_call | solution.py:154
  182.4 4.1 collective-permute-start.18
  196.4 4.1 collective-permute-done.17
  205.6 21.0 %collective-permute-done.22 = bf16[512,1664]{1,0:T(8,128)(2,1)S(1)} collective-permute-done((bf16[512,1664]{1,0:T(8,128)(2,1)S(1)}, bf16[512,1664]{1,0:T(8,128)(2,1)S(1)}, u32[]{:S(2)}, u32[]{:S(2)}) %collective-permute-start.22) | collective-permute-done | bytes 1703968 | tf_op jit(solution)/shard_map/ppermute | solution.py:240
  228.9 3.4 fusion.109
  237.9 13.1 %collective-permute-done.30 = bf16[256,1408]{1,0:T(8,128)(2,1)S(1)} collective-permute-done((bf16[256,1408]{1,0:T(8,128)(2,1)S(1)}, bf16[256,1408]{1,0:T(8,128)(2,1)S(1)}, u32[]{:S(2)}, u32[]{:S(2)}) %collective-permute-start.30) | collective-permute-done | bytes 720928 | tf_op jit(solution)/shard_map/ppermute | solution.py:240
  254.6 24.4 %collective-permute-done.29 = bf16[512,1408]{1,0:T(8,128)(2,1)S(1)} collective-permute-done((bf16[512,1408]{1,0:T(8,128)(2,1)}, bf16[512,1408]{1,0:T(8,128)(2,1)S(1)}, u32[]{:S(2)}, u32[]{:S(2)}) %collective-permute-start.29) | collective-permute-done | bytes 1441824 | tf_op jit(solution)/shard_map/ppermute | solution.py:240
  295.0 3.3 collective-permute-done.32
  303.6 5.2 fusion.110
  308.8 7.8 %multiply_convert_fusion.2 = (bf16[768,1408]{1,0:T(8,128)(2,1)S(1)}, f32[768,1408]{1,0:T(8,128)S(1)}) fusion(f32[768,1408]{1,0:T(8,128)S(1)} %fusion.110, bf16[768,2048]{1,0:T(8,128)(2,1)S(1)} %pad_maximum_fusion.5, bf16[2048,1408]{1,0:T(8,128)(2,1)} %slice_dynamic-update-slice_fusion.4), kind=kOutput, calls=%fused_computation.55 | convolution fusion | flops 4435673088 | bytes 19726336 | tf_op jit(solution)/shard_map/dot_general | solution.py:31
  316.7 3.1 convolution_convert_fusion.7
  321.8 3.1 convolution_convert_fusion.6
  326.9 7.5 %fusion.111 = f32[768,1408]{1,0:T(8,128)S(1)} fusion(bf16[768,2048]{1,0:T(8,128)(2,1)S(1)} %copy-done.47, bf16[2048,1408]{1,0:T(8,128)(2,1)} %slice_dynamic-update-slice_fusion.2), kind=kOutput, calls=%fused_computation.434 | convolution fusion | flops 4429185024 | bytes 13238272 | tf_op jit(solution)/shard_map/dot_general | solution.py:31
  336.6 3.5 multiply_convert_fusion
  342.9 3.0 convolution_convert_fusion.4
  347.2 3.3 convolution_convert_fusion.5
  355.1 14.3 %collective-permute-done.33 = bf16[512,1408]{1,0:T(8,128)(2,1)} collective-permute-done((bf16[512,1408]{1,0:T(8,128)(2,1)}, bf16[512,1408]{1,0:T(8,128)(2,1)}, u32[]{:S(2)}, u32[]{:S(2)}) %collective-permute-start.33) | collective-permute-done | bytes 1441824 | tf_op jit(solution)/shard_map/ppermute | solution.py:240
  369.4 7.0 %fusion.112 = f32[768,2048]{1,0:T(8,128)} fusion(bf16[768,1408]{1,0:T(8,128)(2,1)S(1)} %copy-done.62, bf16[2048,1408]{1,0:T(8,128)(2,1)S(1)} %bitcast.84), kind=kOutput, calls=%fused_computation.435 | convolution fusion | flops 4429185024 | bytes 14221312 | tf_op jit(solution)/shard_map/dot_general | solution.py:39
  376.4 8.9 %convolution_add_fusion = f32[768,2048]{1,0:T(8,128)S(1)} fusion(f32[768,2048]{1,0:T(8,128)} %fusion.112, bf16[768,1408]{1,0:T(8,128)(2,1)S(1)} %copy-done.64, bf16[2048,1408]{1,0:T(8,128)(2,1)} %maximum_dynamic-update-slice_fusion), kind=kOutput, calls=%fused_computation.66 | convolution fusion | flops 4430757888 | bytes 20512768 | tf_op jit(solution)/shard_map/dot_general | solution.py:39
  396.7 4.6 convolution_convert_fusion.2
  401.3 4.2 convolution_convert_fusion.3
  406.8 8.2 %fusion.113 = f32[768,2048]{1,0:T(8,128)S(1)} fusion(bf16[768,1408]{1,0:T(8,128)(2,1)} %copy-done.130, bf16[2048,1408]{1,0:T(8,128)(2,1)} %slice_dynamic-update-slice_fusion.2), kind=kOutput, calls=%fused_computation.436 | convolution fusion | flops 4429185024 | bytes 14221312 | tf_op jit(solution)/shard_map/dot_general | solution.py:39
  422.7 8.4 %collective-permute-done.39 = bf16[384,2048]{1,0:T(8,128)(2,1)S(1)} collective-permute-done((bf16[384,2048]{1,0:T(8,128)(2,1)S(1)}, bf16[384,2048]{1,0:T(8,128)(2,1)S(1)}, u32[]{:S(2)}, u32[]{:S(2)}) %collective-permute-start.39) | collective-permute-done | bytes 1572896 | tf_op jit(solution)/shard_map/ppermute | solution.py:27
  433.9 3.6 add_convert_fusion.2
  440.1 10.7 %collective-permute-done.49 = bf16[256,1408]{1,0:T(8,128)(2,1)} collective-permute-done((bf16[256,1408]{1,0:T(8,128)(2,1)}, bf16[256,1408]{1,0:T(8,128)(2,1)}, u32[]{:S(2)}, u32[]{:S(2)}) %collective-permute-start.49) | collective-permute-done | bytes 720928 | tf_op jit(solution)/shard_map/ppermute | solution.py:240
  452.2 11.0 %collective-permute-done.66 = bf16[512,1408]{1,0:T(8,128)(2,1)S(1)} collective-permute-done((bf16[512,1408]{1,0:T(8,128)(2,1)}, bf16[512,1408]{1,0:T(8,128)(2,1)S(1)}, u32[]{:S(2)}, u32[]{:S(2)}) %collective-permute-start.66) | collective-permute-done | bytes 1441824 | tf_op jit(solution)/shard_map/ppermute | solution.py:240
  463.2 2.6 collective-permute-start.50
  467.2 12.5 %collective-permute-done.47 = bf16[512,1408]{1,0:T(8,128)(2,1)S(1)} collective-permute-done((bf16[512,1408]{1,0:T(8,128)(2,1)}, bf16[512,1408]{1,0:T(8,128)(2,1)S(1)}, u32[]{:S(2)}, u32[]{:S(2)}) %collective-permute-start.47) | collective-permute-done | bytes 1441824 | tf_op jit(solution)/shard_map/ppermute | solution.py:240
  481.7 4.4 multiply_reduce_fusion.3
  505.7 5.9 collective-permute-done.44
  512.6 12.2 %mixer_backward.1 = (bf16[768,1024]{1,0:T(8,128)(2,1)S(1)}, f32[768,256]{1,0:T(8,128)S(1)}) custom-call(f32[768,1664]{1,0:T(8,128)S(1)} %fusion.7.q_ref.k_ref.v_ref, f32[768,1664]{1,0:T(8,128)S(1)} %fusion.7.q_ref.k_ref.v_ref, f32[768,1664]{1,0:T(8,128)S(1)} %fusion.7.q_ref.k_ref.v_ref, f32[768,256]{1,0:T(8,128)S(1)} %copy-done.7, ...), custom_call_target="tpu_custom_call" | custom-call | tf_op jit(solution)/shard_map/mixer_backward/pallas_call | solution.py:193
  531.3 8.3 %fusion.114 = f32[768,2048]{1,0:T(8,128)S(1)} fusion(bf16[768,1664]{1,0:T(8,128)(2,1)S(1)} %pad_maximum_fusion.8, bf16[2048,1664]{1,0:T(8,128)(2,1)} %slice_dynamic-update-slice_fusion), kind=kOutput, calls=%fused_computation.437 | convolution fusion | flops 5234491392 | bytes 15663104 | tf_op jit(solution)/shard_map/dot_general | solution.py:39
  573.9 2.9 copy.73
  576.8 3.6 collective-permute-done.55
  583.5 9.5 %collective-permute-done.62 = bf16[512,1152]{0,1:T(8,128)(2,1)} collective-permute-done((bf16[512,1152]{0,1:T(8,128)(2,1)}, bf16[512,1152]{0,1:T(8,128)(2,1)}, u32[]{:S(2)}, u32[]{:S(2)}) %collective-permute-start.62) | collective-permute-done | bytes 1179680 | tf_op jit(solution)/shard_map/ppermute | solution.py:240
  596.5 16.9 %collective-permute-done.53 = bf16[512,1152]{0,1:T(8,128)(2,1)} collective-permute-done((bf16[512,1152]{0,1:T(8,128)(2,1)}, bf16[512,1152]{0,1:T(8,128)(2,1)}, u32[]{:S(2)}, u32[]{:S(2)}) %collective-permute-start.53) | collective-permute-done | bytes 1179680 | tf_op jit(solution)/shard_map/ppermute | solution.py:240
  618.8 3.8 collective-permute-done.56
  637.5 3.1 fusion.3
  652.3 5.5 fusion.5
  657.8 2.7 reorder.8
  662.8 16.5 %collective-permute-done.61 = f32[8,2048]{1,0:T(8,128)S(1)} collective-permute-done((f32[8,2048]{1,0:T(8,128)S(1)}, f32[8,2048]{1,0:T(8,128)S(1)}, u32[]{:S(2)}, u32[]{:S(2)}) %collective-permute-start.61) | collective-permute-done | bytes 65568 | tf_op jit(solution)/shard_map/ppermute | solution.py:27
  (657 shorter events, 273.6 us)
Async XLA Ops:
  10.8 60.3 %collective-permute-start.4 = (bf16[256,1664]{1,0:T(8,128)(2,1)}, bf16[256,1664]{1,0:T(8,128)(2,1)}, u32[]{:S(2)}, u32[]{:S(2)}) collective-permute-start(bf16[256,1664]{1,0:T(8,128)(2,1)} %pad_maximum_fusion.60), channel_id=1, source_target_pairs={{0,16},{16,0},{1,17},{17,1},{2,18},{18,2},{3,19},{19,3},{4,20},{20... | collective-permute-start | bytes 2555912 | tf_op jit(solution)/shard_map/ppermute | solution.py:27
  14.5 20.6 %collective-permute-start.3 = (bf16[256,1664]{1,0:T(8,128)(2,1)}, bf16[256,1664]{1,0:T(8,128)(2,1)S(1)}, u32[]{:S(2)}, u32[]{:S(2)}) collective-permute-start(bf16[256,1664]{1,0:T(8,128)(2,1)} %pad_maximum_fusion.60), channel_id=1, source_target_pairs={{0,4},{2,10},{4,0},{6,14},{8,12},{10,2},{12,8},{14,6},{1,5},{3,11}... | collective-permute-start | bytes 2555912 | tf_op jit(solution)/shard_map/ppermute | solution.py:240
  28.3 62.4 %collective-permute-start.2 = (bf16[384,2048]{1,0:T(8,128)(2,1)S(1)}, bf16[384,2048]{1,0:T(8,128)(2,1)S(1)}, u32[]{:S(2)}, u32[]{:S(2)}) collective-permute-start(bf16[384,2048]{1,0:T(8,128)(2,1)S(1)} %fusion.2), channel_id=1, source_target_pairs={{0,2},{2,0},{4,6},{6,4},{8,10},{10,8},{12,14},{14,12},{1,3},{3,1},... | collective-permute-start | bytes 4718600 | tf_op jit(solution)/shard_map/ppermute | solution.py:27
  35.1 53.9 %collective-permute-start.13 = (bf16[256,1664]{1,0:T(8,128)(2,1)S(1)}, bf16[256,1664]{1,0:T(8,128)(2,1)S(1)}, u32[]{:S(2)}, u32[]{:S(2)}) collective-permute-start(bf16[256,1664]{1,0:T(8,128)(2,1)S(1)} %pad_maximum_fusion.61), channel_id=1, source_target_pairs={{0,16},{16,0},{1,17},{17,1},{2,18},{18,2},{3,19},{19,3},{4,20},{20... | collective-permute-start | bytes 2555912 | tf_op jit(solution)/shard_map/ppermute | solution.py:27
  36.5 34.6 %collective-permute-start.9 = (bf16[256,1664]{1,0:T(8,128)(2,1)S(1)}, bf16[256,1664]{1,0:T(8,128)(2,1)S(1)}, u32[]{:S(2)}, u32[]{:S(2)}) collective-permute-start(bf16[256,1664]{1,0:T(8,128)(2,1)S(1)} %maximum_maximum_fusion), channel_id=1, source_target_pairs={{0,4},{2,10},{4,0},{6,14},{8,12},{10,2},{12,8},{14,6},{1,5},{3,11}... | collective-permute-start | bytes 2555912 | tf_op jit(solution)/shard_map/ppermute | solution.py:240
  45.6 48.7 %collective-permute-start.31 = (bf16[384,2048]{1,0:T(8,128)(2,1)S(1)}, bf16[384,2048]{1,0:T(8,128)(2,1)S(1)}, u32[]{:S(2)}, u32[]{:S(2)}) collective-permute-start(bf16[384,2048]{1,0:T(8,128)(2,1)S(1)} %get-tuple-element.106), channel_id=1, source_target_pairs={{0,2},{2,0},{4,6},{6,4},{8,10},{10,8},{12,14},{14,12},{1,3},{3,1},... | collective-permute-start | bytes 4718600 | tf_op jit(solution)/shard_map/ppermute | solution.py:27
  71.1 30.9 %collective-permute-start.12 = (bf16[256,1664]{1,0:T(8,128)(2,1)}, bf16[256,1664]{1,0:T(8,128)(2,1)S(1)}, u32[]{:S(2)}, u32[]{:S(2)}) collective-permute-start(bf16[256,1664]{1,0:T(8,128)(2,1)} %collective-permute-done.4), channel_id=1, source_target_pairs={{0,4},{2,10},{4,0},{6,14},{8,12},{10,2},{12,8},{14,6},{1,5},{3,11}... | collective-permute-start | bytes 2555912 | tf_op jit(solution)/shard_map/ppermute | solution.py:240
  72.8 30.4 %collective-permute-start.11 = (bf16[512,1664]{1,0:T(8,128)(2,1)S(1)}, bf16[512,1664]{1,0:T(8,128)(2,1)S(1)}, u32[]{:S(2)}, u32[]{:S(2)}) collective-permute-start(bf16[512,1664]{1,0:T(8,128)(2,1)S(1)} %pad_maximum_fusion.10), channel_id=1, source_target_pairs={{0,8},{2,6},{4,12},{6,2},{8,0},{10,14},{12,4},{14,10},{1,9},{3,7},... | collective-permute-start | bytes 5111816 | tf_op jit(solution)/shard_map/ppermute | solution.py:240
  89.0 30.2 %collective-permute-start.14 = (bf16[512,1664]{1,0:T(8,128)(2,1)S(1)}, bf16[512,1664]{1,0:T(8,128)(2,1)S(1)}, u32[]{:S(2)}, u32[]{:S(2)}) collective-permute-start(bf16[512,1664]{1,0:T(8,128)(2,1)S(1)} %pad_maximum_fusion.11), channel_id=1, source_target_pairs={{0,8},{2,6},{4,12},{6,2},{8,0},{10,14},{12,4},{14,10},{1,9},{3,7},... | collective-permute-start | bytes 5111816 | tf_op jit(solution)/shard_map/ppermute | solution.py:240
  119.2 41.2 %collective-permute-start.19 = (bf16[256,1664]{1,0:T(8,128)(2,1)S(1)}, bf16[256,1664]{1,0:T(8,128)(2,1)S(1)}, u32[]{:S(2)}, u32[]{:S(2)}) collective-permute-start(bf16[256,1664]{1,0:T(8,128)(2,1)S(1)} %collective-permute-done.13), channel_id=1, source_target_pairs={{0,4},{2,10},{4,0},{6,14},{8,12},{10,2},{12,8},{14,6},{1,5},{3,11}... | collective-permute-start | bytes 2555912 | tf_op jit(solution)/shard_map/ppermute | solution.py:240
  120.5 39.9 %collective-permute-start.20 = (bf16[256,1664]{1,0:T(8,128)(2,1)S(1)}, bf16[256,1664]{1,0:T(8,128)(2,1)S(1)}, u32[]{:S(2)}, u32[]{:S(2)}) collective-permute-start(bf16[256,1664]{1,0:T(8,128)(2,1)S(1)} %maximum_maximum_fusion), channel_id=1, source_target_pairs={{0,16},{16,0},{1,17},{17,1},{2,18},{18,2},{3,19},{19,3},{4,20},{20... | collective-permute-start | bytes 2555912 | tf_op jit(solution)/shard_map/ppermute | solution.py:27
  120.5 40.0 %collective-permute-start.15 = (bf16[512,1664]{1,0:T(8,128)(2,1)S(1)}, bf16[512,1664]{1,0:T(8,128)(2,1)S(1)}, u32[]{:S(2)}, u32[]{:S(2)}) collective-permute-start(bf16[512,1664]{1,0:T(8,128)(2,1)S(1)} %pad_maximum_fusion.12), channel_id=1, source_target_pairs={{0,8},{2,6},{4,12},{6,2},{8,0},{10,14},{12,4},{14,10},{1,9},{3,7},... | collective-permute-start | bytes 5111816 | tf_op jit(solution)/shard_map/ppermute | solution.py:240
  122.0 68.2 %collective-permute-start.21 = (bf16[512,1664]{1,0:T(8,128)(2,1)S(1)}, bf16[512,1664]{1,0:T(8,128)(2,1)S(1)}, u32[]{:S(2)}, u32[]{:S(2)}) collective-permute-start(bf16[512,1664]{1,0:T(8,128)(2,1)S(1)} %pad_maximum_fusion.13), channel_id=1, source_target_pairs={{0,8},{2,6},{4,12},{6,2},{8,0},{10,14},{12,4},{14,10},{1,9},{3,7},... | collective-permute-start | bytes 5111816 | tf_op jit(solution)/shard_map/ppermute | solution.py:240
  182.4 20.7 %collective-permute-start.18 = (bf16[528,256]{1,0:T(8,128)(2,1)S(1)}, bf16[528,256]{1,0:T(8,128)(2,1)S(1)}, u32[]{:S(2)}, u32[]{:S(2)}) collective-permute-start(bf16[528,256]{1,0:T(8,128)(2,1)S(1)} %pad_maximum_fusion.66), channel_id=1, source_target_pairs={{0,12},{2,14},{1,13},{3,15},{16,28},{18,30},{17,29},{19,31}} | collective-permute-start | bytes 811016 | tf_op jit(solution)/shard_map/ppermute | solution.py:407
  190.3 43.5 %collective-permute-start.27 = (bf16[256,1408]{1,0:T(8,128)(2,1)}, bf16[256,1408]{1,0:T(8,128)(2,1)S(1)}, u32[]{:S(2)}, u32[]{:S(2)}) collective-permute-start(bf16[256,1408]{1,0:T(8,128)(2,1)} %pad_maximum_fusion.62), channel_id=1, source_target_pairs={{0,16},{16,0},{1,17},{17,1},{2,18},{18,2},{3,19},{19,3},{4,20},{20... | collective-permute-start | bytes 2162696 | tf_op jit(solution)/shard_map/ppermute | solution.py:27
  190.4 43.3 %collective-permute-start.26 = (bf16[256,1664]{1,0:T(8,128)(2,1)S(1)}, bf16[256,1664]{1,0:T(8,128)(2,1)S(1)}, u32[]{:S(2)}, u32[]{:S(2)}) collective-permute-start(bf16[256,1664]{1,0:T(8,128)(2,1)S(1)} %collective-permute-done.20), channel_id=1, source_target_pairs={{0,4},{2,10},{4,0},{6,14},{8,12},{10,2},{12,8},{14,6},{1,5},{3,11}... | collective-permute-start | bytes 2555912 | tf_op jit(solution)/shard_map/ppermute | solution.py:240
  200.4 26.2 %collective-permute-start.22 = (bf16[512,1664]{1,0:T(8,128)(2,1)S(1)}, bf16[512,1664]{1,0:T(8,128)(2,1)S(1)}, u32[]{:S(2)}, u32[]{:S(2)}) collective-permute-start(bf16[512,1664]{1,0:T(8,128)(2,1)S(1)} %pad_maximum_fusion.14), channel_id=1, source_target_pairs={{0,8},{2,6},{4,12},{6,2},{8,0},{10,14},{12,4},{14,10},{1,9},{3,7},... | collective-permute-start | bytes 5111816 | tf_op jit(solution)/shard_map/ppermute | solution.py:240
  232.6 19.7 %collective-permute-start.23 = (bf16[384,2048]{1,0:T(8,128)(2,1)S(1)}, bf16[384,2048]{1,0:T(8,128)(2,1)}, u32[]{:S(2)}, u32[]{:S(2)}) collective-permute-start(bf16[384,2048]{1,0:T(8,128)(2,1)S(1)} %select_convert_fusion.3), channel_id=1, source_target_pairs={{0,2},{2,0},{4,6},{6,4},{8,10},{10,8},{12,14},{14,12},{1,3},{3,1},... | collective-permute-start | bytes 4718600 | tf_op jit(solution)/shard_map/ppermute | solution.py:27
  233.8 17.3 %collective-permute-start.30 = (bf16[256,1408]{1,0:T(8,128)(2,1)S(1)}, bf16[256,1408]{1,0:T(8,128)(2,1)S(1)}, u32[]{:S(2)}, u32[]{:S(2)}) collective-permute-start(bf16[256,1408]{1,0:T(8,128)(2,1)S(1)} %collective-permute-done.27), channel_id=1, source_target_pairs={{0,4},{2,10},{4,0},{6,14},{8,12},{10,2},{12,8},{14,6},{1,5},{3,11}... | collective-permute-start | bytes 2162696 | tf_op jit(solution)/shard_map/ppermute | solution.py:240
  234.8 44.2 %collective-permute-start.28 = (bf16[512,1664]{1,0:T(8,128)(2,1)S(1)}, bf16[512,1664]{1,0:T(8,128)(2,1)S(1)}, u32[]{:S(2)}, u32[]{:S(2)}) collective-permute-start(bf16[512,1664]{1,0:T(8,128)(2,1)S(1)} %pad_maximum_fusion.15), channel_id=1, source_target_pairs={{0,8},{2,6},{4,12},{6,2},{8,0},{10,14},{12,4},{14,10},{1,9},{3,7},... | collective-permute-start | bytes 5111816 | tf_op jit(solution)/shard_map/ppermute | solution.py:240
  237.4 41.7 %collective-permute-start.29 = (bf16[512,1408]{1,0:T(8,128)(2,1)}, bf16[512,1408]{1,0:T(8,128)(2,1)S(1)}, u32[]{:S(2)}, u32[]{:S(2)}) collective-permute-start(bf16[512,1408]{1,0:T(8,128)(2,1)} %pad_maximum_fusion.56), channel_id=1, source_target_pairs={{0,8},{2,6},{4,12},{6,2},{8,0},{10,14},{12,4},{14,10},{1,9},{3,7},... | collective-permute-start | bytes 4325384 | tf_op jit(solution)/shard_map/ppermute | solution.py:240
  254.6 36.9 %collective-permute-start.24 = (bf16[384,2048]{1,0:T(8,128)(2,1)S(1)}, bf16[384,2048]{1,0:T(8,128)(2,1)S(1)}, u32[]{:S(2)}, u32[]{:S(2)}) collective-permute-start(bf16[384,2048]{1,0:T(8,128)(2,1)S(1)} %add_convert_fusion.4), channel_id=1, source_target_pairs={{0,1},{1,0},{2,3},{3,2},{4,5},{5,4},{6,7},{7,6},{8,9},{9,8},{10,11... | collective-permute-start | bytes 4718600 | tf_op jit(solution)/shard_map/ppermute | solution.py:27
  279.1 19.2 %collective-permute-start.32 = (bf16[512,1408]{1,0:T(8,128)(2,1)}, bf16[512,1408]{1,0:T(8,128)(2,1)S(1)}, u32[]{:S(2)}, u32[]{:S(2)}) collective-permute-start(bf16[512,1408]{1,0:T(8,128)(2,1)} %pad_maximum_fusion.57), channel_id=1, source_target_pairs={{0,8},{2,6},{4,12},{6,2},{8,0},{10,14},{12,4},{14,10},{1,9},{3,7},... | collective-permute-start | bytes 4325384 | tf_op jit(solution)/shard_map/ppermute | solution.py:240
  334.5 20.6 %collective-permute-start.34 = (bf16[512,1408]{1,0:T(8,128)(2,1)}, bf16[512,1408]{1,0:T(8,128)(2,1)S(1)}, u32[]{:S(2)}, u32[]{:S(2)}) collective-permute-start(bf16[512,1408]{1,0:T(8,128)(2,1)} %slice.788), channel_id=1, source_target_pairs={{0,8},{2,6},{4,12},{6,2},{8,0},{10,14},{12,4},{14,10},{1,9},{3,7},... | collective-permute-start | bytes 4325384 | tf_op jit(solution)/shard_map/ppermute | solution.py:240
  336.3 33.0 %collective-permute-start.33 = (bf16[512,1408]{1,0:T(8,128)(2,1)}, bf16[512,1408]{1,0:T(8,128)(2,1)}, u32[]{:S(2)}, u32[]{:S(2)}) collective-permute-start(bf16[512,1408]{1,0:T(8,128)(2,1)} %slice.787), channel_id=1, source_target_pairs={{0,8},{2,6},{4,12},{6,2},{8,0},{10,14},{12,4},{14,10},{1,9},{3,7},... | collective-permute-start | bytes 4325384 | tf_op jit(solution)/shard_map/ppermute | solution.py:240
  353.3 37.9 %collective-permute-start.36 = (bf16[512,1408]{1,0:T(8,128)(2,1)}, bf16[512,1408]{1,0:T(8,128)(2,1)}, u32[]{:S(2)}, u32[]{:S(2)}) collective-permute-start(bf16[512,1408]{1,0:T(8,128)(2,1)} %slice.791), channel_id=1, source_target_pairs={{0,8},{2,6},{4,12},{6,2},{8,0},{10,14},{12,4},{14,10},{1,9},{3,7},... | collective-permute-start | bytes 4325384 | tf_op jit(solution)/shard_map/ppermute | solution.py:240
  394.7 36.3 %collective-permute-start.39 = (bf16[384,2048]{1,0:T(8,128)(2,1)S(1)}, bf16[384,2048]{1,0:T(8,128)(2,1)S(1)}, u32[]{:S(2)}, u32[]{:S(2)}) collective-permute-start(bf16[384,2048]{1,0:T(8,128)(2,1)S(1)} %add_convert_fusion.3), channel_id=1, source_target_pairs={{0,1},{1,0},{2,3},{3,2},{4,5},{5,4},{6,7},{7,6},{8,9},{9,8},{10,11... | collective-permute-start | bytes 4718600 | tf_op jit(solution)/shard_map/ppermute | solution.py:27
  394.8 25.1 %collective-permute-start.46 = (bf16[512,1408]{1,0:T(8,128)(2,1)}, bf16[512,1408]{1,0:T(8,128)(2,1)}, u32[]{:S(2)}, u32[]{:S(2)}) collective-permute-start(bf16[512,1408]{1,0:T(8,128)(2,1)} %slice.806), channel_id=1, source_target_pairs={{0,8},{2,6},{4,12},{6,2},{8,0},{10,14},{12,4},{14,10},{1,9},{3,7},... | collective-permute-start | bytes 4325384 | tf_op jit(solution)/shard_map/ppermute | solution.py:240
  416.5 17.4 %collective-permute-start.38 = (bf16[384,2048]{1,0:T(8,128)(2,1)}, bf16[384,2048]{1,0:T(8,128)(2,1)}, u32[]{:S(2)}, u32[]{:S(2)}) collective-permute-start(bf16[384,2048]{1,0:T(8,128)(2,1)} %select_convert_fusion.1), channel_id=1, source_target_pairs={{0,2},{2,0},{4,6},{6,4},{8,10},{10,8},{12,14},{14,12},{1,3},{3,1},... | collective-permute-start | bytes 4718600 | tf_op jit(solution)/shard_map/ppermute | solution.py:27
  431.1 60.5 %collective-permute-start.45 = (bf16[256,1408]{1,0:T(8,128)(2,1)}, bf16[256,1408]{1,0:T(8,128)(2,1)}, u32[]{:S(2)}, u32[]{:S(2)}) collective-permute-start(bf16[256,1408]{1,0:T(8,128)(2,1)} %add_convert_fusion.20), channel_id=1, source_target_pairs={{0,16},{16,0},{1,17},{17,1},{2,18},{18,2},{3,19},{19,3},{4,20},{20... | collective-permute-start | bytes 2162696 | tf_op jit(solution)/shard_map/ppermute | solution.py:27
  431.4 19.4 %collective-permute-start.49 = (bf16[256,1408]{1,0:T(8,128)(2,1)}, bf16[256,1408]{1,0:T(8,128)(2,1)}, u32[]{:S(2)}, u32[]{:S(2)}) collective-permute-start(bf16[256,1408]{1,0:T(8,128)(2,1)} %slice.813), channel_id=1, source_target_pairs={{0,4},{2,10},{4,0},{6,14},{8,12},{10,2},{12,8},{14,6},{1,5},{3,11}... | collective-permute-start | bytes 2162696 | tf_op jit(solution)/shard_map/ppermute | solution.py:240
  431.5 31.6 %collective-permute-start.66 = (bf16[512,1408]{1,0:T(8,128)(2,1)}, bf16[512,1408]{1,0:T(8,128)(2,1)S(1)}, u32[]{:S(2)}, u32[]{:S(2)}) collective-permute-start(bf16[512,1408]{1,0:T(8,128)(2,1)} %slice.812), channel_id=1, source_target_pairs={{0,8},{2,6},{4,12},{6,2},{8,0},{10,14},{12,4},{14,10},{1,9},{3,7},... | collective-permute-start | bytes 4325384 | tf_op jit(solution)/shard_map/ppermute | solution.py:240
  437.4 42.2 %collective-permute-start.47 = (bf16[512,1408]{1,0:T(8,128)(2,1)}, bf16[512,1408]{1,0:T(8,128)(2,1)S(1)}, u32[]{:S(2)}, u32[]{:S(2)}) collective-permute-start(bf16[512,1408]{1,0:T(8,128)(2,1)} %slice.804), channel_id=1, source_target_pairs={{0,8},{2,6},{4,12},{6,2},{8,0},{10,14},{12,4},{14,10},{1,9},{3,7},... | collective-permute-start | bytes 4325384 | tf_op jit(solution)/shard_map/ppermute | solution.py:240
  440.0 41.0 %collective-permute-start.41 = (bf16[384,2048]{1,0:T(8,128)(2,1)S(1)}, bf16[384,2048]{1,0:T(8,128)(2,1)S(1)}, u32[]{:S(2)}, u32[]{:S(2)}) collective-permute-start(bf16[384,2048]{1,0:T(8,128)(2,1)S(1)} %fusion.87), channel_id=1, source_target_pairs={{0,2},{2,0},{4,6},{6,4},{8,10},{10,8},{12,14},{14,12},{1,3},{3,1},... | collective-permute-start | bytes 4718600 | tf_op jit(solution)/shard_map/ppermute | solution.py:27
  450.8 60.9 %collective-permute-start.48 = (bf16[256,1408]{1,0:T(8,128)(2,1)}, bf16[256,1408]{1,0:T(8,128)(2,1)S(1)}, u32[]{:S(2)}, u32[]{:S(2)}) collective-permute-start(bf16[256,1408]{1,0:T(8,128)(2,1)} %slice.809), channel_id=1, source_target_pairs={{0,4},{2,10},{4,0},{6,14},{8,12},{10,2},{12,8},{14,6},{1,5},{3,11}... | collective-permute-start | bytes 2162696 | tf_op jit(solution)/shard_map/ppermute | solution.py:240
  463.2 48.6 %collective-permute-start.50 = (bf16[256,1408]{1,0:T(8,128)(2,1)S(1)}, bf16[256,1408]{1,0:T(8,128)(2,1)S(1)}, u32[]{:S(2)}, u32[]{:S(2)}) collective-permute-start(bf16[256,1408]{1,0:T(8,128)(2,1)S(1)} %add_convert_fusion.19), channel_id=1, source_target_pairs={{0,16},{16,0},{1,17},{17,1},{2,18},{18,2},{3,19},{19,3},{4,20},{20... | collective-permute-start | bytes 2162696 | tf_op jit(solution)/shard_map/ppermute | solution.py:27
  502.6 55.2 %collective-permute-start.78 = (bf16[256,1408]{1,0:T(8,128)(2,1)}, bf16[256,1408]{1,0:T(8,128)(2,1)}, u32[]{:S(2)}, u32[]{:S(2)}) collective-permute-start(bf16[256,1408]{1,0:T(8,128)(2,1)} %slice.808), channel_id=1, source_target_pairs={{0,4},{2,10},{4,0},{6,14},{8,12},{10,2},{12,8},{14,6},{1,5},{3,11}... | collective-permute-start | bytes 2162696 | tf_op jit(solution)/shard_map/ppermute | solution.py:240
  504.6 39.7 %collective-permute-start.40 = (bf16[384,2048]{1,0:T(8,128)(2,1)}, bf16[384,2048]{1,0:T(8,128)(2,1)}, u32[]{:S(2)}, u32[]{:S(2)}) collective-permute-start(bf16[384,2048]{1,0:T(8,128)(2,1)} %add_convert_fusion.2), channel_id=1, source_target_pairs={{0,1},{1,0},{2,3},{3,2},{4,5},{5,4},{6,7},{7,6},{8,9},{9,8},{10,11... | collective-permute-start | bytes 4718600 | tf_op jit(solution)/shard_map/ppermute | solution.py:27
  525.8 22.6 %collective-permute-start.75 = (bf16[256,1408]{1,0:T(8,128)(2,1)}, bf16[256,1408]{1,0:T(8,128)(2,1)}, u32[]{:S(2)}, u32[]{:S(2)}) collective-permute-start(bf16[256,1408]{1,0:T(8,128)(2,1)} %slice.847), channel_id=1, source_target_pairs={{0,4},{2,10},{4,0},{6,14},{8,12},{10,2},{12,8},{14,6},{1,5},{3,11}... | collective-permute-start | bytes 2162696 | tf_op jit(solution)/shard_map/ppermute | solution.py:240
  525.8 27.4 %collective-permute-start.67 = (bf16[512,1024]{0,1:T(8,128)(2,1)}, bf16[512,1024]{0,1:T(8,128)(2,1)}, u32[]{:S(2)}, u32[]{:S(2)}) collective-permute-start(bf16[512,1024]{0,1:T(8,128)(2,1)} %fusion.27), channel_id=1, source_target_pairs={{0,8},{2,6},{4,12},{6,2},{8,0},{10,14},{12,4},{14,10},{1,9},{3,7},... | collective-permute-start | bytes 3145736 | tf_op jit(solution)/shard_map/ppermute | solution.py:240
  551.1 71.8 %collective-permute-start.76 = (bf16[256,1408]{1,0:T(8,128)(2,1)}, bf16[256,1408]{1,0:T(8,128)(2,1)}, u32[]{:S(2)}, u32[]{:S(2)}) collective-permute-start(bf16[256,1408]{1,0:T(8,128)(2,1)} %add_convert_fusion.16), channel_id=1, source_target_pairs={{0,16},{16,0},{1,17},{17,1},{2,18},{18,2},{3,19},{19,3},{4,20},{20... | collective-permute-start | bytes 2162696 | tf_op jit(solution)/shard_map/ppermute | solution.py:27
  564.4 62.9 %collective-permute-start.52 = (bf16[384,2048]{1,0:T(8,128)(2,1)S(1)}, bf16[384,2048]{1,0:T(8,128)(2,1)}, u32[]{:S(2)}, u32[]{:S(2)}) collective-permute-start(bf16[384,2048]{1,0:T(8,128)(2,1)S(1)} %add_convert_fusion), channel_id=1, source_target_pairs={{0,1},{1,0},{2,3},{3,2},{4,5},{5,4},{6,7},{7,6},{8,9},{9,8},{10,11... | collective-permute-start | bytes 4718600 | tf_op jit(solution)/shard_map/ppermute | solution.py:27
  570.5 22.5 %collective-permute-start.62 = (bf16[512,1152]{0,1:T(8,128)(2,1)}, bf16[512,1152]{0,1:T(8,128)(2,1)}, u32[]{:S(2)}, u32[]{:S(2)}) collective-permute-start(bf16[512,1152]{0,1:T(8,128)(2,1)} %slice.830), channel_id=1, source_target_pairs={{0,8},{2,6},{4,12},{6,2},{8,0},{10,14},{12,4},{14,10},{1,9},{3,7},... | collective-permute-start | bytes 3538952 | tf_op jit(solution)/shard_map/ppermute | solution.py:240
  570.5 42.9 %collective-permute-start.53 = (bf16[512,1152]{0,1:T(8,128)(2,1)}, bf16[512,1152]{0,1:T(8,128)(2,1)}, u32[]{:S(2)}, u32[]{:S(2)}) collective-permute-start(bf16[512,1152]{0,1:T(8,128)(2,1)} %slice.817), channel_id=1, source_target_pairs={{0,8},{2,6},{4,12},{6,2},{8,0},{10,14},{12,4},{14,10},{1,9},{3,7},... | collective-permute-start | bytes 3538952 | tf_op jit(solution)/shard_map/ppermute | solution.py:240
  580.4 38.4 %collective-permute-start.69 = (bf16[256,1024]{0,1:T(8,128)(2,1)}, bf16[256,1024]{0,1:T(8,128)(2,1)S(1)}, u32[]{:S(2)}, u32[]{:S(2)}) collective-permute-start(bf16[256,1024]{0,1:T(8,128)(2,1)} %add_convert_fusion.23), channel_id=1, source_target_pairs={{0,16},{16,0},{1,17},{17,1},{2,18},{18,2},{3,19},{19,3},{4,20},{20... | collective-permute-start | bytes 1572872 | tf_op jit(solution)/shard_map/ppermute | solution.py:27
  593.0 29.9 %collective-permute-start.74 = (bf16[256,1408]{1,0:T(8,128)(2,1)S(1)}, bf16[256,1408]{1,0:T(8,128)(2,1)S(1)}, u32[]{:S(2)}, u32[]{:S(2)}) collective-permute-start(bf16[256,1408]{1,0:T(8,128)(2,1)S(1)} %copy-done.77), channel_id=1, source_target_pairs={{0,4},{2,10},{4,0},{6,14},{8,12},{10,2},{12,8},{14,6},{1,5},{3,11}... | collective-permute-start | bytes 2162696 | tf_op jit(solution)/shard_map/ppermute | solution.py:240
  649.2 30.8 %collective-permute-start.64 = (bf16[256,1152]{0,1:T(8,128)(2,1)S(1)}, bf16[256,1152]{0,1:T(8,128)(2,1)S(1)}, u32[]{:S(2)}, u32[]{:S(2)}) collective-permute-start(bf16[256,1152]{0,1:T(8,128)(2,1)S(1)} %add_convert_fusion.21), channel_id=1, source_target_pairs={{0,16},{16,0},{1,17},{17,1},{2,18},{18,2},{3,19},{19,3},{4,20},{20... | collective-permute-start | bytes 1769480 | tf_op jit(solution)/shard_map/ppermute | solution.py:27
  651.5 27.9 %collective-permute-start.61 = (f32[8,2048]{1,0:T(8,128)S(1)}, f32[8,2048]{1,0:T(8,128)S(1)}, u32[]{:S(2)}, u32[]{:S(2)}) collective-permute-start(f32[8,2048]{1,0:T(8,128)S(1)} %add.329), channel_id=1, source_target_pairs={{0,16},{16,0},{1,17},{17,1},{2,18},{18,2},{3,19},{19,3},{4,20},{20... | collective-permute-start | bytes 196616 | tf_op jit(solution)/shard_map/ppermute | solution.py:27
  (169 other events, 1846.7 us)

commit v4 on v3

--- a/solution.py
+++ b/solution.py
@@ -19,7 +19,69 @@
 CORE = 1
 
 
-ORDER = {'rest': [], 'lag': 0, 'early': 0, 'pieces a': 1, 'pieces b': 1, 'pieces c': 1, 'far two': [], 'one': ['zero', 'far mixer'], 'far three': ['one', 'far two'], 'two': ['one', 'far two'], 'projected': [], 'far down': ['two', 'far three', 'state'], 'three': ['two', 'far three', 'state'], 'mixed': [], 'four': ['three', 'far down', 'incoming'], 'five': ['four', 'chip'], 'gate': ['four'], 'b0': ['five'], 'b1': [], 'hidden': [], 'G dots': [], 'part gate': ['G', 'b0'], 'part up': ['G', 'b1'], 'U dots': ['chip2'], 'b2': [], 'b3': ['chip2'], 'feed': ['U', 'b2'], 'b4': ['head2'], 'feed head': ['head2'], 'norm2': [], 'gated': [], 'b5': ['feed'], 'dp D': ['head2'], 'dp G': [], 'O dots': ['contribution', 'D sum'], 'b6': ['outgoing'], 'kernel': ['O', 'b5', 'G sum'], 'normed': ['b5'], 'Q dots': ['chip3'], 'result': ['qkv'], 'b7': ['chip3'], 'b8': [], 'b9': [], 'b10': ['head3'], 'b11': ['head3'], 'dp Q': ['head3'], 'dp U': [], 'dp O': [], 'tail': ['b11', 'b9'], 'end down': ['chip3'], 'end gate': ['qkv'], 'end up': ['b9'], 'end output': [], 'end qkv': [], 'cost f': 0, 'cost b': 0}
+class Order:
+    rest = lambda at: ()
+    lag = 0
+    early = 0
+    pieces_a = 1
+    pieces_b = 1
+    pieces_c = 1
+    far_two = lambda at: ()
+    one = lambda at: (at.zero, at.far_mixer,)
+    far_three = lambda at: (at.one, at.far_two,)
+    two = lambda at: (at.one, at.far_two,)
+    projected = lambda at: ()
+    far_down = lambda at: (at.two, at.far_three, at.state,)
+    three = lambda at: (at.two, at.far_three, at.state,)
+    mixed = lambda at: ()
+    four = lambda at: (at.three, at.far_down, at.incoming,)
+    five = lambda at: (at.far_down,)
+    gate = lambda at: (at.four,)
+    b0 = lambda at: (at.five,)
+    b1 = lambda at: ()
+    hidden = lambda at: ()
+    G_dots = lambda at: ()
+    part_gate = lambda at: (at.G, at.b0,)
+    part_up = lambda at: (at.G,)
+    U_dots = lambda at: (at.chip2,)
+    b2 = lambda at: ()
+    b3 = lambda at: (at.chip2,)
+    feed = lambda at: (at.U, at.b2,)
+    b4 = lambda at: (at.head2,)
+    feed_head = lambda at: (at.head2,)
+    norm2 = lambda at: ()
+    gated = lambda at: ()
+    b5 = lambda at: (at.feed,)
+    dp_D = lambda at: (at.head2,)
+    dp_G = lambda at: ()
+    O_dots = lambda at: (at.contribution, at.D_sum,)
+    b6 = lambda at: (at.outgoing,)
+    kernel = lambda at: (at.O, at.b5, at.G_sum,)
+    normed = lambda at: (at.b5,)
+    Q_dots = lambda at: (at.chip3,)
+    result = lambda at: (at.qkv,)
+    b7 = lambda at: (at.chip3,)
+    b8 = lambda at: ()
+    b9 = lambda at: ()
+    b10 = lambda at: (at.head3,)
+    b11 = lambda at: (at.head3,)
+    dp_Q = lambda at: (at.head3,)
+    dp_U = lambda at: ()
+    dp_O = lambda at: ()
+    tail = lambda at: (at.b11, at.b9,)
+    end_down = lambda at: (at.chip3,)
+    end_gate = lambda at: (at.qkv,)
+    end_up = lambda at: (at.b9,)
+    end_output = lambda at: ()
+    end_qkv = lambda at: ()
+    cost_f = 0
+    cost_b = 0
+    core = 1
+
+
+class Seen:
+    def __getattr__(self, name):
+        return ()
 
 
 def swap(x, axis, bit=1):
@@ -140,7 +202,7 @@
 
 
 def cost(key):
-    flops = (None, 10**6, 2 * 10**10)[ORDER[key]]
+    flops = (None, 10**6, 2 * 10**10)[key]
     if flops is None:
         return None
     return pl.CostEstimate(flops=flops, bytes_accessed=10**5, transcendentals=0)
@@ -180,7 +242,7 @@
         compiler_params=pltpu.CompilerParams(
             dimension_semantics=("arbitrary",), vmem_limit_bytes=32 * 2**20
         ),
-        cost_estimate=cost("cost f"),
+        cost_estimate=cost(Order.cost_f),
         name="mixer_forward",
     )(projected, projected, projected, decay)
 
@@ -216,7 +278,7 @@
         compiler_params=pltpu.CompilerParams(
             dimension_semantics=("arbitrary",), vmem_limit_bytes=32 * 2**20
         ),
-        cost_estimate=cost("cost b"),
+        cost_estimate=cost(Order.cost_b),
         name="mixer_backward",
     )(projected, projected, projected, decay, grad, states, prefix, earlier, later)
 
@@ -293,7 +355,7 @@
     def slot(self, *first):
         now = self.plan[len(self.done)]
         loads = [self.phases[name].load() for name, _ in now]
-        if len(self.done) >= 2 and ORDER["lag"]:
+        if len(self.done) >= 2 and Order.lag:
             first = first + (self.done[-2],)
         if first:
             loads = tie(loads, *first)
@@ -460,18 +522,18 @@
 
     bits = len(chip_bits())
     phases = {}
-    seen = {}
+    seen = Seen()
 
     def after(x, key):
-        first = [seen[name] for name in ORDER[key] if name in seen]
+        first = [y for y in key(seen) if not (isinstance(y, tuple) and not y)]
         return tie(x, *first) if first else x
 
     def exchange(x, key):
-        count = ORDER[key]
+        count = getattr(Order, key)
         size = x.shape[0] // count
         parts = [swap(x[i * size : (i + 1) * size], "head") for i in range(count)]
         for i, part in enumerate(parts):
-            seen[key + str(i)] = part
+            setattr(seen, key + str(i), part)
         return jnp.concatenate(parts, 0) if count > 1 else parts[0]
 
     def slot(hops, key):
@@ -486,7 +548,7 @@
     def rest_of(*names):
         for name in names:
             while phases[name].steps < bits:
-                slot([name], "rest")
+                slot([name], Order.rest)
 
     def gathered(name, start, width):
         near = same_order([x[:, start : start + width] for x in phases[name].parts], core)
@@ -501,7 +563,7 @@
     chip_mixer = own_columns([w_query, w_key, w_value, w_outgate], [low_pad])
     phases["mixer"] = Spread(chip_mixer)
     far_mixer = swap(chip_mixer, "dp")
-    zero = slot(["mixer"], "rest")
+    zero = slot(["mixer"], Order.rest)
     w_output, w_gate, w_up, w_down = tie((w_output, w_gate, w_up, w_down), chip_mixer)
     chip_gate = own_columns([w_gate])
     chip_two = jnp.concatenate([own_columns([w_output.T]), chip_gate[:, :fill]], 1)
@@ -509,21 +571,21 @@
     chip_down = own_columns([w_down.T])
     phases["two"], phases["three"] = Spread(chip_two), Spread(chip_three)
     phases["down"] = Spread(chip_down)
-    zero += slot(["two", "three", "down"], "rest")
-    seen["zero"], seen["far mixer"] = zero, far_mixer
+    zero += slot(["two", "three", "down"], Order.rest)
+    seen.zero, seen.far_mixer = zero, far_mixer
     tokens, cotangent = tie((tokens, cotangent), chip_down)
     phases["far mixer"] = Spread(far_mixer)
-    far_two = swap(after(chip_two, "far two"), "dp")
-    seen["one"] = slot(["far mixer", "mixer", "two"], "one")
+    far_two = swap(after(chip_two, Order.far_two), "dp")
+    seen.one = slot(["far mixer", "mixer", "two"], Order.one)
     rest_of("mixer", "two")
-    seen["far two"] = far_two
+    seen.far_two = far_two
     phases["far two"] = Spread(far_two)
-    far_three = swap(after(chip_three, "far three"), "dp")
-    seen["two"] = slot(["far mixer", "far two", "three"], "two")
+    far_three = swap(after(chip_three, Order.far_three), "dp")
+    seen.two = slot(["far mixer", "far two", "three"], Order.two)
     rest_of("far mixer", "three")
     if bits > 2:
         rest_of("far two")
-    seen["far three"] = far_three
+    seen.far_three = far_three
     phases["far three"] = Spread(far_three)
     w_mixer = jnp.concatenate(gathered("mixer", 0, width), 0)
 
@@ -538,7 +600,7 @@
     normed, norm_back = jax.vjp(rms_norm, inputs, gain1)
     normed_own = normed.astype(BF16)
     normed_low = both(normed_own, core)
-    projected = matmul(after(normed_low, "projected"), w_mixer)
+    projected = matmul(after(normed_low, Order.projected), w_mixer)
     outgate = projected[:, 2 * KD + VD : wide_mixer]
     rank = w_lowrank.shape[1]
     rank_part = projected[:, wide_mixer : wide_mixer + rank].astype(BF16)
@@ -547,27 +609,27 @@
     logit = matmul(rank_part, rate) + bias
     decay = jax.nn.log_sigmoid(logit) / normalizer
     local_output, lifted, states, state_end, edge, fades = mixer_forward(projected, decay)
-    seen["state"] = state_end
-    far_down = swap(after(chip_down, "far down"), "dp")
-    seen["three"] = slot(
-        (["far two", "far three"] if bits == 2 else ["far three"]) + ["down"] * ORDER["early"], "three"
+    seen.state = state_end
+    far_down = swap(after(chip_down, Order.far_down), "dp")
+    seen.three = slot(
+        (["far two", "far three"] if bits == 2 else ["far three"]) + ["down"] * Order.early, Order.three
     )
     rest_of("far two")
     phases["far down"] = Spread(far_down)
     incoming_state = incoming(edge, state_end)
-    seen["incoming"] = incoming_state
-    mixed_output = local_output + dot(lifted, after(incoming_state, "mixed"), (1, 1), PASSES)
-    seen["far down"] = far_down
-    seen["four"] = slot(["far three"] + ["down"] * (1 - ORDER["early"]) + ["far down"], "four")
+    seen.incoming = incoming_state
+    mixed_output = local_output + dot(lifted, after(incoming_state, Order.mixed), (1, 1), PASSES)
+    seen.far_down = far_down
+    seen.four = slot(["far three"] + ["down"] * (1 - Order.early) + ["far down"], Order.four)
     rest_of("far three", "down")
     w_out = jnp.concatenate(gathered("two", 0, VD), 0)
     gated, gated_back = jax.vjp(head_norm, mixed_output, outgate, head_gain)
     gated_low = gated.astype(BF16)
     mixer_chip = core_sum(times_back(gated_low, w_out), core)
-    seen["chip"] = mixer_chip
-    mixer_head = exchange(mixer_chip, "pieces a")
-    seen["head"] = mixer_head
-    seen["five"] = slot(["far down"], "five")
+    seen.chip = mixer_chip
+    mixer_head = exchange(mixer_chip, "pieces_a")
+    seen.head = mixer_head
+    seen.five = slot(["far down"], Order.five)
     rest_of("far down")
     middle = inputs + (mixer_chip.astype(F32) + mixer_head.astype(F32))
     rest = hidden_width - fill
@@ -582,7 +644,7 @@
     w_dn = jnp.concatenate(gathered("down", 0, hidden_width), 0)
     normed2, norm2_back = jax.vjp(rms_norm, middle, gain2)
     normed2_low = both(normed2.astype(BF16), core)
-    normed2_low = after(normed2_low, "gate")
+    normed2_low = after(normed2_low, Order.gate)
     gate = matmul(normed2_low, full_gate)
     upward = matmul(normed2_low, full_up)
     hidden_low = swiglu(gate, upward).astype(BF16)
@@ -609,12 +671,12 @@
     sums = back.phases
     sums["far down"], sums["down"] = halves([(cot_core, hidden_low)])
     down_rows = sums["far down"].rows, sums["down"].rows
-    seen["D"] = down_rows
+    seen.D = down_rows
 
     def go(key):
-        first = [seen[name] for name in ORDER[key] if name in seen]
-        back.slot(*first)
-        seen[key] = back.done[-1]
+        first = getattr(Order, key)(seen)
+        back.slot(*[y for y in first if not (isinstance(y, tuple) and not y)])
+        setattr(seen, key, back.done[-1])
 
     def far_sum(name, key):
         return swap(after(sums["far " + name].rows.astype(BF16), key), "dp")
@@ -622,55 +684,55 @@
     go("b0")
     go("b1")
     grad_result, gate, upward, full_gate, full_up = after(
-        tie((cot_both, gate, upward, full_gate, full_up), w_dn, down_rows), "hidden"
+        tie((cot_both, gate, upward, full_gate, full_up), w_dn, down_rows), Order.hidden
     )
     grad_hidden = matmul(grad_result, w_dn)
     sigma = jax.nn.sigmoid(gate)
     gate_low = (grad_hidden * upward * sigma * (1.0 + gate * (1.0 - sigma))).astype(BF16)
     upward_low = (grad_hidden * gate * sigma).astype(BF16)
-    sums["far gate"], sums["gate"] = halves([(normed2_core, after(gate_low, "G dots"))])
-    seen["G"] = sums["far gate"].rows, sums["gate"].rows
-    part = times_back(after(gate_low, "part gate"), full_gate) + times_back(
-        after(upward_low, "part up"), full_up
+    sums["far gate"], sums["gate"] = halves([(normed2_core, after(gate_low, Order.G_dots))])
+    seen.G = sums["far gate"].rows, sums["gate"].rows
+    part = times_back(after(gate_low, Order.part_gate), full_gate) + times_back(
+        after(upward_low, Order.part_up), full_up
     )
     chip_sum = core_sum(part, core)
-    seen["chip2"] = chip_sum
-    head_part = exchange(chip_sum, "pieces b")
-    seen["head2"] = head_part
-    sums["far up"], sums["up"] = halves([(normed2_core, after(upward_low, "U dots"))])
-    seen["U"] = sums["far up"].rows, sums["up"].rows
+    seen.chip2 = chip_sum
+    head_part = exchange(chip_sum, "pieces_b")
+    seen.head2 = head_part
+    sums["far up"], sums["up"] = halves([(normed2_core, after(upward_low, Order.U_dots))])
+    seen.U = sums["far up"].rows, sums["up"].rows
     go("b2")
     go("b3")
-    feed_chip = core_sum(times_back(after(hidden_low, "feed"), w_dn), core)
-    seen["feed"] = feed_chip
+    feed_chip = core_sum(times_back(after(hidden_low, Order.feed), w_dn), core)
+    seen.feed = feed_chip
     go("b4")
-    feed_head = swap(after(feed_chip, "feed head"), "head")
-    grad_normed2 = chip_sum.astype(F32) + after(head_part, "norm2").astype(F32)
+    feed_head = swap(after(feed_chip, Order.feed_head), "head")
+    grad_normed2 = chip_sum.astype(F32) + after(head_part, Order.norm2).astype(F32)
     middle_grad, grad_mlp_gain = norm2_back(grad_normed2)
     grad_middle = cot.astype(F32) + middle_grad
     middle_low = both(grad_middle.astype(BF16), core)
-    seen["middle"] = middle_low
-    grad_gated = matmul(after(middle_low, "gated"), w_out)
+    seen.middle = middle_low
+    grad_gated = matmul(after(middle_low, Order.gated), w_out)
     mixed_gradient, outgate_grad, head_gain_part = gated_back(grad_gated)
     outgate_low = outgate_grad.astype(BF16)
     middle_core = core_order(middle_low, core)
     contribution = dot(mixed_gradient, lifted, (0, 0), PASSES)
-    seen["contribution"] = contribution
+    seen.contribution = contribution
     go("b5")
     outgoing = incoming(edge, contribution, reverse=True)
-    seen["outgoing"] = outgoing
+    seen.outgoing = outgoing
     far_sums = {}
     if bits == 2:
-        far_sums["down"], far_sums["gate"] = far_sum("down", "dp D"), far_sum("gate", "dp G")
-        seen["D sum"], seen["G sum"] = far_sums["down"], far_sums["gate"]
-    outgate_late = after(outgate_low, "O dots")
+        far_sums["down"], far_sums["gate"] = far_sum("down", Order.dp_D), far_sum("gate", Order.dp_G)
+        seen.D_sum, seen.G_sum = far_sums["down"], far_sums["gate"]
+    outgate_late = after(outgate_low, Order.O_dots)
     sums["far output"], sums["output"] = halves(
         [(middle_core, gated_low), (normed_core, outgate_late)]
     )
-    seen["O"] = sums["far output"].rows, sums["output"].rows
+    seen.O = sums["far output"].rows, sums["output"].rows
     if bits == 2:
         go("b6")
-    outgoing = after(outgoing, "kernel")
+    outgoing = after(outgoing, Order.kernel)
     qkv_low, decay_grad = mixer_backward(
         projected, decay, mixed_gradient, states, fades, incoming_state, outgoing
     )
@@ -680,40 +742,40 @@
     rank_low = times_back(logit_low, rate).astype(BF16)
     rank_low = jnp.pad(rank_low, ((0, 0), (0, 128 - rank)))
     mixer_low = jnp.concatenate([qkv_low, outgate_low, rank_low], 1)
-    seen["qkv"] = qkv_low
-    normed_chip = core_sum(times_back(after(mixer_low, "normed"), w_mixer), core)
-    seen["chip3"] = normed_chip
-    normed_head = exchange(normed_chip, "pieces c")
-    seen["head3"] = normed_head
-    qkv_rank = after(jnp.concatenate([qkv_low, rank_low], 1), "Q dots")
-    feed_head = after(feed_head, "result")
+    seen.qkv = qkv_low
+    normed_chip = core_sum(times_back(after(mixer_low, Order.normed), w_mixer), core)
+    seen.chip3 = normed_chip
+    normed_head = exchange(normed_chip, "pieces_c")
+    seen.head3 = normed_head
+    qkv_rank = after(jnp.concatenate([qkv_low, rank_low], 1), Order.Q_dots)
+    feed_head = after(feed_head, Order.result)
     result = (middle + (feed_chip.astype(F32) + feed_head.astype(F32))).astype(BF16)
     result = reorder(back_place, result)[0]
-    seen["result_"] = result
+    seen.result_ = result
     sums["far qkv"], sums["qkv"] = halves([(normed_core, qkv_rank)])
-    seen["Q"] = sums["far qkv"].rows, sums["qkv"].rows
+    seen.Q = sums["far qkv"].rows, sums["qkv"].rows
     if bits == 2:
         go("b7")
     go("b8")
     go("b9")
     go("b10")
     if bits == 2:
-        far_sums["qkv"] = far_sum("qkv", "dp Q")
-        seen["Q sum"] = far_sums["qkv"]
+        far_sums["qkv"] = far_sum("qkv", Order.dp_Q)
+        seen.Q_sum = far_sums["qkv"]
     go("b11")
     back.until(*sums)
     if bits == 2:
-        far_sums["up"], far_sums["output"] = far_sum("up", "dp U"), far_sum("output", "dp O")
-        seen["U sum"], seen["O sum"] = far_sums["up"], far_sums["output"]
-    normed_head = after(normed_head, "tail")
+        far_sums["up"], far_sums["output"] = far_sum("up", Order.dp_U), far_sum("output", Order.dp_O)
+        seen.U_sum, seen.O_sum = far_sums["up"], far_sums["output"]
+    normed_head = after(normed_head, Order.tail)
     grad_normed = normed_chip.astype(F32) + normed_head.astype(F32)
     inputs_grad, grad_mix_gain = norm_back(grad_normed)
     grad_tokens = reorder(back_place, grad_middle + inputs_grad)[0]
 
     finished = []
     for name in ("down", "gate", "up", "output", "qkv"):
-        got = far_sums[name] if name in far_sums else far_sum(name, "rest")
-        got = after(got, "end " + name)
+        got = far_sums[name] if name in far_sums else far_sum(name, Order.rest)
+        got = after(got, getattr(Order, "end_" + name))
         finished.append(sums[name].rows.astype(F32) + got.astype(F32))
     grad_down, grad_gate, grad_up, grad_output, grad_qkv = finished
 

time: 694 us -> 689 us (level)
  waiting for transfers between devices: 286 us -> 267 us
  starting transfers between devices: 77.3 us -> 87.9 us
    ppermute x36, waiting for transfers between devices: 173 us -> 151 us  [hop(): return lax.ppermute(x, 'seq', [(i, i ^ there[i % 2]) for i in range(count)])]
    ppermute x36, starting transfers between devices: 42.2 us -> 52.2 us  [hop(): return lax.ppermute(x, 'seq', [(i, i ^ there[i % 2]) for i in range(count)])]
    unnamed x288 -> x274, local copies, waits for them, and re-layouts: 35.9 us -> 32.5 us
    unnamed x38 -> x37, other arithmetic: 35.6 us -> 35.5 us
  transfers between devices with their start and end apart: 80 -> 80, of which waited for: 30 -> 29; matrix products, arithmetic and copies ran while one was open for 34% -> 35% of each run, Pallas kernels for 4% -> 4%
where the time goes in v4:
time: 689 us; the launch traced here: 685 us
  waiting for transfers between devices  267 us (39%)
  other arithmetic  134 us (19%)
  matrix products  107 us (16%)
  starting transfers between devices  87.9 us (13%)
  local copies, waits for them, and re-layouts  58.1 us (8%)
  Pallas kernels  27.6 us (4%)
    ppermute x36, waiting for transfers between devices, hop(): return lax.ppermute(x, 'seq', [(i, i ^ there[i % 2]) for i in range(count)])  151 us
    ppermute x38, waiting for transfers between devices, swap(): return lax.ppermute(x, axis, [(i, i ^ bit) for i in range(count)])  109 us
    ppermute x36, starting transfers between devices, hop(): return lax.ppermute(x, 'seq', [(i, i ^ there[i % 2]) for i in range(count)])  52.2 us
    dot_general x6, matrix products, matmul(): return jnp.dot(left, right, preferred_element_type=F32)  38 us
    dot_general x6, matrix products, times_back(): lax.dot_general(grad, weight, (((1,), (1,)), ((), ())), preferred_element...  36.2 us
    unnamed x37, other arithmetic  35.5 us
    unnamed x274, local copies, waits for them, and re-layouts  32.5 us
    dot_general x13, matrix products, inner(): lax.dot_general(left, right, (((0,), (0,)), ((), ())), preferred_element_...  31.7 us
  transfers between devices with their start and end apart: 80, of which 29 were waited for; matrix products, arithmetic and copies ran while one was open for 35% of the time, Pallas kernels for 4%

profile of v4, /device:TPU:0, one launch (start us, length us, event | category | flops | bytes accessed | tf_op | source)
XLA Modules:
  0.0 684.7 jit_solution(14859811631691412612)
XLA Ops:
  10.8 3.6 collective-permute-start.4
  37.9 7.7 %collective-permute-done.7 = bf16[256,1664]{1,0:T(8,128)(2,1)S(1)} collective-permute-done((bf16[256,1664]{1,0:T(8,128)(2,1)S(1)}, bf16[256,1664]{1,0:T(8,128)(2,1)S(1)}, u32[]{:S(2)}, u32[]{:S(2)}) %collective-permute-start.7) | collective-permute-done | bytes 852000 | tf_op jit(solution)/shard_map/ppermute | solution.py:302
  46.9 24.2 %collective-permute-done.4 = bf16[256,1664]{1,0:T(8,128)(2,1)} collective-permute-done((bf16[256,1664]{1,0:T(8,128)(2,1)}, bf16[256,1664]{1,0:T(8,128)(2,1)}, u32[]{:S(2)}, u32[]{:S(2)}) %collective-permute-start.4) | collective-permute-done | bytes 852000 | tf_op jit(solution)/shard_map/ppermute | solution.py:89
  74.3 14.6 %collective-permute-done.13 = bf16[256,1664]{1,0:T(8,128)(2,1)S(1)} collective-permute-done((bf16[256,1664]{1,0:T(8,128)(2,1)S(1)}, bf16[256,1664]{1,0:T(8,128)(2,1)S(1)}, u32[]{:S(2)}, u32[]{:S(2)}) %collective-permute-start.13) | collective-permute-done | bytes 852000 | tf_op jit(solution)/shard_map/ppermute | solution.py:89
  103.1 16.1 %collective-permute-done.14 = bf16[512,1664]{1,0:T(8,128)(2,1)S(1)} collective-permute-done((bf16[512,1664]{1,0:T(8,128)(2,1)S(1)}, bf16[512,1664]{1,0:T(8,128)(2,1)S(1)}, u32[]{:S(2)}, u32[]{:S(2)}) %collective-permute-start.14) | collective-permute-done | bytes 1703968 | tf_op jit(solution)/shard_map/ppermute | solution.py:302
  131.1 29.3 %collective-permute-done.20 = bf16[256,1664]{1,0:T(8,128)(2,1)S(1)} collective-permute-done((bf16[256,1664]{1,0:T(8,128)(2,1)S(1)}, bf16[256,1664]{1,0:T(8,128)(2,1)S(1)}, u32[]{:S(2)}, u32[]{:S(2)}) %collective-permute-start.20) | collective-permute-done | bytes 852000 | tf_op jit(solution)/shard_map/ppermute | solution.py:89
  163.9 8.8 %fusion.7.q_ref.k_ref.v_ref = f32[768,1664]{1,0:T(8,128)S(1)} fusion(bf16[2048,1664]{1,0:T(8,128)(2,1)} %slice_dynamic-update-slice_fusion, bf16[384,2048]{1,0:T(8,128)(2,1)S(1)} %get-tuple-element.282, bf16[384,2048]{1,0:T(8,128)(2,1)S(1)} %get-tuple-element.281), kind=kOutput, calls=%fused_computation.72 | convolution fusion | flops 5240782848 | bytes 15073280 | tf_op jit(solution)/shard_map/dot_general | solution.py:93
  174.4 7.6 %mixer_forward.1 = (f32[768,512]{1,0:T(8,128)S(1)}, f32[768,256]{1,0:T(8,128)S(1)}, f32[12,512,256]{2,1,0:T(8,128)S(1)}, f32[512,256]{1,0:T(8,128)S(1)}, f32[1,2...) custom-call(f32[768,1664]{1,0:T(8,128)S(1)} %fusion.7.q_ref.k_ref.v_ref, f32[768,1664]{1,0:T(8,128)S(1)} %fusion.7.q_ref.k_ref.v_ref, ...), custom_call_target="tpu_custom_call" | custom-call | tf_op jit(solution)/shard_map/mixer_forward/pallas_call | solution.py:216
  182.1 4.1 collective-permute-start.18
  196.0 4.2 collective-permute-done.17
  205.3 21.0 %collective-permute-done.22 = bf16[512,1664]{1,0:T(8,128)(2,1)S(1)} collective-permute-done((bf16[512,1664]{1,0:T(8,128)(2,1)S(1)}, bf16[512,1664]{1,0:T(8,128)(2,1)S(1)}, u32[]{:S(2)}, u32[]{:S(2)}) %collective-permute-start.22) | collective-permute-done | bytes 1703968 | tf_op jit(solution)/shard_map/ppermute | solution.py:302
  228.6 3.4 fusion.109
  237.6 13.1 %collective-permute-done.30 = bf16[256,1408]{1,0:T(8,128)(2,1)S(1)} collective-permute-done((bf16[256,1408]{1,0:T(8,128)(2,1)S(1)}, bf16[256,1408]{1,0:T(8,128)(2,1)S(1)}, u32[]{:S(2)}, u32[]{:S(2)}) %collective-permute-start.30) | collective-permute-done | bytes 720928 | tf_op jit(solution)/shard_map/ppermute | solution.py:302
  252.0 4.2 collective-permute-start.32
  258.5 4.8 collective-permute-done.28
  265.2 13.6 %collective-permute-done.29 = bf16[512,1408]{1,0:T(8,128)(2,1)S(1)} collective-permute-done((bf16[512,1408]{1,0:T(8,128)(2,1)}, bf16[512,1408]{1,0:T(8,128)(2,1)S(1)}, u32[]{:S(2)}, u32[]{:S(2)}) %collective-permute-start.29) | collective-permute-done | bytes 1441824 | tf_op jit(solution)/shard_map/ppermute | solution.py:302
  285.3 6.8 collective-permute-done.24
  301.6 7.7 %fusion.110 = f32[768,1408]{1,0:T(8,128)S(1)} fusion(bf16[768,2048]{1,0:T(8,128)(2,1)S(1)} %pad_maximum_fusion.5, bf16[2048,1408]{1,0:T(8,128)(2,1)} %maximum_dynamic-update-slice_fusion), kind=kOutput, calls=%fused_computation.433 | convolution fusion | flops 4429185024 | bytes 13238272 | tf_op jit(solution)/shard_map/dot_general | solution.py:93
  309.4 7.9 %multiply_convert_fusion.2 = (bf16[768,1408]{1,0:T(8,128)(2,1)S(1)}, f32[768,1408]{1,0:T(8,128)S(1)}) fusion(f32[768,1408]{1,0:T(8,128)S(1)} %fusion.110, bf16[768,2048]{1,0:T(8,128)(2,1)S(1)} %pad_maximum_fusion.5, bf16[2048,1408]{1,0:T(8,128)(2,1)} %slice_dynamic-update-slice_fusion.4), kind=kOutput, calls=%fused_computation.55 | convolution fusion | flops 4435673088 | bytes 19726336 | tf_op jit(solution)/shard_map/dot_general | solution.py:93
  317.3 3.1 convolution_convert_fusion.7
  322.4 3.1 convolution_convert_fusion.6
  327.6 7.5 %fusion.111 = f32[768,1408]{1,0:T(8,128)S(1)} fusion(bf16[768,2048]{1,0:T(8,128)(2,1)S(1)} %copy-done.47, bf16[2048,1408]{1,0:T(8,128)(2,1)} %slice_dynamic-update-slice_fusion.2), kind=kOutput, calls=%fused_computation.434 | convolution fusion | flops 4429185024 | bytes 13238272 | tf_op jit(solution)/shard_map/dot_general | solution.py:93
  337.2 3.5 multiply_convert_fusion
  340.8 5.1 convolution_convert_fusion.4
  348.0 3.1 convolution_convert_fusion.5
  355.8 6.9 %fusion.112 = f32[768,2048]{1,0:T(8,128)} fusion(bf16[768,1408]{1,0:T(8,128)(2,1)S(1)} %copy-done.62, bf16[2048,1408]{1,0:T(8,128)(2,1)S(1)} %bitcast.82), kind=kOutput, calls=%fused_computation.435 | convolution fusion | flops 4429185024 | bytes 14221312 | tf_op jit(solution)/shard_map/dot_general | solution.py:101
  362.7 7.2 %collective-permute-done.33 = bf16[512,1408]{1,0:T(8,128)(2,1)S(1)} collective-permute-done((bf16[512,1408]{1,0:T(8,128)(2,1)}, bf16[512,1408]{1,0:T(8,128)(2,1)S(1)}, u32[]{:S(2)}, u32[]{:S(2)}) %collective-permute-start.33) | collective-permute-done | bytes 1441824 | tf_op jit(solution)/shard_map/ppermute | solution.py:302
  369.9 9.5 %convolution_add_fusion = f32[768,2048]{1,0:T(8,128)S(1)} fusion(f32[768,2048]{1,0:T(8,128)} %fusion.112, bf16[768,1408]{1,0:T(8,128)(2,1)S(1)} %copy-done.64, bf16[2048,1408]{1,0:T(8,128)(2,1)} %maximum_dynamic-update-slice_fusion), kind=kOutput, calls=%fused_computation.66 | convolution fusion | flops 4430757888 | bytes 20512768 | tf_op jit(solution)/shard_map/dot_general | solution.py:101
  392.4 4.6 convolution_convert_fusion.2
  397.1 4.3 convolution_convert_fusion.3
  401.4 7.8 %fusion.113 = f32[768,2048]{1,0:T(8,128)S(1)} fusion(bf16[768,1408]{1,0:T(8,128)(2,1)} %copy-done.125, bf16[2048,1408]{1,0:T(8,128)(2,1)} %slice_dynamic-update-slice_fusion.2), kind=kOutput, calls=%fused_computation.436 | convolution fusion | flops 4429185024 | bytes 14221312 | tf_op jit(solution)/shard_map/dot_general | solution.py:101
  416.9 8.7 %collective-permute-done.38 = bf16[384,2048]{1,0:T(8,128)(2,1)S(1)} collective-permute-done((bf16[384,2048]{1,0:T(8,128)(2,1)S(1)}, bf16[384,2048]{1,0:T(8,128)(2,1)S(1)}, u32[]{:S(2)}, u32[]{:S(2)}) %collective-permute-start.38) | collective-permute-done | bytes 1572896 | tf_op jit(solution)/shard_map/ppermute | solution.py:89
  431.0 3.6 add_convert_fusion.2
  436.4 9.0 %collective-permute-done.49 = bf16[256,1408]{1,0:T(8,128)(2,1)} collective-permute-done((bf16[256,1408]{1,0:T(8,128)(2,1)}, bf16[256,1408]{1,0:T(8,128)(2,1)}, u32[]{:S(2)}, u32[]{:S(2)}) %collective-permute-start.49) | collective-permute-done | bytes 720928 | tf_op jit(solution)/shard_map/ppermute | solution.py:302
  448.4 9.3 %collective-permute-done.66 = bf16[512,1408]{1,0:T(8,128)(2,1)S(1)} collective-permute-done((bf16[512,1408]{1,0:T(8,128)(2,1)}, bf16[512,1408]{1,0:T(8,128)(2,1)S(1)}, u32[]{:S(2)}, u32[]{:S(2)}) %collective-permute-start.66) | collective-permute-done | bytes 1441824 | tf_op jit(solution)/shard_map/ppermute | solution.py:302
  461.6 11.5 %collective-permute-done.47 = bf16[512,1408]{1,0:T(8,128)(2,1)S(1)} collective-permute-done((bf16[512,1408]{1,0:T(8,128)(2,1)}, bf16[512,1408]{1,0:T(8,128)(2,1)S(1)}, u32[]{:S(2)}, u32[]{:S(2)}) %collective-permute-start.47) | collective-permute-done | bytes 1441824 | tf_op jit(solution)/shard_map/ppermute | solution.py:302
  474.9 4.4 multiply_reduce_fusion.3
  496.0 4.6 collective-permute-start.78
  502.4 3.8 collective-permute-done.43
  507.2 12.2 %mixer_backward.1 = (bf16[768,1024]{1,0:T(8,128)(2,1)S(1)}, f32[768,256]{1,0:T(8,128)S(1)}) custom-call(f32[768,1664]{1,0:T(8,128)S(1)} %fusion.7.q_ref.k_ref.v_ref, f32[768,1664]{1,0:T(8,128)S(1)} %fusion.7.q_ref.k_ref.v_ref, f32[768,1664]{1,0:T(8,128)S(1)} %fusion.7.q_ref.k_ref.v_ref, f32[768,256]{1,0:T(8,128)S(1)} %copy-done.7, ...), custom_call_target="tpu_custom_call" | custom-call | tf_op jit(solution)/shard_map/mixer_backward/pallas_call | solution.py:255
  525.9 8.5 %fusion.114 = f32[768,2048]{1,0:T(8,128)S(1)} fusion(bf16[768,1664]{1,0:T(8,128)(2,1)S(1)} %pad_maximum_fusion.8, bf16[2048,1664]{1,0:T(8,128)(2,1)} %slice_dynamic-update-slice_fusion), kind=kOutput, calls=%fused_computation.437 | convolution fusion | flops 5234491392 | bytes 15663104 | tf_op jit(solution)/shard_map/dot_general | solution.py:101
  571.6 3.6 collective-permute-done.55
  578.3 9.6 %collective-permute-done.62 = bf16[512,1152]{0,1:T(8,128)(2,1)} collective-permute-done((bf16[512,1152]{0,1:T(8,128)(2,1)}, bf16[512,1152]{0,1:T(8,128)(2,1)}, u32[]{:S(2)}, u32[]{:S(2)}) %collective-permute-start.62) | collective-permute-done | bytes 1179680 | tf_op jit(solution)/shard_map/ppermute | solution.py:302
  591.4 16.8 %collective-permute-done.53 = bf16[512,1152]{0,1:T(8,128)(2,1)} collective-permute-done((bf16[512,1152]{0,1:T(8,128)(2,1)}, bf16[512,1152]{0,1:T(8,128)(2,1)}, u32[]{:S(2)}, u32[]{:S(2)}) %collective-permute-start.53) | collective-permute-done | bytes 1179680 | tf_op jit(solution)/shard_map/ppermute | solution.py:302
  613.6 3.8 collective-permute-done.56
  632.4 3.0 fusion.3
  647.2 5.5 fusion.5
  657.7 16.5 %collective-permute-done.61 = f32[8,2048]{1,0:T(8,128)S(1)} collective-permute-done((f32[8,2048]{1,0:T(8,128)S(1)}, f32[8,2048]{1,0:T(8,128)S(1)}, u32[]{:S(2)}, u32[]{:S(2)}) %collective-permute-start.61) | collective-permute-done | bytes 65568 | tf_op jit(solution)/shard_map/ppermute | solution.py:89
  (642 shorter events, 278.5 us)
Async XLA Ops:
  10.8 60.3 %collective-permute-start.4 = (bf16[256,1664]{1,0:T(8,128)(2,1)}, bf16[256,1664]{1,0:T(8,128)(2,1)}, u32[]{:S(2)}, u32[]{:S(2)}) collective-permute-start(bf16[256,1664]{1,0:T(8,128)(2,1)} %pad_maximum_fusion.60), channel_id=1, source_target_pairs={{0,16},{16,0},{1,17},{17,1},{2,18},{18,2},{3,19},{19,3},{4,20},{20... | collective-permute-start | bytes 2555912 | tf_op jit(solution)/shard_map/ppermute | solution.py:89
  14.4 21.0 %collective-permute-start.3 = (bf16[256,1664]{1,0:T(8,128)(2,1)}, bf16[256,1664]{1,0:T(8,128)(2,1)S(1)}, u32[]{:S(2)}, u32[]{:S(2)}) collective-permute-start(bf16[256,1664]{1,0:T(8,128)(2,1)} %pad_maximum_fusion.60), channel_id=1, source_target_pairs={{0,4},{2,10},{4,0},{6,14},{8,12},{10,2},{12,8},{14,6},{1,5},{3,11}... | collective-permute-start | bytes 2555912 | tf_op jit(solution)/shard_map/ppermute | solution.py:302
  28.7 62.1 %collective-permute-start.2 = (bf16[384,2048]{1,0:T(8,128)(2,1)S(1)}, bf16[384,2048]{1,0:T(8,128)(2,1)S(1)}, u32[]{:S(2)}, u32[]{:S(2)}) collective-permute-start(bf16[384,2048]{1,0:T(8,128)(2,1)S(1)} %fusion.2), channel_id=1, source_target_pairs={{0,2},{2,0},{4,6},{6,4},{8,10},{10,8},{12,14},{14,12},{1,3},{3,1},... | collective-permute-start | bytes 4718600 | tf_op jit(solution)/shard_map/ppermute | solution.py:89
  35.4 53.6 %collective-permute-start.13 = (bf16[256,1664]{1,0:T(8,128)(2,1)S(1)}, bf16[256,1664]{1,0:T(8,128)(2,1)S(1)}, u32[]{:S(2)}, u32[]{:S(2)}) collective-permute-start(bf16[256,1664]{1,0:T(8,128)(2,1)S(1)} %pad_maximum_fusion.61), channel_id=1, source_target_pairs={{0,16},{16,0},{1,17},{17,1},{2,18},{18,2},{3,19},{19,3},{4,20},{20... | collective-permute-start | bytes 2555912 | tf_op jit(solution)/shard_map/ppermute | solution.py:89
  36.4 34.6 %collective-permute-start.9 = (bf16[256,1664]{1,0:T(8,128)(2,1)S(1)}, bf16[256,1664]{1,0:T(8,128)(2,1)S(1)}, u32[]{:S(2)}, u32[]{:S(2)}) collective-permute-start(bf16[256,1664]{1,0:T(8,128)(2,1)S(1)} %maximum_maximum_fusion), channel_id=1, source_target_pairs={{0,4},{2,10},{4,0},{6,14},{8,12},{10,2},{12,8},{14,6},{1,5},{3,11}... | collective-permute-start | bytes 2555912 | tf_op jit(solution)/shard_map/ppermute | solution.py:302
  45.6 48.6 %collective-permute-start.31 = (bf16[384,2048]{1,0:T(8,128)(2,1)S(1)}, bf16[384,2048]{1,0:T(8,128)(2,1)S(1)}, u32[]{:S(2)}, u32[]{:S(2)}) collective-permute-start(bf16[384,2048]{1,0:T(8,128)(2,1)S(1)} %get-tuple-element.106), channel_id=1, source_target_pairs={{0,2},{2,0},{4,6},{6,4},{8,10},{10,8},{12,14},{14,12},{1,3},{3,1},... | collective-permute-start | bytes 4718600 | tf_op jit(solution)/shard_map/ppermute | solution.py:89
  71.1 30.7 %collective-permute-start.12 = (bf16[256,1664]{1,0:T(8,128)(2,1)}, bf16[256,1664]{1,0:T(8,128)(2,1)S(1)}, u32[]{:S(2)}, u32[]{:S(2)}) collective-permute-start(bf16[256,1664]{1,0:T(8,128)(2,1)} %collective-permute-done.4), channel_id=1, source_target_pairs={{0,4},{2,10},{4,0},{6,14},{8,12},{10,2},{12,8},{14,6},{1,5},{3,11}... | collective-permute-start | bytes 2555912 | tf_op jit(solution)/shard_map/ppermute | solution.py:302
  72.8 30.3 %collective-permute-start.11 = (bf16[512,1664]{1,0:T(8,128)(2,1)S(1)}, bf16[512,1664]{1,0:T(8,128)(2,1)S(1)}, u32[]{:S(2)}, u32[]{:S(2)}) collective-permute-start(bf16[512,1664]{1,0:T(8,128)(2,1)S(1)} %pad_maximum_fusion.10), channel_id=1, source_target_pairs={{0,8},{2,6},{4,12},{6,2},{8,0},{10,14},{12,4},{14,10},{1,9},{3,7},... | collective-permute-start | bytes 5111816 | tf_op jit(solution)/shard_map/ppermute | solution.py:302
  89.0 30.2 %collective-permute-start.14 = (bf16[512,1664]{1,0:T(8,128)(2,1)S(1)}, bf16[512,1664]{1,0:T(8,128)(2,1)S(1)}, u32[]{:S(2)}, u32[]{:S(2)}) collective-permute-start(bf16[512,1664]{1,0:T(8,128)(2,1)S(1)} %pad_maximum_fusion.11), channel_id=1, source_target_pairs={{0,8},{2,6},{4,12},{6,2},{8,0},{10,14},{12,4},{14,10},{1,9},{3,7},... | collective-permute-start | bytes 5111816 | tf_op jit(solution)/shard_map/ppermute | solution.py:302
  119.2 41.2 %collective-permute-start.19 = (bf16[256,1664]{1,0:T(8,128)(2,1)S(1)}, bf16[256,1664]{1,0:T(8,128)(2,1)S(1)}, u32[]{:S(2)}, u32[]{:S(2)}) collective-permute-start(bf16[256,1664]{1,0:T(8,128)(2,1)S(1)} %collective-permute-done.13), channel_id=1, source_target_pairs={{0,4},{2,10},{4,0},{6,14},{8,12},{10,2},{12,8},{14,6},{1,5},{3,11}... | collective-permute-start | bytes 2555912 | tf_op jit(solution)/shard_map/ppermute | solution.py:302
  120.5 39.9 %collective-permute-start.20 = (bf16[256,1664]{1,0:T(8,128)(2,1)S(1)}, bf16[256,1664]{1,0:T(8,128)(2,1)S(1)}, u32[]{:S(2)}, u32[]{:S(2)}) collective-permute-start(bf16[256,1664]{1,0:T(8,128)(2,1)S(1)} %maximum_maximum_fusion), channel_id=1, source_target_pairs={{0,16},{16,0},{1,17},{17,1},{2,18},{18,2},{3,19},{19,3},{4,20},{20... | collective-permute-start | bytes 2555912 | tf_op jit(solution)/shard_map/ppermute | solution.py:89
  120.5 40.0 %collective-permute-start.15 = (bf16[512,1664]{1,0:T(8,128)(2,1)S(1)}, bf16[512,1664]{1,0:T(8,128)(2,1)S(1)}, u32[]{:S(2)}, u32[]{:S(2)}) collective-permute-start(bf16[512,1664]{1,0:T(8,128)(2,1)S(1)} %pad_maximum_fusion.12), channel_id=1, source_target_pairs={{0,8},{2,6},{4,12},{6,2},{8,0},{10,14},{12,4},{14,10},{1,9},{3,7},... | collective-permute-start | bytes 5111816 | tf_op jit(solution)/shard_map/ppermute | solution.py:302
  122.0 68.0 %collective-permute-start.21 = (bf16[512,1664]{1,0:T(8,128)(2,1)S(1)}, bf16[512,1664]{1,0:T(8,128)(2,1)S(1)}, u32[]{:S(2)}, u32[]{:S(2)}) collective-permute-start(bf16[512,1664]{1,0:T(8,128)(2,1)S(1)} %pad_maximum_fusion.13), channel_id=1, source_target_pairs={{0,8},{2,6},{4,12},{6,2},{8,0},{10,14},{12,4},{14,10},{1,9},{3,7},... | collective-permute-start | bytes 5111816 | tf_op jit(solution)/shard_map/ppermute | solution.py:302
  182.1 20.7 %collective-permute-start.18 = (bf16[528,256]{1,0:T(8,128)(2,1)S(1)}, bf16[528,256]{1,0:T(8,128)(2,1)S(1)}, u32[]{:S(2)}, u32[]{:S(2)}) collective-permute-start(bf16[528,256]{1,0:T(8,128)(2,1)S(1)} %pad_maximum_fusion.66), channel_id=1, source_target_pairs={{0,12},{2,14},{1,13},{3,15},{16,28},{18,30},{17,29},{19,31}} | collective-permute-start | bytes 811016 | tf_op jit(solution)/shard_map/ppermute | solution.py:469
  190.0 43.4 %collective-permute-start.27 = (bf16[256,1408]{1,0:T(8,128)(2,1)}, bf16[256,1408]{1,0:T(8,128)(2,1)S(1)}, u32[]{:S(2)}, u32[]{:S(2)}) collective-permute-start(bf16[256,1408]{1,0:T(8,128)(2,1)} %pad_maximum_fusion.62), channel_id=1, source_target_pairs={{0,16},{16,0},{1,17},{17,1},{2,18},{18,2},{3,19},{19,3},{4,20},{20... | collective-permute-start | bytes 2162696 | tf_op jit(solution)/shard_map/ppermute | solution.py:89
  190.1 43.2 %collective-permute-start.26 = (bf16[256,1664]{1,0:T(8,128)(2,1)S(1)}, bf16[256,1664]{1,0:T(8,128)(2,1)S(1)}, u32[]{:S(2)}, u32[]{:S(2)}) collective-permute-start(bf16[256,1664]{1,0:T(8,128)(2,1)S(1)} %collective-permute-done.20), channel_id=1, source_target_pairs={{0,4},{2,10},{4,0},{6,14},{8,12},{10,2},{12,8},{14,6},{1,5},{3,11}... | collective-permute-start | bytes 2555912 | tf_op jit(solution)/shard_map/ppermute | solution.py:302
  200.2 26.2 %collective-permute-start.22 = (bf16[512,1664]{1,0:T(8,128)(2,1)S(1)}, bf16[512,1664]{1,0:T(8,128)(2,1)S(1)}, u32[]{:S(2)}, u32[]{:S(2)}) collective-permute-start(bf16[512,1664]{1,0:T(8,128)(2,1)S(1)} %pad_maximum_fusion.14), channel_id=1, source_target_pairs={{0,8},{2,6},{4,12},{6,2},{8,0},{10,14},{12,4},{14,10},{1,9},{3,7},... | collective-permute-start | bytes 5111816 | tf_op jit(solution)/shard_map/ppermute | solution.py:302
  232.3 23.8 %collective-permute-start.23 = (bf16[384,2048]{1,0:T(8,128)(2,1)S(1)}, bf16[384,2048]{1,0:T(8,128)(2,1)}, u32[]{:S(2)}, u32[]{:S(2)}) collective-permute-start(bf16[384,2048]{1,0:T(8,128)(2,1)S(1)} %select_convert_fusion.3), channel_id=1, source_target_pairs={{0,2},{2,0},{4,6},{6,4},{8,10},{10,8},{12,14},{14,12},{1,3},{3,1},... | collective-permute-start | bytes 4718600 | tf_op jit(solution)/shard_map/ppermute | solution.py:89
  234.5 28.8 %collective-permute-start.28 = (bf16[512,1664]{1,0:T(8,128)(2,1)S(1)}, bf16[512,1664]{1,0:T(8,128)(2,1)S(1)}, u32[]{:S(2)}, u32[]{:S(2)}) collective-permute-start(bf16[512,1664]{1,0:T(8,128)(2,1)S(1)} %pad_maximum_fusion.15), channel_id=1, source_target_pairs={{0,8},{2,6},{4,12},{6,2},{8,0},{10,14},{12,4},{14,10},{1,9},{3,7},... | collective-permute-start | bytes 5111816 | tf_op jit(solution)/shard_map/ppermute | solution.py:302
  237.1 41.7 %collective-permute-start.29 = (bf16[512,1408]{1,0:T(8,128)(2,1)}, bf16[512,1408]{1,0:T(8,128)(2,1)S(1)}, u32[]{:S(2)}, u32[]{:S(2)}) collective-permute-start(bf16[512,1408]{1,0:T(8,128)(2,1)} %pad_maximum_fusion.56), channel_id=1, source_target_pairs={{0,8},{2,6},{4,12},{6,2},{8,0},{10,14},{12,4},{14,10},{1,9},{3,7},... | collective-permute-start | bytes 4325384 | tf_op jit(solution)/shard_map/ppermute | solution.py:302
  252.0 42.9 %collective-permute-start.32 = (bf16[512,1408]{1,0:T(8,128)(2,1)}, bf16[512,1408]{1,0:T(8,128)(2,1)S(1)}, u32[]{:S(2)}, u32[]{:S(2)}) collective-permute-start(bf16[512,1408]{1,0:T(8,128)(2,1)} %pad_maximum_fusion.57), channel_id=1, source_target_pairs={{0,8},{2,6},{4,12},{6,2},{8,0},{10,14},{12,4},{14,10},{1,9},{3,7},... | collective-permute-start | bytes 4325384 | tf_op jit(solution)/shard_map/ppermute | solution.py:302
  258.5 33.6 %collective-permute-start.24 = (bf16[384,2048]{1,0:T(8,128)(2,1)S(1)}, bf16[384,2048]{1,0:T(8,128)(2,1)S(1)}, u32[]{:S(2)}, u32[]{:S(2)}) collective-permute-start(bf16[384,2048]{1,0:T(8,128)(2,1)S(1)} %add_convert_fusion.4), channel_id=1, source_target_pairs={{0,1},{1,0},{2,3},{3,2},{4,5},{5,4},{6,7},{7,6},{8,9},{9,8},{10,11... | collective-permute-start | bytes 4718600 | tf_op jit(solution)/shard_map/ppermute | solution.py:89
  335.2 44.6 %collective-permute-start.45 = (bf16[512,1408]{1,0:T(8,128)(2,1)}, bf16[512,1408]{1,0:T(8,128)(2,1)}, u32[]{:S(2)}, u32[]{:S(2)}) collective-permute-start(bf16[512,1408]{1,0:T(8,128)(2,1)} %slice.807), channel_id=1, source_target_pairs={{0,8},{2,6},{4,12},{6,2},{8,0},{10,14},{12,4},{14,10},{1,9},{3,7},... | collective-permute-start | bytes 4325384 | tf_op jit(solution)/shard_map/ppermute | solution.py:302
  337.1 32.8 %collective-permute-start.33 = (bf16[512,1408]{1,0:T(8,128)(2,1)}, bf16[512,1408]{1,0:T(8,128)(2,1)S(1)}, u32[]{:S(2)}, u32[]{:S(2)}) collective-permute-start(bf16[512,1408]{1,0:T(8,128)(2,1)} %slice.787), channel_id=1, source_target_pairs={{0,8},{2,6},{4,12},{6,2},{8,0},{10,14},{12,4},{14,10},{1,9},{3,7},... | collective-permute-start | bytes 4325384 | tf_op jit(solution)/shard_map/ppermute | solution.py:302
  353.9 32.6 %collective-permute-start.35 = (bf16[512,1408]{1,0:T(8,128)(2,1)}, bf16[512,1408]{1,0:T(8,128)(2,1)}, u32[]{:S(2)}, u32[]{:S(2)}) collective-permute-start(bf16[512,1408]{1,0:T(8,128)(2,1)} %slice.790), channel_id=1, source_target_pairs={{0,8},{2,6},{4,12},{6,2},{8,0},{10,14},{12,4},{14,10},{1,9},{3,7},... | collective-permute-start | bytes 4325384 | tf_op jit(solution)/shard_map/ppermute | solution.py:302
  390.1 35.6 %collective-permute-start.38 = (bf16[384,2048]{1,0:T(8,128)(2,1)S(1)}, bf16[384,2048]{1,0:T(8,128)(2,1)S(1)}, u32[]{:S(2)}, u32[]{:S(2)}) collective-permute-start(bf16[384,2048]{1,0:T(8,128)(2,1)S(1)} %add_convert_fusion.3), channel_id=1, source_target_pairs={{0,1},{1,0},{2,3},{3,2},{4,5},{5,4},{6,7},{7,6},{8,9},{9,8},{10,11... | collective-permute-start | bytes 4718600 | tf_op jit(solution)/shard_map/ppermute | solution.py:89
  390.4 23.7 %collective-permute-start.46 = (bf16[512,1408]{1,0:T(8,128)(2,1)}, bf16[512,1408]{1,0:T(8,128)(2,1)}, u32[]{:S(2)}, u32[]{:S(2)}) collective-permute-start(bf16[512,1408]{1,0:T(8,128)(2,1)} %slice.805), channel_id=1, source_target_pairs={{0,8},{2,6},{4,12},{6,2},{8,0},{10,14},{12,4},{14,10},{1,9},{3,7},... | collective-permute-start | bytes 4325384 | tf_op jit(solution)/shard_map/ppermute | solution.py:302
  410.7 20.3 %collective-permute-start.37 = (bf16[384,2048]{1,0:T(8,128)(2,1)}, bf16[384,2048]{1,0:T(8,128)(2,1)}, u32[]{:S(2)}, u32[]{:S(2)}) collective-permute-start(bf16[384,2048]{1,0:T(8,128)(2,1)} %select_convert_fusion.1), channel_id=1, source_target_pairs={{0,2},{2,0},{4,6},{6,4},{8,10},{10,8},{12,14},{14,12},{1,3},{3,1},... | collective-permute-start | bytes 4718600 | tf_op jit(solution)/shard_map/ppermute | solution.py:89
  425.6 59.2 %collective-permute-start.44 = (bf16[256,1408]{1,0:T(8,128)(2,1)}, bf16[256,1408]{1,0:T(8,128)(2,1)}, u32[]{:S(2)}, u32[]{:S(2)}) collective-permute-start(bf16[256,1408]{1,0:T(8,128)(2,1)} %add_convert_fusion.20), channel_id=1, source_target_pairs={{0,16},{16,0},{1,17},{17,1},{2,18},{18,2},{3,19},{19,3},{4,20},{20... | collective-permute-start | bytes 2162696 | tf_op jit(solution)/shard_map/ppermute | solution.py:89
  426.0 19.4 %collective-permute-start.49 = (bf16[256,1408]{1,0:T(8,128)(2,1)}, bf16[256,1408]{1,0:T(8,128)(2,1)}, u32[]{:S(2)}, u32[]{:S(2)}) collective-permute-start(bf16[256,1408]{1,0:T(8,128)(2,1)} %slice.813), channel_id=1, source_target_pairs={{0,4},{2,10},{4,0},{6,14},{8,12},{10,2},{12,8},{14,6},{1,5},{3,11}... | collective-permute-start | bytes 2162696 | tf_op jit(solution)/shard_map/ppermute | solution.py:302
  427.7 30.0 %collective-permute-start.66 = (bf16[512,1408]{1,0:T(8,128)(2,1)}, bf16[512,1408]{1,0:T(8,128)(2,1)S(1)}, u32[]{:S(2)}, u32[]{:S(2)}) collective-permute-start(bf16[512,1408]{1,0:T(8,128)(2,1)} %slice.812), channel_id=1, source_target_pairs={{0,8},{2,6},{4,12},{6,2},{8,0},{10,14},{12,4},{14,10},{1,9},{3,7},... | collective-permute-start | bytes 4325384 | tf_op jit(solution)/shard_map/ppermute | solution.py:302
  434.6 38.6 %collective-permute-start.47 = (bf16[512,1408]{1,0:T(8,128)(2,1)}, bf16[512,1408]{1,0:T(8,128)(2,1)S(1)}, u32[]{:S(2)}, u32[]{:S(2)}) collective-permute-start(bf16[512,1408]{1,0:T(8,128)(2,1)} %slice.803), channel_id=1, source_target_pairs={{0,8},{2,6},{4,12},{6,2},{8,0},{10,14},{12,4},{14,10},{1,9},{3,7},... | collective-permute-start | bytes 4325384 | tf_op jit(solution)/shard_map/ppermute | solution.py:302
  436.3 38.3 %collective-permute-start.40 = (bf16[384,2048]{1,0:T(8,128)(2,1)S(1)}, bf16[384,2048]{1,0:T(8,128)(2,1)S(1)}, u32[]{:S(2)}, u32[]{:S(2)}) collective-permute-start(bf16[384,2048]{1,0:T(8,128)(2,1)S(1)} %fusion.87), channel_id=1, source_target_pairs={{0,2},{2,0},{4,6},{6,4},{8,10},{10,8},{12,14},{14,12},{1,3},{3,1},... | collective-permute-start | bytes 4718600 | tf_op jit(solution)/shard_map/ppermute | solution.py:89
  445.4 60.9 %collective-permute-start.48 = (bf16[256,1408]{1,0:T(8,128)(2,1)}, bf16[256,1408]{1,0:T(8,128)(2,1)S(1)}, u32[]{:S(2)}, u32[]{:S(2)}) collective-permute-start(bf16[256,1408]{1,0:T(8,128)(2,1)} %slice.809), channel_id=1, source_target_pairs={{0,4},{2,10},{4,0},{6,14},{8,12},{10,2},{12,8},{14,6},{1,5},{3,11}... | collective-permute-start | bytes 2162696 | tf_op jit(solution)/shard_map/ppermute | solution.py:302
  457.7 48.6 %collective-permute-start.50 = (bf16[256,1408]{1,0:T(8,128)(2,1)S(1)}, bf16[256,1408]{1,0:T(8,128)(2,1)S(1)}, u32[]{:S(2)}, u32[]{:S(2)}) collective-permute-start(bf16[256,1408]{1,0:T(8,128)(2,1)S(1)} %add_convert_fusion.19), channel_id=1, source_target_pairs={{0,16},{16,0},{1,17},{17,1},{2,18},{18,2},{3,19},{19,3},{4,20},{20... | collective-permute-start | bytes 2162696 | tf_op jit(solution)/shard_map/ppermute | solution.py:89
  482.8 17.9 %collective-permute-start.41 = (bf16[528,256]{1,0:T(8,128)(2,1)S(1)}, bf16[528,256]{1,0:T(8,128)(2,1)S(1)}, u32[]{:S(2)}, u32[]{:S(2)}) collective-permute-start(bf16[528,256]{1,0:T(8,128)(2,1)S(1)} %pad_maximum_fusion.65), channel_id=1, source_target_pairs={{4,0},{6,2},{8,4},{10,6},{12,8},{14,10},{5,1},{7,3},{9,5},{11,7},{... | collective-permute-start | bytes 811016 | tf_op jit(solution)/shard_map/ppermute | solution.py:469
  496.0 56.6 %collective-permute-start.78 = (bf16[256,1408]{1,0:T(8,128)(2,1)}, bf16[256,1408]{1,0:T(8,128)(2,1)}, u32[]{:S(2)}, u32[]{:S(2)}) collective-permute-start(bf16[256,1408]{1,0:T(8,128)(2,1)} %slice.808), channel_id=1, source_target_pairs={{0,4},{2,10},{4,0},{6,14},{8,12},{10,2},{12,8},{14,6},{1,5},{3,11}... | collective-permute-start | bytes 2162696 | tf_op jit(solution)/shard_map/ppermute | solution.py:302
  500.7 38.4 %collective-permute-start.39 = (bf16[384,2048]{1,0:T(8,128)(2,1)}, bf16[384,2048]{1,0:T(8,128)(2,1)}, u32[]{:S(2)}, u32[]{:S(2)}) collective-permute-start(bf16[384,2048]{1,0:T(8,128)(2,1)} %add_convert_fusion.2), channel_id=1, source_target_pairs={{0,1},{1,0},{2,3},{3,2},{4,5},{5,4},{6,7},{7,6},{8,9},{9,8},{10,11... | collective-permute-start | bytes 4718600 | tf_op jit(solution)/shard_map/ppermute | solution.py:89
  520.4 22.8 %collective-permute-start.75 = (bf16[256,1408]{1,0:T(8,128)(2,1)}, bf16[256,1408]{1,0:T(8,128)(2,1)}, u32[]{:S(2)}, u32[]{:S(2)}) collective-permute-start(bf16[256,1408]{1,0:T(8,128)(2,1)} %slice.847), channel_id=1, source_target_pairs={{0,4},{2,10},{4,0},{6,14},{8,12},{10,2},{12,8},{14,6},{1,5},{3,11}... | collective-permute-start | bytes 2162696 | tf_op jit(solution)/shard_map/ppermute | solution.py:302
  520.4 27.7 %collective-permute-start.67 = (bf16[512,1024]{0,1:T(8,128)(2,1)}, bf16[512,1024]{0,1:T(8,128)(2,1)}, u32[]{:S(2)}, u32[]{:S(2)}) collective-permute-start(bf16[512,1024]{0,1:T(8,128)(2,1)} %fusion.27), channel_id=1, source_target_pairs={{0,8},{2,6},{4,12},{6,2},{8,0},{10,14},{12,4},{14,10},{1,9},{3,7},... | collective-permute-start | bytes 3145736 | tf_op jit(solution)/shard_map/ppermute | solution.py:302
  546.0 71.8 %collective-permute-start.76 = (bf16[256,1408]{1,0:T(8,128)(2,1)}, bf16[256,1408]{1,0:T(8,128)(2,1)}, u32[]{:S(2)}, u32[]{:S(2)}) collective-permute-start(bf16[256,1408]{1,0:T(8,128)(2,1)} %add_convert_fusion.16), channel_id=1, source_target_pairs={{0,16},{16,0},{1,17},{17,1},{2,18},{18,2},{3,19},{19,3},{4,20},{20... | collective-permute-start | bytes 2162696 | tf_op jit(solution)/shard_map/ppermute | solution.py:89
  559.2 62.9 %collective-permute-start.52 = (bf16[384,2048]{1,0:T(8,128)(2,1)S(1)}, bf16[384,2048]{1,0:T(8,128)(2,1)}, u32[]{:S(2)}, u32[]{:S(2)}) collective-permute-start(bf16[384,2048]{1,0:T(8,128)(2,1)S(1)} %add_convert_fusion), channel_id=1, source_target_pairs={{0,1},{1,0},{2,3},{3,2},{4,5},{5,4},{6,7},{7,6},{8,9},{9,8},{10,11... | collective-permute-start | bytes 4718600 | tf_op jit(solution)/shard_map/ppermute | solution.py:89
  565.4 22.5 %collective-permute-start.62 = (bf16[512,1152]{0,1:T(8,128)(2,1)}, bf16[512,1152]{0,1:T(8,128)(2,1)}, u32[]{:S(2)}, u32[]{:S(2)}) collective-permute-start(bf16[512,1152]{0,1:T(8,128)(2,1)} %slice.830), channel_id=1, source_target_pairs={{0,8},{2,6},{4,12},{6,2},{8,0},{10,14},{12,4},{14,10},{1,9},{3,7},... | collective-permute-start | bytes 3538952 | tf_op jit(solution)/shard_map/ppermute | solution.py:302
  565.4 42.9 %collective-permute-start.53 = (bf16[512,1152]{0,1:T(8,128)(2,1)}, bf16[512,1152]{0,1:T(8,128)(2,1)}, u32[]{:S(2)}, u32[]{:S(2)}) collective-permute-start(bf16[512,1152]{0,1:T(8,128)(2,1)} %slice.817), channel_id=1, source_target_pairs={{0,8},{2,6},{4,12},{6,2},{8,0},{10,14},{12,4},{14,10},{1,9},{3,7},... | collective-permute-start | bytes 3538952 | tf_op jit(solution)/shard_map/ppermute | solution.py:302
  575.3 38.3 %collective-permute-start.69 = (bf16[256,1024]{0,1:T(8,128)(2,1)}, bf16[256,1024]{0,1:T(8,128)(2,1)S(1)}, u32[]{:S(2)}, u32[]{:S(2)}) collective-permute-start(bf16[256,1024]{0,1:T(8,128)(2,1)} %add_convert_fusion.23), channel_id=1, source_target_pairs={{0,16},{16,0},{1,17},{17,1},{2,18},{18,2},{3,19},{19,3},{4,20},{20... | collective-permute-start | bytes 1572872 | tf_op jit(solution)/shard_map/ppermute | solution.py:89
  587.9 29.9 %collective-permute-start.74 = (bf16[256,1408]{1,0:T(8,128)(2,1)S(1)}, bf16[256,1408]{1,0:T(8,128)(2,1)S(1)}, u32[]{:S(2)}, u32[]{:S(2)}) collective-permute-start(bf16[256,1408]{1,0:T(8,128)(2,1)S(1)} %copy-done.77), channel_id=1, source_target_pairs={{0,4},{2,10},{4,0},{6,14},{8,12},{10,2},{12,8},{14,6},{1,5},{3,11}... | collective-permute-start | bytes 2162696 | tf_op jit(solution)/shard_map/ppermute | solution.py:302
  644.1 30.7 %collective-permute-start.64 = (bf16[256,1152]{0,1:T(8,128)(2,1)S(1)}, bf16[256,1152]{0,1:T(8,128)(2,1)S(1)}, u32[]{:S(2)}, u32[]{:S(2)}) collective-permute-start(bf16[256,1152]{0,1:T(8,128)(2,1)S(1)} %add_convert_fusion.21), channel_id=1, source_target_pairs={{0,16},{16,0},{1,17},{17,1},{2,18},{18,2},{3,19},{19,3},{4,20},{20... | collective-permute-start | bytes 1769480 | tf_op jit(solution)/shard_map/ppermute | solution.py:89
  646.3 27.8 %collective-permute-start.61 = (f32[8,2048]{1,0:T(8,128)S(1)}, f32[8,2048]{1,0:T(8,128)S(1)}, u32[]{:S(2)}, u32[]{:S(2)}) collective-permute-start(f32[8,2048]{1,0:T(8,128)S(1)} %add.329), channel_id=1, source_target_pairs={{0,16},{16,0},{1,17},{17,1},{2,18},{18,2},{3,19},{19,3},{4,20},{20... | collective-permute-start | bytes 196616 | tf_op jit(solution)/shard_map/ppermute | solution.py:89
  (162 other events, 1794.0 us)

commit v5 on v4

--- a/solution.py
+++ b/solution.py
@@ -26,7 +26,7 @@
     pieces_a = 1
     pieces_b = 1
     pieces_c = 1
-    far_two = lambda at: ()
+    far_two = lambda at: (at.far_mixer,)
     one = lambda at: (at.zero, at.far_mixer,)
     far_three = lambda at: (at.one, at.far_two,)
     two = lambda at: (at.one, at.far_two,)

time: 689 us -> 683 us (level)
  transfers between devices with their start and end apart: 80 -> 80, of which waited for: 29 -> 28; matrix products, arithmetic and copies ran while one was open for 35% -> 35% of each run, Pallas kernels for 4% -> 4%
where the time goes in v5:
time: 683 us; the launch traced here: 679 us
  waiting for transfers between devices  261 us (38%)
  other arithmetic  134 us (20%)
  matrix products  107 us (16%)
  starting transfers between devices  87.9 us (13%)
  local copies, waits for them, and re-layouts  58.1 us (9%)
  Pallas kernels  27.6 us (4%)
    ppermute x36, waiting for transfers between devices, hop(): return lax.ppermute(x, 'seq', [(i, i ^ there[i % 2]) for i in range(count)])  144 us
    ppermute x38, waiting for transfers between devices, swap(): return lax.ppermute(x, axis, [(i, i ^ bit) for i in range(count)])  109 us
    ppermute x36, starting transfers between devices, hop(): return lax.ppermute(x, 'seq', [(i, i ^ there[i % 2]) for i in range(count)])  51.7 us
    dot_general x6, matrix products, matmul(): return jnp.dot(left, right, preferred_element_type=F32)  38 us
    dot_general x6, matrix products, times_back(): lax.dot_general(grad, weight, (((1,), (1,)), ((), ())), preferred_element...  36.2 us
    unnamed x37, other arithmetic  35.5 us
    unnamed x274, local copies, waits for them, and re-layouts  32.5 us
    dot_general x13, matrix products, inner(): lax.dot_general(left, right, (((0,), (0,)), ((), ())), preferred_element_...  31.7 us
  transfers between devices with their start and end apart: 80, of which 28 were waited for; matrix products, arithmetic and copies ran while one was open for 35% of the time, Pallas kernels for 4%

profile of v5, /device:TPU:0, one launch (start us, length us, event | category | flops | bytes accessed | tf_op | source)
XLA Modules:
  0.0 679.1 jit_solution(232314083645205858)
XLA Ops:
  10.8 3.6 collective-permute-start.4
  35.4 17.2 %collective-permute-done.4 = bf16[256,1664]{1,0:T(8,128)(2,1)} collective-permute-done((bf16[256,1664]{1,0:T(8,128)(2,1)}, bf16[256,1664]{1,0:T(8,128)(2,1)}, u32[]{:S(2)}, u32[]{:S(2)}) %collective-permute-start.4) | collective-permute-done | bytes 852000 | tf_op jit(solution)/shard_map/ppermute | solution.py:89
  55.9 9.4 %collective-permute-done.9 = bf16[256,1664]{1,0:T(8,128)(2,1)S(1)} collective-permute-done((bf16[256,1664]{1,0:T(8,128)(2,1)S(1)}, bf16[256,1664]{1,0:T(8,128)(2,1)S(1)}, u32[]{:S(2)}, u32[]{:S(2)}) %collective-permute-start.9) | collective-permute-done | bytes 852000 | tf_op jit(solution)/shard_map/ppermute | solution.py:302
  68.4 25.3 %collective-permute-done.13 = bf16[256,1664]{1,0:T(8,128)(2,1)S(1)} collective-permute-done((bf16[256,1664]{1,0:T(8,128)(2,1)S(1)}, bf16[256,1664]{1,0:T(8,128)(2,1)S(1)}, u32[]{:S(2)}, u32[]{:S(2)}) %collective-permute-start.13) | collective-permute-done | bytes 852000 | tf_op jit(solution)/shard_map/ppermute | solution.py:89
  106.8 8.8 %collective-permute-done.14 = bf16[512,1664]{1,0:T(8,128)(2,1)S(1)} collective-permute-done((bf16[512,1664]{1,0:T(8,128)(2,1)S(1)}, bf16[512,1664]{1,0:T(8,128)(2,1)S(1)}, u32[]{:S(2)}, u32[]{:S(2)}) %collective-permute-start.14) | collective-permute-done | bytes 1703968 | tf_op jit(solution)/shard_map/ppermute | solution.py:302
  127.6 26.5 %collective-permute-done.20 = bf16[256,1664]{1,0:T(8,128)(2,1)S(1)} collective-permute-done((bf16[256,1664]{1,0:T(8,128)(2,1)S(1)}, bf16[256,1664]{1,0:T(8,128)(2,1)S(1)}, u32[]{:S(2)}, u32[]{:S(2)}) %collective-permute-start.20) | collective-permute-done | bytes 852000 | tf_op jit(solution)/shard_map/ppermute | solution.py:89
  157.7 8.8 %fusion.7.q_ref.k_ref.v_ref = f32[768,1664]{1,0:T(8,128)S(1)} fusion(bf16[2048,1664]{1,0:T(8,128)(2,1)} %slice_dynamic-update-slice_fusion, bf16[384,2048]{1,0:T(8,128)(2,1)S(1)} %get-tuple-element.284, bf16[384,2048]{1,0:T(8,128)(2,1)S(1)} %get-tuple-element.283), kind=kOutput, calls=%fused_computation.72 | convolution fusion | flops 5240782848 | bytes 15073280 | tf_op jit(solution)/shard_map/dot_general | solution.py:93
  168.2 7.6 %mixer_forward.1 = (f32[768,512]{1,0:T(8,128)S(1)}, f32[768,256]{1,0:T(8,128)S(1)}, f32[12,512,256]{2,1,0:T(8,128)S(1)}, f32[512,256]{1,0:T(8,128)S(1)}, f32[1,2...) custom-call(f32[768,1664]{1,0:T(8,128)S(1)} %fusion.7.q_ref.k_ref.v_ref, f32[768,1664]{1,0:T(8,128)S(1)} %fusion.7.q_ref.k_ref.v_ref, ...), custom_call_target="tpu_custom_call" | custom-call | tf_op jit(solution)/shard_map/mixer_forward/pallas_call | solution.py:216
  175.9 4.8 collective-permute-start.18
  190.5 4.2 collective-permute-done.17
  199.8 20.9 %collective-permute-done.22 = bf16[512,1664]{1,0:T(8,128)(2,1)S(1)} collective-permute-done((bf16[512,1664]{1,0:T(8,128)(2,1)S(1)}, bf16[512,1664]{1,0:T(8,128)(2,1)S(1)}, u32[]{:S(2)}, u32[]{:S(2)}) %collective-permute-start.22) | collective-permute-done | bytes 1703968 | tf_op jit(solution)/shard_map/ppermute | solution.py:302
  223.0 3.4 fusion.109
  232.0 13.1 %collective-permute-done.30 = bf16[256,1408]{1,0:T(8,128)(2,1)S(1)} collective-permute-done((bf16[256,1408]{1,0:T(8,128)(2,1)S(1)}, bf16[256,1408]{1,0:T(8,128)(2,1)S(1)}, u32[]{:S(2)}, u32[]{:S(2)}) %collective-permute-start.30) | collective-permute-done | bytes 720928 | tf_op jit(solution)/shard_map/ppermute | solution.py:302
  246.3 4.2 collective-permute-start.32
  252.9 4.8 collective-permute-done.28
  259.6 13.6 %collective-permute-done.29 = bf16[512,1408]{1,0:T(8,128)(2,1)S(1)} collective-permute-done((bf16[512,1408]{1,0:T(8,128)(2,1)}, bf16[512,1408]{1,0:T(8,128)(2,1)S(1)}, u32[]{:S(2)}, u32[]{:S(2)}) %collective-permute-start.29) | collective-permute-done | bytes 1441824 | tf_op jit(solution)/shard_map/ppermute | solution.py:302
  279.7 6.8 %collective-permute-done.24 = bf16[384,2048]{1,0:T(8,128)(2,1)S(1)} collective-permute-done((bf16[384,2048]{1,0:T(8,128)(2,1)S(1)}, bf16[384,2048]{1,0:T(8,128)(2,1)S(1)}, u32[]{:S(2)}, u32[]{:S(2)}) %collective-permute-start.24) | collective-permute-done | bytes 1572896 | tf_op jit(solution)/shard_map/ppermute | solution.py:89
  296.0 7.7 %fusion.110 = f32[768,1408]{1,0:T(8,128)S(1)} fusion(bf16[768,2048]{1,0:T(8,128)(2,1)S(1)} %pad_maximum_fusion.5, bf16[2048,1408]{1,0:T(8,128)(2,1)} %maximum_dynamic-update-slice_fusion), kind=kOutput, calls=%fused_computation.433 | convolution fusion | flops 4429185024 | bytes 13238272 | tf_op jit(solution)/shard_map/dot_general | solution.py:93
  303.8 7.9 %multiply_convert_fusion.2 = (bf16[768,1408]{1,0:T(8,128)(2,1)S(1)}, f32[768,1408]{1,0:T(8,128)S(1)}) fusion(f32[768,1408]{1,0:T(8,128)S(1)} %fusion.110, bf16[768,2048]{1,0:T(8,128)(2,1)S(1)} %pad_maximum_fusion.5, bf16[2048,1408]{1,0:T(8,128)(2,1)} %slice_dynamic-update-slice_fusion.4), kind=kOutput, calls=%fused_computation.55 | convolution fusion | flops 4435673088 | bytes 19726336 | tf_op jit(solution)/shard_map/dot_general | solution.py:93
  311.7 3.1 convolution_convert_fusion.7
  316.8 3.1 convolution_convert_fusion.6
  321.9 7.5 %fusion.111 = f32[768,1408]{1,0:T(8,128)S(1)} fusion(bf16[768,2048]{1,0:T(8,128)(2,1)S(1)} %copy-done.47, bf16[2048,1408]{1,0:T(8,128)(2,1)} %slice_dynamic-update-slice_fusion.2), kind=kOutput, calls=%fused_computation.434 | convolution fusion | flops 4429185024 | bytes 13238272 | tf_op jit(solution)/shard_map/dot_general | solution.py:93
  331.6 3.5 multiply_convert_fusion
  335.1 5.1 convolution_convert_fusion.4
  342.4 3.1 convolution_convert_fusion.5
  350.2 6.9 %fusion.112 = f32[768,2048]{1,0:T(8,128)} fusion(bf16[768,1408]{1,0:T(8,128)(2,1)S(1)} %copy-done.62, bf16[2048,1408]{1,0:T(8,128)(2,1)S(1)} %bitcast.82), kind=kOutput, calls=%fused_computation.435 | convolution fusion | flops 4429185024 | bytes 14221312 | tf_op jit(solution)/shard_map/dot_general | solution.py:101
  357.1 7.2 %collective-permute-done.33 = bf16[512,1408]{1,0:T(8,128)(2,1)S(1)} collective-permute-done((bf16[512,1408]{1,0:T(8,128)(2,1)}, bf16[512,1408]{1,0:T(8,128)(2,1)S(1)}, u32[]{:S(2)}, u32[]{:S(2)}) %collective-permute-start.33) | collective-permute-done | bytes 1441824 | tf_op jit(solution)/shard_map/ppermute | solution.py:302
  364.3 9.5 %convolution_add_fusion = f32[768,2048]{1,0:T(8,128)S(1)} fusion(f32[768,2048]{1,0:T(8,128)} %fusion.112, bf16[768,1408]{1,0:T(8,128)(2,1)S(1)} %copy-done.64, bf16[2048,1408]{1,0:T(8,128)(2,1)} %maximum_dynamic-update-slice_fusion), kind=kOutput, calls=%fused_computation.66 | convolution fusion | flops 4430757888 | bytes 20512768 | tf_op jit(solution)/shard_map/dot_general | solution.py:101
  386.8 4.6 convolution_convert_fusion.2
  391.5 4.3 convolution_convert_fusion.3
  395.8 7.8 %fusion.113 = f32[768,2048]{1,0:T(8,128)S(1)} fusion(bf16[768,1408]{1,0:T(8,128)(2,1)} %copy-done.125, bf16[2048,1408]{1,0:T(8,128)(2,1)} %slice_dynamic-update-slice_fusion.2), kind=kOutput, calls=%fused_computation.436 | convolution fusion | flops 4429185024 | bytes 14221312 | tf_op jit(solution)/shard_map/dot_general | solution.py:101
  411.3 8.7 %collective-permute-done.38 = bf16[384,2048]{1,0:T(8,128)(2,1)S(1)} collective-permute-done((bf16[384,2048]{1,0:T(8,128)(2,1)S(1)}, bf16[384,2048]{1,0:T(8,128)(2,1)S(1)}, u32[]{:S(2)}, u32[]{:S(2)}) %collective-permute-start.38) | collective-permute-done | bytes 1572896 | tf_op jit(solution)/shard_map/ppermute | solution.py:89
  425.5 3.6 add_convert_fusion.2
  430.9 9.0 %collective-permute-done.49 = bf16[256,1408]{1,0:T(8,128)(2,1)} collective-permute-done((bf16[256,1408]{1,0:T(8,128)(2,1)}, bf16[256,1408]{1,0:T(8,128)(2,1)}, u32[]{:S(2)}, u32[]{:S(2)}) %collective-permute-start.49) | collective-permute-done | bytes 720928 | tf_op jit(solution)/shard_map/ppermute | solution.py:302
  442.9 9.3 %collective-permute-done.66 = bf16[512,1408]{1,0:T(8,128)(2,1)S(1)} collective-permute-done((bf16[512,1408]{1,0:T(8,128)(2,1)}, bf16[512,1408]{1,0:T(8,128)(2,1)S(1)}, u32[]{:S(2)}, u32[]{:S(2)}) %collective-permute-start.66) | collective-permute-done | bytes 1441824 | tf_op jit(solution)/shard_map/ppermute | solution.py:302
  456.0 11.7 %collective-permute-done.47 = bf16[512,1408]{1,0:T(8,128)(2,1)S(1)} collective-permute-done((bf16[512,1408]{1,0:T(8,128)(2,1)}, bf16[512,1408]{1,0:T(8,128)(2,1)S(1)}, u32[]{:S(2)}, u32[]{:S(2)}) %collective-permute-start.47) | collective-permute-done | bytes 1441824 | tf_op jit(solution)/shard_map/ppermute | solution.py:302
  469.4 4.4 multiply_reduce_fusion.3
  490.5 4.7 collective-permute-start.78
  496.9 3.8 collective-permute-done.43
  501.8 12.2 %mixer_backward.1 = (bf16[768,1024]{1,0:T(8,128)(2,1)S(1)}, f32[768,256]{1,0:T(8,128)S(1)}) custom-call(f32[768,1664]{1,0:T(8,128)S(1)} %fusion.7.q_ref.k_ref.v_ref, f32[768,1664]{1,0:T(8,128)S(1)} %fusion.7.q_ref.k_ref.v_ref, f32[768,1664]{1,0:T(8,128)S(1)} %fusion.7.q_ref.k_ref.v_ref, f32[768,256]{1,0:T(8,128)S(1)} %copy-done.7, ...), custom_call_target="tpu_custom_call" | custom-call | tf_op jit(solution)/shard_map/mixer_backward/pallas_call | solution.py:255
  520.4 8.5 %fusion.114 = f32[768,2048]{1,0:T(8,128)S(1)} fusion(bf16[768,1664]{1,0:T(8,128)(2,1)S(1)} %pad_maximum_fusion.8, bf16[2048,1664]{1,0:T(8,128)(2,1)} %slice_dynamic-update-slice_fusion), kind=kOutput, calls=%fused_computation.437 | convolution fusion | flops 5234491392 | bytes 15663104 | tf_op jit(solution)/shard_map/dot_general | solution.py:101
  566.0 3.6 collective-permute-done.55
  572.8 9.5 %collective-permute-done.62 = bf16[512,1152]{0,1:T(8,128)(2,1)} collective-permute-done((bf16[512,1152]{0,1:T(8,128)(2,1)}, bf16[512,1152]{0,1:T(8,128)(2,1)}, u32[]{:S(2)}, u32[]{:S(2)}) %collective-permute-start.62) | collective-permute-done | bytes 1179680 | tf_op jit(solution)/shard_map/ppermute | solution.py:302
  585.8 16.8 %collective-permute-done.53 = bf16[512,1152]{0,1:T(8,128)(2,1)} collective-permute-done((bf16[512,1152]{0,1:T(8,128)(2,1)}, bf16[512,1152]{0,1:T(8,128)(2,1)}, u32[]{:S(2)}, u32[]{:S(2)}) %collective-permute-start.53) | collective-permute-done | bytes 1179680 | tf_op jit(solution)/shard_map/ppermute | solution.py:302
  608.0 3.8 collective-permute-done.56
  626.8 3.0 fusion.3
  641.5 5.5 fusion.5
  652.0 16.5 %collective-permute-done.61 = f32[8,2048]{1,0:T(8,128)S(1)} collective-permute-done((f32[8,2048]{1,0:T(8,128)S(1)}, f32[8,2048]{1,0:T(8,128)S(1)}, u32[]{:S(2)}, u32[]{:S(2)}) %collective-permute-start.61) | collective-permute-done | bytes 65568 | tf_op jit(solution)/shard_map/ppermute | solution.py:89
  (642 shorter events, 277.1 us)
Async XLA Ops:
  10.8 41.8 %collective-permute-start.4 = (bf16[256,1664]{1,0:T(8,128)(2,1)}, bf16[256,1664]{1,0:T(8,128)(2,1)}, u32[]{:S(2)}, u32[]{:S(2)}) collective-permute-start(bf16[256,1664]{1,0:T(8,128)(2,1)} %pad_maximum_fusion.60), channel_id=1, source_target_pairs={{0,16},{16,0},{1,17},{17,1},{2,18},{18,2},{3,19},{19,3},{4,20},{20... | collective-permute-start | bytes 2555912 | tf_op jit(solution)/shard_map/ppermute | solution.py:89
  14.4 39.8 %collective-permute-start.3 = (bf16[256,1664]{1,0:T(8,128)(2,1)}, bf16[256,1664]{1,0:T(8,128)(2,1)S(1)}, u32[]{:S(2)}, u32[]{:S(2)}) collective-permute-start(bf16[256,1664]{1,0:T(8,128)(2,1)} %pad_maximum_fusion.60), channel_id=1, source_target_pairs={{0,4},{2,10},{4,0},{6,14},{8,12},{10,2},{12,8},{14,6},{1,5},{3,11}... | collective-permute-start | bytes 2555912 | tf_op jit(solution)/shard_map/ppermute | solution.py:302
  24.9 29.5 %collective-permute-start.10 = (bf16[256,1408]{1,0:T(8,128)(2,1)}, bf16[256,1408]{1,0:T(8,128)(2,1)S(1)}, u32[]{:S(2)}, u32[]{:S(2)}) collective-permute-start(bf16[256,1408]{1,0:T(8,128)(2,1)} %pad_maximum_fusion.62), channel_id=1, source_target_pairs={{0,4},{2,10},{4,0},{6,14},{8,12},{10,2},{12,8},{14,6},{1,5},{3,11}... | collective-permute-start | bytes 2162696 | tf_op jit(solution)/shard_map/ppermute | solution.py:302
  28.7 65.8 %collective-permute-start.2 = (bf16[384,2048]{1,0:T(8,128)(2,1)S(1)}, bf16[384,2048]{1,0:T(8,128)(2,1)S(1)}, u32[]{:S(2)}, u32[]{:S(2)}) collective-permute-start(bf16[384,2048]{1,0:T(8,128)(2,1)S(1)} %fusion.2), channel_id=1, source_target_pairs={{0,2},{2,0},{4,6},{6,4},{8,10},{10,8},{12,14},{14,12},{1,3},{3,1},... | collective-permute-start | bytes 4718600 | tf_op jit(solution)/shard_map/ppermute | solution.py:89
  32.0 23.8 %collective-permute-start.7 = (bf16[256,1664]{1,0:T(8,128)(2,1)S(1)}, bf16[256,1664]{1,0:T(8,128)(2,1)S(1)}, u32[]{:S(2)}, u32[]{:S(2)}) collective-permute-start(bf16[256,1664]{1,0:T(8,128)(2,1)S(1)} %pad_maximum_fusion.61), channel_id=1, source_target_pairs={{0,4},{2,10},{4,0},{6,14},{8,12},{10,2},{12,8},{14,6},{1,5},{3,11}... | collective-permute-start | bytes 2555912 | tf_op jit(solution)/shard_map/ppermute | solution.py:302
  54.2 39.5 %collective-permute-start.13 = (bf16[256,1664]{1,0:T(8,128)(2,1)S(1)}, bf16[256,1664]{1,0:T(8,128)(2,1)S(1)}, u32[]{:S(2)}, u32[]{:S(2)}) collective-permute-start(bf16[256,1664]{1,0:T(8,128)(2,1)S(1)} %pad_maximum_fusion.61), channel_id=1, source_target_pairs={{0,16},{16,0},{1,17},{17,1},{2,18},{18,2},{3,19},{19,3},{4,20},{20... | collective-permute-start | bytes 2555912 | tf_op jit(solution)/shard_map/ppermute | solution.py:89
  54.5 43.4 %collective-permute-start.31 = (bf16[384,2048]{1,0:T(8,128)(2,1)S(1)}, bf16[384,2048]{1,0:T(8,128)(2,1)S(1)}, u32[]{:S(2)}, u32[]{:S(2)}) collective-permute-start(bf16[384,2048]{1,0:T(8,128)(2,1)S(1)} %get-tuple-element.108), channel_id=1, source_target_pairs={{0,2},{2,0},{4,6},{6,4},{8,10},{10,8},{12,14},{14,12},{1,3},{3,1},... | collective-permute-start | bytes 4718600 | tf_op jit(solution)/shard_map/ppermute | solution.py:89
  65.3 40.2 %collective-permute-start.12 = (bf16[256,1664]{1,0:T(8,128)(2,1)}, bf16[256,1664]{1,0:T(8,128)(2,1)S(1)}, u32[]{:S(2)}, u32[]{:S(2)}) collective-permute-start(bf16[256,1664]{1,0:T(8,128)(2,1)} %collective-permute-done.4), channel_id=1, source_target_pairs={{0,4},{2,10},{4,0},{6,14},{8,12},{10,2},{12,8},{14,6},{1,5},{3,11}... | collective-permute-start | bytes 2555912 | tf_op jit(solution)/shard_map/ppermute | solution.py:302
  66.8 40.0 %collective-permute-start.11 = (bf16[512,1664]{1,0:T(8,128)(2,1)S(1)}, bf16[512,1664]{1,0:T(8,128)(2,1)S(1)}, u32[]{:S(2)}, u32[]{:S(2)}) collective-permute-start(bf16[512,1664]{1,0:T(8,128)(2,1)S(1)} %pad_maximum_fusion.10), channel_id=1, source_target_pairs={{0,8},{2,6},{4,12},{6,2},{8,0},{10,14},{12,4},{14,10},{1,9},{3,7},... | collective-permute-start | bytes 5111816 | tf_op jit(solution)/shard_map/ppermute | solution.py:302
  93.7 21.8 %collective-permute-start.14 = (bf16[512,1664]{1,0:T(8,128)(2,1)S(1)}, bf16[512,1664]{1,0:T(8,128)(2,1)S(1)}, u32[]{:S(2)}, u32[]{:S(2)}) collective-permute-start(bf16[512,1664]{1,0:T(8,128)(2,1)S(1)} %pad_maximum_fusion.11), channel_id=1, source_target_pairs={{0,8},{2,6},{4,12},{6,2},{8,0},{10,14},{12,4},{14,10},{1,9},{3,7},... | collective-permute-start | bytes 5111816 | tf_op jit(solution)/shard_map/ppermute | solution.py:302
  115.5 38.6 %collective-permute-start.19 = (bf16[256,1664]{1,0:T(8,128)(2,1)S(1)}, bf16[256,1664]{1,0:T(8,128)(2,1)S(1)}, u32[]{:S(2)}, u32[]{:S(2)}) collective-permute-start(bf16[256,1664]{1,0:T(8,128)(2,1)S(1)} %collective-permute-done.13), channel_id=1, source_target_pairs={{0,4},{2,10},{4,0},{6,14},{8,12},{10,2},{12,8},{14,6},{1,5},{3,11}... | collective-permute-start | bytes 2555912 | tf_op jit(solution)/shard_map/ppermute | solution.py:302
  117.0 37.1 %collective-permute-start.20 = (bf16[256,1664]{1,0:T(8,128)(2,1)S(1)}, bf16[256,1664]{1,0:T(8,128)(2,1)S(1)}, u32[]{:S(2)}, u32[]{:S(2)}) collective-permute-start(bf16[256,1664]{1,0:T(8,128)(2,1)S(1)} %maximum_maximum_fusion), channel_id=1, source_target_pairs={{0,16},{16,0},{1,17},{17,1},{2,18},{18,2},{3,19},{19,3},{4,20},{20... | collective-permute-start | bytes 2555912 | tf_op jit(solution)/shard_map/ppermute | solution.py:89
  117.0 37.2 %collective-permute-start.15 = (bf16[512,1664]{1,0:T(8,128)(2,1)S(1)}, bf16[512,1664]{1,0:T(8,128)(2,1)S(1)}, u32[]{:S(2)}, u32[]{:S(2)}) collective-permute-start(bf16[512,1664]{1,0:T(8,128)(2,1)S(1)} %pad_maximum_fusion.12), channel_id=1, source_target_pairs={{0,8},{2,6},{4,12},{6,2},{8,0},{10,14},{12,4},{14,10},{1,9},{3,7},... | collective-permute-start | bytes 5111816 | tf_op jit(solution)/shard_map/ppermute | solution.py:302
  117.5 67.0 %collective-permute-start.21 = (bf16[512,1664]{1,0:T(8,128)(2,1)S(1)}, bf16[512,1664]{1,0:T(8,128)(2,1)S(1)}, u32[]{:S(2)}, u32[]{:S(2)}) collective-permute-start(bf16[512,1664]{1,0:T(8,128)(2,1)S(1)} %pad_maximum_fusion.13), channel_id=1, source_target_pairs={{0,8},{2,6},{4,12},{6,2},{8,0},{10,14},{12,4},{14,10},{1,9},{3,7},... | collective-permute-start | bytes 5111816 | tf_op jit(solution)/shard_map/ppermute | solution.py:302
  175.9 21.4 %collective-permute-start.18 = (bf16[528,256]{1,0:T(8,128)(2,1)S(1)}, bf16[528,256]{1,0:T(8,128)(2,1)S(1)}, u32[]{:S(2)}, u32[]{:S(2)}) collective-permute-start(bf16[528,256]{1,0:T(8,128)(2,1)S(1)} %pad_maximum_fusion.66), channel_id=1, source_target_pairs={{0,12},{2,14},{1,13},{3,15},{16,28},{18,30},{17,29},{19,31}} | collective-permute-start | bytes 811016 | tf_op jit(solution)/shard_map/ppermute | solution.py:469
  184.5 43.3 %collective-permute-start.27 = (bf16[256,1408]{1,0:T(8,128)(2,1)}, bf16[256,1408]{1,0:T(8,128)(2,1)S(1)}, u32[]{:S(2)}, u32[]{:S(2)}) collective-permute-start(bf16[256,1408]{1,0:T(8,128)(2,1)} %pad_maximum_fusion.62), channel_id=1, source_target_pairs={{0,16},{16,0},{1,17},{17,1},{2,18},{18,2},{3,19},{19,3},{4,20},{20... | collective-permute-start | bytes 2162696 | tf_op jit(solution)/shard_map/ppermute | solution.py:89
  184.6 43.1 %collective-permute-start.26 = (bf16[256,1664]{1,0:T(8,128)(2,1)S(1)}, bf16[256,1664]{1,0:T(8,128)(2,1)S(1)}, u32[]{:S(2)}, u32[]{:S(2)}) collective-permute-start(bf16[256,1664]{1,0:T(8,128)(2,1)S(1)} %collective-permute-done.20), channel_id=1, source_target_pairs={{0,4},{2,10},{4,0},{6,14},{8,12},{10,2},{12,8},{14,6},{1,5},{3,11}... | collective-permute-start | bytes 2555912 | tf_op jit(solution)/shard_map/ppermute | solution.py:302
  194.7 26.0 %collective-permute-start.22 = (bf16[512,1664]{1,0:T(8,128)(2,1)S(1)}, bf16[512,1664]{1,0:T(8,128)(2,1)S(1)}, u32[]{:S(2)}, u32[]{:S(2)}) collective-permute-start(bf16[512,1664]{1,0:T(8,128)(2,1)S(1)} %pad_maximum_fusion.14), channel_id=1, source_target_pairs={{0,8},{2,6},{4,12},{6,2},{8,0},{10,14},{12,4},{14,10},{1,9},{3,7},... | collective-permute-start | bytes 5111816 | tf_op jit(solution)/shard_map/ppermute | solution.py:302
  226.7 23.8 %collective-permute-start.23 = (bf16[384,2048]{1,0:T(8,128)(2,1)S(1)}, bf16[384,2048]{1,0:T(8,128)(2,1)}, u32[]{:S(2)}, u32[]{:S(2)}) collective-permute-start(bf16[384,2048]{1,0:T(8,128)(2,1)S(1)} %select_convert_fusion.3), channel_id=1, source_target_pairs={{0,2},{2,0},{4,6},{6,4},{8,10},{10,8},{12,14},{14,12},{1,3},{3,1},... | collective-permute-start | bytes 4718600 | tf_op jit(solution)/shard_map/ppermute | solution.py:89
  228.9 28.8 %collective-permute-start.28 = (bf16[512,1664]{1,0:T(8,128)(2,1)S(1)}, bf16[512,1664]{1,0:T(8,128)(2,1)S(1)}, u32[]{:S(2)}, u32[]{:S(2)}) collective-permute-start(bf16[512,1664]{1,0:T(8,128)(2,1)S(1)} %pad_maximum_fusion.15), channel_id=1, source_target_pairs={{0,8},{2,6},{4,12},{6,2},{8,0},{10,14},{12,4},{14,10},{1,9},{3,7},... | collective-permute-start | bytes 5111816 | tf_op jit(solution)/shard_map/ppermute | solution.py:302
  231.5 41.7 %collective-permute-start.29 = (bf16[512,1408]{1,0:T(8,128)(2,1)}, bf16[512,1408]{1,0:T(8,128)(2,1)S(1)}, u32[]{:S(2)}, u32[]{:S(2)}) collective-permute-start(bf16[512,1408]{1,0:T(8,128)(2,1)} %pad_maximum_fusion.56), channel_id=1, source_target_pairs={{0,8},{2,6},{4,12},{6,2},{8,0},{10,14},{12,4},{14,10},{1,9},{3,7},... | collective-permute-start | bytes 4325384 | tf_op jit(solution)/shard_map/ppermute | solution.py:302
  246.3 42.9 %collective-permute-start.32 = (bf16[512,1408]{1,0:T(8,128)(2,1)}, bf16[512,1408]{1,0:T(8,128)(2,1)S(1)}, u32[]{:S(2)}, u32[]{:S(2)}) collective-permute-start(bf16[512,1408]{1,0:T(8,128)(2,1)} %pad_maximum_fusion.57), channel_id=1, source_target_pairs={{0,8},{2,6},{4,12},{6,2},{8,0},{10,14},{12,4},{14,10},{1,9},{3,7},... | collective-permute-start | bytes 4325384 | tf_op jit(solution)/shard_map/ppermute | solution.py:302
  252.8 33.6 %collective-permute-start.24 = (bf16[384,2048]{1,0:T(8,128)(2,1)S(1)}, bf16[384,2048]{1,0:T(8,128)(2,1)S(1)}, u32[]{:S(2)}, u32[]{:S(2)}) collective-permute-start(bf16[384,2048]{1,0:T(8,128)(2,1)S(1)} %add_convert_fusion.4), channel_id=1, source_target_pairs={{0,1},{1,0},{2,3},{3,2},{4,5},{5,4},{6,7},{7,6},{8,9},{9,8},{10,11... | collective-permute-start | bytes 4718600 | tf_op jit(solution)/shard_map/ppermute | solution.py:89
  329.5 44.6 %collective-permute-start.45 = (bf16[512,1408]{1,0:T(8,128)(2,1)}, bf16[512,1408]{1,0:T(8,128)(2,1)}, u32[]{:S(2)}, u32[]{:S(2)}) collective-permute-start(bf16[512,1408]{1,0:T(8,128)(2,1)} %slice.807), channel_id=1, source_target_pairs={{0,8},{2,6},{4,12},{6,2},{8,0},{10,14},{12,4},{14,10},{1,9},{3,7},... | collective-permute-start | bytes 4325384 | tf_op jit(solution)/shard_map/ppermute | solution.py:302
  331.5 32.8 %collective-permute-start.33 = (bf16[512,1408]{1,0:T(8,128)(2,1)}, bf16[512,1408]{1,0:T(8,128)(2,1)S(1)}, u32[]{:S(2)}, u32[]{:S(2)}) collective-permute-start(bf16[512,1408]{1,0:T(8,128)(2,1)} %slice.787), channel_id=1, source_target_pairs={{0,8},{2,6},{4,12},{6,2},{8,0},{10,14},{12,4},{14,10},{1,9},{3,7},... | collective-permute-start | bytes 4325384 | tf_op jit(solution)/shard_map/ppermute | solution.py:302
  348.3 32.6 %collective-permute-start.35 = (bf16[512,1408]{1,0:T(8,128)(2,1)}, bf16[512,1408]{1,0:T(8,128)(2,1)}, u32[]{:S(2)}, u32[]{:S(2)}) collective-permute-start(bf16[512,1408]{1,0:T(8,128)(2,1)} %slice.790), channel_id=1, source_target_pairs={{0,8},{2,6},{4,12},{6,2},{8,0},{10,14},{12,4},{14,10},{1,9},{3,7},... | collective-permute-start | bytes 4325384 | tf_op jit(solution)/shard_map/ppermute | solution.py:302
  384.4 35.6 %collective-permute-start.38 = (bf16[384,2048]{1,0:T(8,128)(2,1)S(1)}, bf16[384,2048]{1,0:T(8,128)(2,1)S(1)}, u32[]{:S(2)}, u32[]{:S(2)}) collective-permute-start(bf16[384,2048]{1,0:T(8,128)(2,1)S(1)} %add_convert_fusion.3), channel_id=1, source_target_pairs={{0,1},{1,0},{2,3},{3,2},{4,5},{5,4},{6,7},{7,6},{8,9},{9,8},{10,11... | collective-permute-start | bytes 4718600 | tf_op jit(solution)/shard_map/ppermute | solution.py:89
  384.8 23.7 %collective-permute-start.46 = (bf16[512,1408]{1,0:T(8,128)(2,1)}, bf16[512,1408]{1,0:T(8,128)(2,1)}, u32[]{:S(2)}, u32[]{:S(2)}) collective-permute-start(bf16[512,1408]{1,0:T(8,128)(2,1)} %slice.805), channel_id=1, source_target_pairs={{0,8},{2,6},{4,12},{6,2},{8,0},{10,14},{12,4},{14,10},{1,9},{3,7},... | collective-permute-start | bytes 4325384 | tf_op jit(solution)/shard_map/ppermute | solution.py:302
  405.1 20.5 %collective-permute-start.37 = (bf16[384,2048]{1,0:T(8,128)(2,1)}, bf16[384,2048]{1,0:T(8,128)(2,1)}, u32[]{:S(2)}, u32[]{:S(2)}) collective-permute-start(bf16[384,2048]{1,0:T(8,128)(2,1)} %select_convert_fusion.1), channel_id=1, source_target_pairs={{0,2},{2,0},{4,6},{6,4},{8,10},{10,8},{12,14},{14,12},{1,3},{3,1},... | collective-permute-start | bytes 4718600 | tf_op jit(solution)/shard_map/ppermute | solution.py:89
  420.0 59.3 %collective-permute-start.44 = (bf16[256,1408]{1,0:T(8,128)(2,1)}, bf16[256,1408]{1,0:T(8,128)(2,1)}, u32[]{:S(2)}, u32[]{:S(2)}) collective-permute-start(bf16[256,1408]{1,0:T(8,128)(2,1)} %add_convert_fusion.20), channel_id=1, source_target_pairs={{0,16},{16,0},{1,17},{17,1},{2,18},{18,2},{3,19},{19,3},{4,20},{20... | collective-permute-start | bytes 2162696 | tf_op jit(solution)/shard_map/ppermute | solution.py:89
  420.5 19.4 %collective-permute-start.49 = (bf16[256,1408]{1,0:T(8,128)(2,1)}, bf16[256,1408]{1,0:T(8,128)(2,1)}, u32[]{:S(2)}, u32[]{:S(2)}) collective-permute-start(bf16[256,1408]{1,0:T(8,128)(2,1)} %slice.813), channel_id=1, source_target_pairs={{0,4},{2,10},{4,0},{6,14},{8,12},{10,2},{12,8},{14,6},{1,5},{3,11}... | collective-permute-start | bytes 2162696 | tf_op jit(solution)/shard_map/ppermute | solution.py:302
  422.2 30.0 %collective-permute-start.66 = (bf16[512,1408]{1,0:T(8,128)(2,1)}, bf16[512,1408]{1,0:T(8,128)(2,1)S(1)}, u32[]{:S(2)}, u32[]{:S(2)}) collective-permute-start(bf16[512,1408]{1,0:T(8,128)(2,1)} %slice.812), channel_id=1, source_target_pairs={{0,8},{2,6},{4,12},{6,2},{8,0},{10,14},{12,4},{14,10},{1,9},{3,7},... | collective-permute-start | bytes 4325384 | tf_op jit(solution)/shard_map/ppermute | solution.py:302
  429.1 38.5 %collective-permute-start.47 = (bf16[512,1408]{1,0:T(8,128)(2,1)}, bf16[512,1408]{1,0:T(8,128)(2,1)S(1)}, u32[]{:S(2)}, u32[]{:S(2)}) collective-permute-start(bf16[512,1408]{1,0:T(8,128)(2,1)} %slice.803), channel_id=1, source_target_pairs={{0,8},{2,6},{4,12},{6,2},{8,0},{10,14},{12,4},{14,10},{1,9},{3,7},... | collective-permute-start | bytes 4325384 | tf_op jit(solution)/shard_map/ppermute | solution.py:302
  430.8 38.3 %collective-permute-start.40 = (bf16[384,2048]{1,0:T(8,128)(2,1)S(1)}, bf16[384,2048]{1,0:T(8,128)(2,1)S(1)}, u32[]{:S(2)}, u32[]{:S(2)}) collective-permute-start(bf16[384,2048]{1,0:T(8,128)(2,1)S(1)} %fusion.87), channel_id=1, source_target_pairs={{0,2},{2,0},{4,6},{6,4},{8,10},{10,8},{12,14},{14,12},{1,3},{3,1},... | collective-permute-start | bytes 4718600 | tf_op jit(solution)/shard_map/ppermute | solution.py:89
  439.9 60.9 %collective-permute-start.48 = (bf16[256,1408]{1,0:T(8,128)(2,1)}, bf16[256,1408]{1,0:T(8,128)(2,1)S(1)}, u32[]{:S(2)}, u32[]{:S(2)}) collective-permute-start(bf16[256,1408]{1,0:T(8,128)(2,1)} %slice.809), channel_id=1, source_target_pairs={{0,4},{2,10},{4,0},{6,14},{8,12},{10,2},{12,8},{14,6},{1,5},{3,11}... | collective-permute-start | bytes 2162696 | tf_op jit(solution)/shard_map/ppermute | solution.py:302
  452.2 48.6 %collective-permute-start.50 = (bf16[256,1408]{1,0:T(8,128)(2,1)S(1)}, bf16[256,1408]{1,0:T(8,128)(2,1)S(1)}, u32[]{:S(2)}, u32[]{:S(2)}) collective-permute-start(bf16[256,1408]{1,0:T(8,128)(2,1)S(1)} %add_convert_fusion.19), channel_id=1, source_target_pairs={{0,16},{16,0},{1,17},{17,1},{2,18},{18,2},{3,19},{19,3},{4,20},{20... | collective-permute-start | bytes 2162696 | tf_op jit(solution)/shard_map/ppermute | solution.py:89
  490.5 56.5 %collective-permute-start.78 = (bf16[256,1408]{1,0:T(8,128)(2,1)}, bf16[256,1408]{1,0:T(8,128)(2,1)}, u32[]{:S(2)}, u32[]{:S(2)}) collective-permute-start(bf16[256,1408]{1,0:T(8,128)(2,1)} %slice.808), channel_id=1, source_target_pairs={{0,4},{2,10},{4,0},{6,14},{8,12},{10,2},{12,8},{14,6},{1,5},{3,11}... | collective-permute-start | bytes 2162696 | tf_op jit(solution)/shard_map/ppermute | solution.py:302
  495.2 38.4 %collective-permute-start.39 = (bf16[384,2048]{1,0:T(8,128)(2,1)}, bf16[384,2048]{1,0:T(8,128)(2,1)}, u32[]{:S(2)}, u32[]{:S(2)}) collective-permute-start(bf16[384,2048]{1,0:T(8,128)(2,1)} %add_convert_fusion.2), channel_id=1, source_target_pairs={{0,1},{1,0},{2,3},{3,2},{4,5},{5,4},{6,7},{7,6},{8,9},{9,8},{10,11... | collective-permute-start | bytes 4718600 | tf_op jit(solution)/shard_map/ppermute | solution.py:89
  514.9 22.8 %collective-permute-start.75 = (bf16[256,1408]{1,0:T(8,128)(2,1)}, bf16[256,1408]{1,0:T(8,128)(2,1)}, u32[]{:S(2)}, u32[]{:S(2)}) collective-permute-start(bf16[256,1408]{1,0:T(8,128)(2,1)} %slice.847), channel_id=1, source_target_pairs={{0,4},{2,10},{4,0},{6,14},{8,12},{10,2},{12,8},{14,6},{1,5},{3,11}... | collective-permute-start | bytes 2162696 | tf_op jit(solution)/shard_map/ppermute | solution.py:302
  514.9 27.6 %collective-permute-start.67 = (bf16[512,1024]{0,1:T(8,128)(2,1)}, bf16[512,1024]{0,1:T(8,128)(2,1)}, u32[]{:S(2)}, u32[]{:S(2)}) collective-permute-start(bf16[512,1024]{0,1:T(8,128)(2,1)} %fusion.27), channel_id=1, source_target_pairs={{0,8},{2,6},{4,12},{6,2},{8,0},{10,14},{12,4},{14,10},{1,9},{3,7},... | collective-permute-start | bytes 3145736 | tf_op jit(solution)/shard_map/ppermute | solution.py:302
  540.5 71.7 %collective-permute-start.76 = (bf16[256,1408]{1,0:T(8,128)(2,1)}, bf16[256,1408]{1,0:T(8,128)(2,1)}, u32[]{:S(2)}, u32[]{:S(2)}) collective-permute-start(bf16[256,1408]{1,0:T(8,128)(2,1)} %add_convert_fusion.16), channel_id=1, source_target_pairs={{0,16},{16,0},{1,17},{17,1},{2,18},{18,2},{3,19},{19,3},{4,20},{20... | collective-permute-start | bytes 2162696 | tf_op jit(solution)/shard_map/ppermute | solution.py:89
  553.6 62.9 %collective-permute-start.52 = (bf16[384,2048]{1,0:T(8,128)(2,1)S(1)}, bf16[384,2048]{1,0:T(8,128)(2,1)}, u32[]{:S(2)}, u32[]{:S(2)}) collective-permute-start(bf16[384,2048]{1,0:T(8,128)(2,1)S(1)} %add_convert_fusion), channel_id=1, source_target_pairs={{0,1},{1,0},{2,3},{3,2},{4,5},{5,4},{6,7},{7,6},{8,9},{9,8},{10,11... | collective-permute-start | bytes 4718600 | tf_op jit(solution)/shard_map/ppermute | solution.py:89
  559.8 22.5 %collective-permute-start.62 = (bf16[512,1152]{0,1:T(8,128)(2,1)}, bf16[512,1152]{0,1:T(8,128)(2,1)}, u32[]{:S(2)}, u32[]{:S(2)}) collective-permute-start(bf16[512,1152]{0,1:T(8,128)(2,1)} %slice.830), channel_id=1, source_target_pairs={{0,8},{2,6},{4,12},{6,2},{8,0},{10,14},{12,4},{14,10},{1,9},{3,7},... | collective-permute-start | bytes 3538952 | tf_op jit(solution)/shard_map/ppermute | solution.py:302
  559.8 42.9 %collective-permute-start.53 = (bf16[512,1152]{0,1:T(8,128)(2,1)}, bf16[512,1152]{0,1:T(8,128)(2,1)}, u32[]{:S(2)}, u32[]{:S(2)}) collective-permute-start(bf16[512,1152]{0,1:T(8,128)(2,1)} %slice.817), channel_id=1, source_target_pairs={{0,8},{2,6},{4,12},{6,2},{8,0},{10,14},{12,4},{14,10},{1,9},{3,7},... | collective-permute-start | bytes 3538952 | tf_op jit(solution)/shard_map/ppermute | solution.py:302
  569.7 38.3 %collective-permute-start.69 = (bf16[256,1024]{0,1:T(8,128)(2,1)}, bf16[256,1024]{0,1:T(8,128)(2,1)S(1)}, u32[]{:S(2)}, u32[]{:S(2)}) collective-permute-start(bf16[256,1024]{0,1:T(8,128)(2,1)} %add_convert_fusion.23), channel_id=1, source_target_pairs={{0,16},{16,0},{1,17},{17,1},{2,18},{18,2},{3,19},{19,3},{4,20},{20... | collective-permute-start | bytes 1572872 | tf_op jit(solution)/shard_map/ppermute | solution.py:89
  582.3 29.9 %collective-permute-start.74 = (bf16[256,1408]{1,0:T(8,128)(2,1)S(1)}, bf16[256,1408]{1,0:T(8,128)(2,1)S(1)}, u32[]{:S(2)}, u32[]{:S(2)}) collective-permute-start(bf16[256,1408]{1,0:T(8,128)(2,1)S(1)} %copy-done.77), channel_id=1, source_target_pairs={{0,4},{2,10},{4,0},{6,14},{8,12},{10,2},{12,8},{14,6},{1,5},{3,11}... | collective-permute-start | bytes 2162696 | tf_op jit(solution)/shard_map/ppermute | solution.py:302
  638.4 30.7 %collective-permute-start.64 = (bf16[256,1152]{0,1:T(8,128)(2,1)S(1)}, bf16[256,1152]{0,1:T(8,128)(2,1)S(1)}, u32[]{:S(2)}, u32[]{:S(2)}) collective-permute-start(bf16[256,1152]{0,1:T(8,128)(2,1)S(1)} %add_convert_fusion.21), channel_id=1, source_target_pairs={{0,16},{16,0},{1,17},{17,1},{2,18},{18,2},{3,19},{19,3},{4,20},{20... | collective-permute-start | bytes 1769480 | tf_op jit(solution)/shard_map/ppermute | solution.py:89
  640.7 27.8 %collective-permute-start.61 = (f32[8,2048]{1,0:T(8,128)S(1)}, f32[8,2048]{1,0:T(8,128)S(1)}, u32[]{:S(2)}, u32[]{:S(2)}) collective-permute-start(f32[8,2048]{1,0:T(8,128)S(1)} %add.329), channel_id=1, source_target_pairs={{0,16},{16,0},{1,17},{17,1},{2,18},{18,2},{3,19},{19,3},{4,20},{20... | collective-permute-start | bytes 196616 | tf_op jit(solution)/shard_map/ppermute | solution.py:89
  (162 other events, 1839.1 us)
